TPU v7x, 32 devices: a whole 2x2x4 slice. The times are simulated.
32 devices in a mesh: pb: 4 (over z), pa: 8 (over y, x, core).
Axes of the slice: x: 2, y: 2, z: 4, core: 2. Of those that a mesh axis runs over, the one named last changes fastest.
Arguments:
- queries: float32 [4096, 768], P(('pb', 'pa')), may hold values from -5 to 5
- passages: float32 [4096, 768], P(('pb', 'pa')), may hold values from -5 to 5
- hard_ids: int32 [4096, 32], P(('pb', 'pa')), may hold values from 0 to 4095, as said below
- list_lengths: int32 [4096], P(('pb', 'pa')), may hold values from 1 to 32, 98304 in all
Outputs:
- loss: float32 [], replicated
- grad_queries: float32 [4096, 768], P(('pb', 'pa'))
- grad_passages: float32 [4096, 768], P(('pb', 'pa'))
Inputs may be any that keep to these rules, and one draw needn't show every extreme that they name: `hard_ids`: cut the rows into aligned blocks of 128 (the rows of one device) and the passage ids into blocks of 128 consecutive ids: the 32 listed ids of one row block, live or not, fall at most 160 times into any one id block; in every draw some id block receives exactly 160 ids from every row block.
All inputs are finite; a program needn't handle non-finite values. No bound on the sum of `list_lengths` on one device may be relied on, other than what follows from the above.
Results may differ from a plain program's by a relative error of at most 0.0014.
The roundings to bfloat16 on the way count: a program that leaves them out, or rounds other values in their place, can miss the bound.
Values may be sent and summed in bfloat16 or wider, within the bound.
No kernel may reach another device: no remote copies, remote signals or barrier semaphores. Data moves between devices by JAX's collectives and lax.ppermute only.
A program may use at most 128 MiB of HBM per device.

v0:
```python
import math

import jax
import jax.numpy as jnp
from jax import lax
from jax.sharding import PartitionSpec as P


def merged(value, axis, combine):
    everything = jax.tree.map(lambda part: lax.all_gather(part, axis), value)
    leading = jax.tree.map(lambda part: part[0], everything)

    def turn(k, so_far):
        return combine(so_far, jax.tree.map(lambda part: part[k], everything))

    return lax.fori_loop(1, lax.axis_size(axis), turn, leading)


def tile_scores(left_rows, right_rows):
    return lax.dot_general(
        left_rows, right_rows, (((1,), (1,)), ((), ())), preferred_element_type=jnp.float32
    )


def slot_places(owner_rank, devices):
    pair_count = owner_rank.shape[0]
    group_width = 128
    one_hot = (owner_rank[:, None] == jnp.arange(devices, dtype=jnp.int32)[None, :]).astype(
        jnp.float32
    )
    grouped = one_hot.reshape(pair_count // group_width, group_width, devices)
    lower_mask = (jnp.arange(group_width)[None, :] < jnp.arange(group_width)[:, None]).astype(
        jnp.float32
    )
    within = jnp.einsum("ij,bjd->bid", lower_mask, grouped, precision=lax.Precision.HIGHEST)
    counts = grouped.sum(1)
    before = jnp.cumsum(counts, 0) - counts
    slot_rank = jnp.sum((within + before[:, None, :]) * grouped, -1)
    return slot_rank.reshape(pair_count).astype(jnp.int32)


def combine_stats(first_pair, second_pair):
    first_top, first_total = first_pair
    second_top, second_total = second_pair
    new_top = jnp.maximum(first_top, second_top)
    return (
        new_top,
        first_total * jnp.exp(first_top - new_top) + second_total * jnp.exp(second_top - new_top),
    )


def per_device(queries, passages, hard_ids, list_lengths):
    row_count, feature_width = queries.shape
    listed = hard_ids.shape[1]
    span_across = lax.axis_size("pa")
    span_down = lax.axis_size("pb")
    devices = span_across * span_down
    capacity = (5 * listed * row_count + 4 * devices - 1) // (4 * devices)
    col_index = lax.axis_index("pa")
    row_index = lax.axis_index("pb")
    query_own = queries.astype(jnp.bfloat16)
    passage_own = passages.astype(jnp.bfloat16)
    query_block = lax.all_gather(query_own, "pa", axis=0, tiled=True)
    passage_block = lax.all_gather(passage_own, "pb", axis=0, tiled=True)
    pair_count = row_count * listed
    flat_ids = hard_ids.reshape(pair_count)
    owner_rank = flat_ids // row_count
    local_row = flat_ids % row_count
    slot_place = owner_rank * capacity + slot_places(owner_rank, devices)
    live_mask = jnp.arange(listed, dtype=jnp.int32)[None, :] < list_lengths[:, None]
    request = (
        jnp.zeros((devices * capacity,), jnp.int32)
        .at[slot_place]
        .set(local_row)
        .reshape(devices, capacity)
    )
    pair_queries = jnp.repeat(query_own, listed, axis=0)
    asked_rows = lax.all_to_all(request, ("pb", "pa"), split_axis=0, concat_axis=0, tiled=True)
    found_rows = passage_own[asked_rows]
    fetched = lax.all_to_all(found_rows, ("pb", "pa"), split_axis=0, concat_axis=0, tiled=True)
    neg_rows = fetched.reshape(devices * capacity, feature_width)[slot_place].reshape(
        row_count, listed, feature_width
    )
    hard_score = jnp.einsum("rd,rhd->rh", query_own, neg_rows, preferred_element_type=jnp.float32)
    masked = jnp.where(live_mask, hard_score, -jnp.inf)
    tall_rows = query_block.shape[0]
    wide_cols = passage_block.shape[0]
    block_rows = math.gcd(tall_rows, 512)

    def sweep_block(carried, query_part):
        col_top, col_total = carried
        scores = tile_scores(query_part, passage_block)
        part_top = scores.max(1)
        part_total = jnp.exp(scores - part_top[:, None]).sum(1)
        new_top = jnp.maximum(col_top, scores.max(0))
        col_total = col_total * jnp.exp(col_top - new_top) + jnp.exp(scores - new_top[None, :]).sum(
            0
        )
        return ((new_top, col_total), (part_top, part_total))

    start_state = (
        jnp.full((wide_cols,), -jnp.inf, jnp.float32),
        jnp.zeros((wide_cols,), jnp.float32),
    )
    (col_top, col_total), (row_top, row_total) = lax.scan(
        sweep_block,
        start_state,
        query_block.reshape(tall_rows // block_rows, block_rows, feature_width),
    )
    row_top = row_top.reshape(tall_rows)
    row_total = row_total.reshape(tall_rows)
    own_top = lax.dynamic_slice_in_dim(row_top, col_index * row_count, row_count)
    own_total = lax.dynamic_slice_in_dim(row_total, col_index * row_count, row_count)
    merged_top = jnp.maximum(own_top, masked.max(1))
    merged_total = own_total * jnp.exp(own_top - merged_top) + jnp.exp(
        masked - merged_top[:, None]
    ).sum(1)
    row_top = lax.dynamic_update_slice_in_dim(row_top, merged_top, col_index * row_count, 0)
    row_total = lax.dynamic_update_slice_in_dim(row_total, merged_total, col_index * row_count, 0)
    row_peak, row_sum = merged((row_top, row_total), "pa", combine_stats)
    col_peak, col_sum = merged((col_top, col_total), "pb", combine_stats)
    row_lse = row_peak + jnp.log(row_sum)
    column_lse = col_peak + jnp.log(col_sum)
    diagonal = jnp.einsum("rd,rd->r", query_own, passage_own, preferred_element_type=jnp.float32)
    own_row = lax.dynamic_slice_in_dim(row_lse, col_index * row_count, row_count)
    own_column = lax.dynamic_slice_in_dim(column_lse, row_index * row_count, row_count)
    partial_loss = jnp.sum(own_row - diagonal) + jnp.sum(own_column - diagonal)
    loss = lax.psum(partial_loss, ("pb", "pa")) / (2.0 * row_count * devices)
    hard_weight = jnp.exp(masked - own_row[:, None]).astype(jnp.bfloat16)
    hard_query = jnp.einsum("rh,rhd->rd", hard_weight, neg_rows, preferred_element_type=jnp.float32)
    flat_weight = hard_weight.reshape(pair_count)
    contribution = (
        jnp.zeros((devices * capacity, feature_width), jnp.float32)
        .at[slot_place]
        .set(flat_weight.astype(jnp.float32)[:, None] * pair_queries.astype(jnp.float32))
    )
    arrived_rows = lax.all_to_all(
        contribution.reshape(devices, capacity, feature_width).astype(jnp.bfloat16),
        ("pb", "pa"),
        split_axis=0,
        concat_axis=0,
        tiled=True,
    ).astype(jnp.float32)
    hard_passage = (
        jnp.zeros((row_count, feature_width), jnp.float32)
        .at[asked_rows.reshape(-1)]
        .add(arrived_rows.reshape(-1, feature_width))
    )
    row_span = lax.axis_size("pa") * row_count
    query_part = query_block
    level_part = row_lse
    inner_rows = math.gcd(row_span, 512)

    def query_piece_work(inputs):
        left_rows, level_rows = inputs
        scores = tile_scores(left_rows, passage_block)
        weights = (
            jnp.exp(scores - level_rows[:, None]) + jnp.exp(scores - column_lse[None, :])
        ).astype(jnp.bfloat16)
        return jnp.dot(weights, passage_block, preferred_element_type=jnp.float32)

    results = lax.map(
        query_piece_work,
        (
            query_part.reshape(row_span // inner_rows, inner_rows, feature_width),
            level_part.reshape(row_span // inner_rows, inner_rows),
        ),
    )
    query_sum = lax.psum_scatter(
        results.reshape(row_span, feature_width), "pa", scatter_dimension=0, tiled=True
    )
    row_span = lax.axis_size("pb") * row_count
    level_part = column_lse
    inner_rows = math.gcd(row_span, 512)

    def passage_piece_work(inputs):
        left_rows, level_rows = inputs
        scores = tile_scores(left_rows, query_block)
        weights = (
            jnp.exp(scores - row_lse[None, :]) + jnp.exp(scores - level_rows[:, None])
        ).astype(jnp.bfloat16)
        return jnp.dot(weights, query_block, preferred_element_type=jnp.float32)

    results = lax.map(
        passage_piece_work,
        (
            passage_block.reshape(row_span // inner_rows, inner_rows, feature_width),
            level_part.reshape(row_span // inner_rows, inner_rows),
        ),
    )
    passage_sum = lax.psum_scatter(
        results.reshape(row_span, feature_width), "pb", scatter_dimension=0, tiled=True
    )
    grad_queries = 0.5 * (query_sum + hard_query - 2.0 * passage_own.astype(jnp.float32))
    grad_passages = 0.5 * (passage_sum + hard_passage - 2.0 * query_own.astype(jnp.float32))
    return (loss, grad_queries, grad_passages)


def solution(mesh):
    return jax.shard_map(
        per_device,
        mesh=mesh,
        in_specs=(
            P(("pb", "pa"), None),
            P(("pb", "pa"), None),
            P(("pb", "pa"), None),
            P(("pb", "pa")),
        ),
        out_specs=(P(), P(("pb", "pa"), None), P(("pb", "pa"), None)),
        check_vma=False,
    )
```

profile of v0, /device:TPU:0, one launch (start us, length us, event | category | flops | bytes accessed | tf_op | source)
XLA Modules:
  0.0 647.6 jit_solution(18313451305385212321)
XLA Ops:
  7.2 0.8 copy.18
  9.0 15.5 %scatter_custom_fusion = s32[5120]{0:T(1024)S(1)} fusion(s32[4096]{0:T(1024)S(1)} %bitcast.139, s32[4096]{0:T(1024)S(1)} %add_select_fusion, s32[]{:T(128)} %constant.162.clone.1), kind=kCustom, calls=%fused_computation.85 | custom fusion | bytes 20484 | tf_op jit(solution)/shard_map/scatter | solution.py:74
  25.3 7.3 %all-to-all-start = ((s32[32,1,160]{2,1,0:T(1,128)}), s32[32,1,160]{2,1,0:T(1,128)S(1)}, u32[]{:S(2)}, u32[]{:S(2)}) async-start(s32[32,1,160]{2,1,0:T(1,128)} %all_to_all.14), calls=%async_computation | async-start | bytes 65536 | tf_op jit(solution)/shard_map/all_to_all | solution.py:78
  32.6 1.0 fusion.48
  33.6 1.2 fusion.27
  34.8 5.0 all-to-all-done
  40.0 22.0 %gather_fusion = bf16[5120,768]{1,0:T(8,128)(2,1)} fusion(bf16[128,768]{1,0:T(8,128)(2,1)S(1)} %get-tuple-element.454, s32[5120]{0:T(1024)S(1)} %broadcast_clamp_fusion), kind=kCustom, calls=%fused_computation | custom fusion | bytes 15749120 | tf_op jit(solution)/shard_map/gather | solution.py:79
  62.0 3.6 all-to-all-start.1
  66.5 188.9 %all_gather.35 = bf16[512,768]{1,0:T(8,128)(2,1)S(1)} all-gather(bf16[128,768]{1,0:T(8,128)(2,1)S(1)} %get-tuple-element.454), channel_id=1, replica_groups=mesh['pb'=4,'pa'=8] {'pb'}, dimensions={0}, use_global_device_ids=true | all-gather | bytes 983040 | tf_op jit(solution)/shard_map/all_gather | solution.py:64
  255.4 4.6 while.68
  255.4 1.8 fusion.69
  257.7 1.8 fusion.69
  260.1 11.9 %all-gather.5 = f32[4,1,512]{2,1,0:T(1,128)S(1)} all-gather(f32[1,1,512]{2,1,0:T(1,128)S(1)} %bitcast.138), channel_id=3, replica_groups=mesh['pb'=4,'pa'=8] {'pb'}, dimensions={0}, use_global_device_ids=true | all-gather | bytes 10240 | tf_op jit(solution)/shard_map/all_gather | solution.py:10
  271.9 11.9 %all-gather.4 = f32[4,1,512]{2,1,0:T(1,128)S(1)} all-gather(f32[1,1,512]{2,1,0:T(1,128)S(1)} %bitcast.127), channel_id=2, replica_groups=mesh['pb'=4,'pa'=8] {'pb'}, dimensions={0}, use_global_device_ids=true | all-gather | bytes 10240 | tf_op jit(solution)/shard_map/all_gather | solution.py:10
  284.1 23.3 %gather_fusion.1 = bf16[4096,768]{1,0:T(8,128)(2,1)} fusion(bf16[5120,768]{1,0:T(8,128)(2,1)} %bitcast.14, s32[4096]{0:T(1024)S(1)} %broadcast_clamp_fusion.1), kind=kCustom, calls=%fused_computation.1 | custom fusion | bytes 12599296 | tf_op jit(solution)/shard_map/gather | solution.py:81
  307.4 4.5 fusion.30
  312.5 6.9 %all-gather.3 = f32[8,1,1024]{2,1,0:T(1,128)S(1)} all-gather(f32[1,1,1024]{2,1,0:T(1,128)S(1)} %bitcast_dynamic-update-slice_fusion.1), channel_id=1, replica_groups=mesh['pb'=4,'pa'=8] {'pa'}, dimensions={0}, use_global_device_ids=true | all-gather | bytes 36864 | tf_op jit(solution)/shard_map/all_gather | solution.py:10
  319.4 10.4 %all-gather.2 = f32[8,1,1024]{2,1,0:T(1,128)S(1)} all-gather(f32[1,1,1024]{2,1,0:T(1,128)S(1)} %get-tuple-element.451), channel_id=1, replica_groups=mesh['pb'=4,'pa'=8] {'pa'}, dimensions={0}, use_global_device_ids=true | all-gather | bytes 36864 | tf_op jit(solution)/shard_map/all_gather | solution.py:10
  331.8 5.5 bitcast_multiply_fusion
  337.3 24.7 %scatter_custom_fusion.1 = f32[5120,768]{1,0:T(8,128)} fusion(s32[4096]{0:T(1024)S(1)} %bitcast.141, f32[4096,768]{1,0:T(8,128)} %bitcast_multiply_fusion, f32[]{:T(128)} %constant.164.clone.1), kind=kCustom, calls=%fused_computation.32 | custom fusion | bytes 15729152 | tf_op jit(solution)/shard_map/scatter | solution.py:135
  362.0 9.3 %convert_element_type.74 = bf16[5120,768]{1,0:T(8,128)(2,1)} convert(f32[5120,768]{1,0:T(8,128)} %scatter_custom_fusion.1) | non-fusion elementwise | flops 3932160 | bytes 23592960 | tf_op jit(solution)/shard_map/convert_element_type | solution.py:138
  371.3 3.6 all-to-all-start.2
  375.0 5.6 while.67
  375.1 2.8 bitcast_dynamic-update-slice_fusion.4
  377.9 2.8 bitcast_dynamic-update-slice_fusion.4
  380.7 1.7 copy-done
  382.5 5.2 fusion.24
  389.3 206.0 %psum.7 = f32[]{:T(128)} all-reduce(f32[]{:T(128)S(6)} %add.230), channel_id=1, replica_groups=mesh['pb'=4,'pa'=8] {'pb','pa'}, use_global_device_ids=true, to_apply=%region_18.19 | all-reduce | flops 1 | bytes 8 | tf_op jit(solution)/shard_map/psum | solution.py:128
  595.9 3.7 fusion.33
  599.6 1.8 fusion.29
  601.5 36.7 %scatter_custom_fusion.2 = f32[128,768]{1,0:T(8,128)} fusion(f32[128,768]{1,0:T(8,128)} %reduce-scatter.5.cloned.1.call-done, s32[5120]{0:T(1024)S(1)} %bitcast.146, bf16[5120,768]{1,0:T(8,128)(2,1)} %bitcast.37), kind=kCustom, calls=%fused_computation.29 | custom fusion | flops 7864320 | bytes 8257536 | tf_op jit(solution)/shard_map/scatter-add | solution.py:147
  638.2 1.8 subtract_multiply_fusion
  (108 shorter events, 6.9 us)
Async XLA Ops:
  25.3 14.6 %all-to-all-start = ((s32[32,1,160]{2,1,0:T(1,128)}), s32[32,1,160]{2,1,0:T(1,128)S(1)}, u32[]{:S(2)}, u32[]{:S(2)}) async-start(s32[32,1,160]{2,1,0:T(1,128)} %all_to_all.14), calls=%async_computation | async-start | bytes 65536 | tf_op jit(solution)/shard_map/all_to_all | solution.py:78
  33.6 28.4 %copy-start.1 = (bf16[128,768]{1,0:T(8,128)(2,1)}, bf16[128,768]{1,0:T(8,128)(2,1)S(1)}, u32[]{:S(2)}) copy-start(bf16[128,768]{1,0:T(8,128)(2,1)S(1)} %get-tuple-element.449) | copy-start | bytes 589828
  39.8 22.2 %copy-start.5 = (s32[32,1,160]{2,1,0:T(1,128)}, s32[32,1,160]{2,1,0:T(1,128)S(1)}, u32[]{:S(2)}) copy-start(s32[32,1,160]{2,1,0:T(1,128)S(1)} %all-to-all-done) | copy-start | bytes 61444
  62.0 222.0 %all-to-all-start.1 = ((bf16[32,160,768]{2,1,0:T(8,128)(2,1)}), bf16[32,160,768]{2,1,0:T(8,128)(2,1)}, u32[]{:S(2)}, u32[]{:S(2)}) async-start(bf16[32,160,768]{2,1,0:T(8,128)(2,1)} %bitcast.117), calls=%async_computation.1 | async-start | bytes 15728640 | tf_op jit(solution)/shard_map/all_to_all | solution.py:80
  65.7 189.7 %all-gather.8.cloned.1.call-start = ((), (), s32[]{:S(2)}) async-start(), calls=%async_computation.5 | async-start | bytes 1769472 | tf_op jit(solution)/shard_map/all_gather | solution.py:63
  260.0 47.4 %copy-start.3 = (bf16[512,768]{1,0:T(8,128)(2,1)}, bf16[512,768]{1,0:T(8,128)(2,1)S(1)}, u32[]{:S(2)}) copy-start(bf16[512,768]{1,0:T(8,128)(2,1)S(1)} %get-tuple-element.739) | copy-start | bytes 2359300
  284.1 23.4 %copy-start.2 = (bf16[128,768]{1,0:T(8,128)(2,1)S(1)}, bf16[128,768]{1,0:T(8,128)(2,1)}, u32[]{:S(2)}) copy-start(bf16[128,768]{1,0:T(8,128)(2,1)} %copy-done.1) | copy-start | bytes 589828
  307.4 4.5 copy-start.7
  371.3 230.1 %all-to-all-start.2 = ((bf16[32,160,768]{2,1,0:T(8,128)(2,1)}), bf16[32,160,768]{2,1,0:T(8,128)(2,1)}, u32[]{:S(2)}, u32[]{:S(2)}) async-start(bf16[32,160,768]{2,1,0:T(8,128)(2,1)} %bitcast.116), calls=%async_computation.4 | async-start | bytes 15728640 | tf_op jit(solution)/shard_map/all_to_all | solution.py:137
  375.0 224.7 %reduce-scatter.3.cloned.1.call-start = ((), (), s32[]{:S(2)}) async-start(), calls=%async_computation.6 | async-start | bytes 3538944 | tf_op jit(solution)/shard_map/reduce_scatter | solution.py:169
  380.7 1.7 copy-start
  382.4 5.3 copy-start.6
  382.4 213.5 %copy-start.4 = (bf16[128,32,1]{1,0,2:T(8,128)(2,1)S(1)}, bf16[128,32,1]{1,0,2:T(8,128)(2,1)}, u32[]{:S(2)}) copy-start(bf16[128,32,1]{1,0,2:T(8,128)(2,1)} %get-tuple-element.461) | copy-start | bytes 24580
  382.4 219.0 %reduce-scatter.5.cloned.1.call-start = ((), (), s32[]{:S(2)}) async-start(), calls=%async_computation.7 | async-start | bytes 1966080 | tf_op jit(solution)/shard_map/reduce_scatter | solution.py:191
Sparse Core Ops, SparseCore 0:
  69.0 64.4 all-gather.7
  382.5 91.8 reduce-scatter.2
  476.8 62.4 reduce-scatter.4
where the time goes:
time: 649 us; the launch traced here: 648 us
  blocking collectives  436 us (67%)
  local copies, waits for them, and re-layouts  89.7 us (14%)
  other arithmetic  61 us (9%)
  matrix products  22.9 us (4%)
  between operations  17.2 us (3%)
  starting transfers between devices  14.7 us (2%)
    psum x1, blocking collectives, per_device(): loss = lax.psum(partial_loss, ('pb', 'pa')) / (2.0 * row_count * devices)  206 us
    all_gather x1, blocking collectives, per_device(): passage_block = lax.all_gather(passage_own, 'pb', axis=0, tiled=True)  189 us
    all_gather x4, blocking collectives, merged(): everything = jax.tree.map(lambda part: lax.all_gather(part, axis), value)  41.1 us
    scatter-add x1, other arithmetic, per_device(): hard_passage = jnp.zeros((row_count, feature_width), jnp.float32).at[aske...  36.7 us
    scatter x1, local copies, waits for them, and re-layouts, per_device(): contribution = jnp.zeros((devices * capacity, feature_width), jnp.float32...  24.7 us
    gather x1, local copies, waits for them, and re-layouts, per_device(): fetched.reshape(devices * capacity, feature_width)[slot_place]  23.3 us
    gather x1, local copies, waits for them, and re-layouts, per_device(): found_rows = passage_own[asked_rows]  22 us
    scatter x1, local copies, waits for them, and re-layouts, per_device(): request = jnp.zeros((devices * capacity,), jnp.int32).at[slot_place].set(...  15.5 us
  transfers between devices with their start and end apart: 6, of which 1 were waited for; matrix products, arithmetic and copies ran while one was open for 4% of the time, Pallas kernels for 0%

commit v1 on v0

v1 whole, which is shorter than its diff:
```python
import jax
import jax.numpy as jnp
from jax import lax
from jax.experimental import pallas as pl
from jax.experimental.pallas import tpu as pltpu
from jax.sharding import PartitionSpec as P

F32 = jnp.float32
BF16 = jnp.bfloat16
VMEM_LIMIT = 56 * 1024 * 1024
F16_TOP = 30000.0


def exchange(value, axis, turn):
    size = lax.axis_size(axis)
    return lax.ppermute(value, axis, [(i, i ^ turn) for i in range(size)])


def call(kernel, out_shape, scratch_shapes, cost, *operands, scalars=0):
    flops, moved = cost
    spaces = [pl.BlockSpec(memory_space=pltpu.SMEM)] * scalars
    spaces += [pl.BlockSpec(memory_space=pltpu.VMEM)] * (len(operands) - scalars)
    return pl.pallas_call(
        kernel,
        out_shape=out_shape,
        in_specs=spaces,
        out_specs=jax.tree.map(lambda _: pl.BlockSpec(memory_space=pltpu.VMEM), out_shape),
        scratch_shapes=scratch_shapes,
        compiler_params=pltpu.CompilerParams(vmem_limit_bytes=VMEM_LIMIT),
        cost_estimate=pl.CostEstimate(flops=flops, bytes_accessed=moved, transcendentals=0),
    )(*operands)


def count_listed(keys, row_slots, col_slots, rows, row_axis_size, place):
    listed = keys.shape[1]

    def kernel(place_ref, keys_ref, out_ref):
        down, across = place_ref[0], place_ref[1]
        steps = lax.broadcasted_iota(jnp.int32, (rows, rows), 0)

        def one_tile(index, carry):
            k, j = index // col_slots, index % col_slots
            base = ((down ^ j) * row_axis_size + across) * rows
            local = keys_ref[across ^ k] - base
            total = jnp.zeros((rows, rows), jnp.int32)
            for h in range(listed):
                total = total + jnp.where(local[h : h + 1, :] == steps, 1, 0)
            out_ref[
                pl.ds(pl.multiple_of(j * rows, rows), rows),
                pl.ds(pl.multiple_of(k * rows, rows), rows),
            ] = total.astype(F32).astype(BF16)
            return carry

        lax.fori_loop(0, row_slots * col_slots, one_tile, 0)

    tall, wide = row_slots * rows, col_slots * rows
    return call(
        kernel,
        jax.ShapeDtypeStruct((wide, tall), BF16),
        [],
        (tall * wide * listed * 3, tall * wide * 2),
        place,
        keys,
        scalars=1,
    )


def score_sweep(query_slots, passage_slots, counts):
    row_slots, col_slots = len(query_slots), len(passage_slots)
    rows, width = query_slots[0].shape
    tall, wide = row_slots * rows, col_slots * rows
    lanes = 2 * rows

    def kernel(*refs):
        q_refs, refs = refs[:row_slots], refs[row_slots:]
        p_refs, refs = refs[:col_slots], refs[col_slots:]
        c_ref, s_ref, row_ref, col_ref, q_all, p_all, top_acc, sum_acc = refs
        query_most = jnp.zeros((1, 1), F32)
        passage_most = jnp.zeros((1, 1), F32)
        for k in range(row_slots):
            part = q_refs[k][...]
            q_all[k * rows : (k + 1) * rows, :] = part
            most = jnp.max(jnp.abs(part.astype(F32)), axis=0, keepdims=True)
            query_most = jnp.maximum(query_most, jnp.max(most, axis=1, keepdims=True))
        for j in range(col_slots):
            part = p_refs[j][...]
            p_all[j * rows : (j + 1) * rows, :] = part
            most = jnp.max(jnp.abs(part.astype(F32)), axis=0, keepdims=True)
            passage_most = jnp.maximum(passage_most, jnp.max(most, axis=1, keepdims=True))
        row_ref[...] = jnp.zeros_like(row_ref)
        col_ref[...] = jnp.zeros_like(col_ref)
        row_ref[2:3, :] = jnp.broadcast_to(passage_most, (1, tall))
        col_ref[2:3, :] = jnp.broadcast_to(query_most, (1, wide))
        top_acc[...] = jnp.full_like(top_acc, -jnp.inf)
        sum_acc[...] = jnp.zeros_like(sum_acc)

        def first(t, carry):
            spot = pl.ds(pl.multiple_of(t * lanes, lanes), lanes)
            s_ref[:, spot] = lax.dot_general(
                p_all[...], q_all[spot, :], (((1,), (1,)), ((), ())), preferred_element_type=F32
            )
            top = jnp.full((1, lanes), -jnp.inf, F32)
            for j in range(col_slots):
                part = s_ref[j * rows : (j + 1) * rows, spot]
                top = jnp.maximum(top, jnp.max(part, axis=0, keepdims=True))
                here = slice(j * rows, (j + 1) * rows)
                top_acc[here, :] = jnp.maximum(
                    top_acc[here, :], jnp.maximum(part[:, :rows], part[:, rows:])
                )
            total = jnp.zeros((1, lanes), F32)
            for j in range(col_slots):
                here = slice(j * rows, (j + 1) * rows)
                times = 1.0 + c_ref[here, spot].astype(F32)
                total = total + jnp.sum(
                    jnp.exp(s_ref[here, spot] - top) * times, axis=0, keepdims=True
                )
            row_ref[0:1, spot] = top
            row_ref[1:2, spot] = total
            return carry

        lax.fori_loop(0, tall // lanes, first, 0)
        for j in range(col_slots):
            here = slice(j * rows, (j + 1) * rows)
            acc = top_acc[here, :]
            col_ref[0:1, here] = jnp.max(acc.T, axis=0, keepdims=True)
            top_acc[here, :] = jnp.broadcast_to(
                jnp.max(acc, axis=1, keepdims=True), (rows, rows)
            )

        def second(t, carry):
            spot = pl.ds(pl.multiple_of(t * rows, rows), rows)
            for j in range(col_slots):
                here = slice(j * rows, (j + 1) * rows)
                sum_acc[here, :] += jnp.exp(s_ref[here, spot] - top_acc[here, :])
            return carry

        lax.fori_loop(0, row_slots, second, 0)
        for j in range(col_slots):
            here = slice(j * rows, (j + 1) * rows)
            col_ref[1:2, here] = jnp.sum(sum_acc[here, :].T, axis=0, keepdims=True)

    return call(
        kernel,
        (
            jax.ShapeDtypeStruct((wide, tall), F32),
            jax.ShapeDtypeStruct((8, tall), F32),
            jax.ShapeDtypeStruct((8, wide), F32),
        ),
        [
            pltpu.VMEM((tall, width), BF16),
            pltpu.VMEM((wide, width), BF16),
            pltpu.VMEM((wide, rows), F32),
            pltpu.VMEM((wide, rows), F32),
        ],
        (2 * tall * wide * width, tall * wide * 6),
        *query_slots,
        *passage_slots,
        counts,
    )


def turned(value, turn, rows):
    slots = value.shape[1] // rows
    return jnp.concatenate(
        [value[:, (k ^ turn) * rows : ((k ^ turn) + 1) * rows] for k in range(slots)], axis=1
    )


def join(messages, turns, rows):
    values = [turned(m, t, rows) for m, t in zip(messages, turns)]
    top = values[0][0:1]
    most = values[0][2:3]
    for v in values[1:]:
        top = jnp.maximum(top, v[0:1])
        most = jnp.maximum(most, v[2:3])
    total = jnp.zeros_like(top)
    for v in values:
        total = total + v[1:2] * jnp.exp(v[0:1] - top)
    return top, total, most


def join_pair(own, other, rows):
    def kernel(own_ref, other_ref, out_ref):
        top, total, most = join([own_ref[...], other_ref[...]], [0, 1], rows)
        out_ref[...] = jnp.zeros_like(out_ref)
        out_ref[0:1, :] = top
        out_ref[1:2, :] = total
        out_ref[2:3, :] = most

    return call(
        kernel, jax.ShapeDtypeStruct(own.shape, F32), [], (own.size * 4, own.size * 8), own, other
    )


def weight_sweep(scores, counts, row_stats, row_turns, col_stats, col_turns, query_slots):
    rows, width = query_slots[0].shape
    wide, tall = scores.shape
    row_slots, col_slots = tall // rows, wide // rows
    n_row, n_col = len(row_stats), len(col_stats)

    def kernel(*refs):
        s_ref, c_ref, refs = refs[0], refs[1], refs[2:]
        r_refs, refs = refs[:n_row], refs[n_row:]
        k_refs, refs = refs[:n_col], refs[n_col:]
        q_refs, refs = refs[:row_slots], refs[row_slots:]
        hi_ref, lo_ref, own_ref = refs[:3]
        out_refs, refs = refs[3 : 2 + col_slots], refs[2 + col_slots :]
        info_ref, q_all, row_level, col_level = refs
        for k in range(row_slots):
            q_all[k * rows : (k + 1) * rows, :] = q_refs[k][...]
        top, total, passage_most = join([r[...] for r in r_refs], row_turns, rows)
        row_level[...] = top + jnp.log(total)
        top, total, query_most = join([r[...] for r in k_refs], col_turns, rows)
        columns = top + jnp.log(total)
        for j in range(col_slots):
            here = slice(j * rows, (j + 1) * rows)
            col_level[here, :] = jnp.broadcast_to(columns[:, here], (rows, rows)).T
        unit = (
            lax.broadcasted_iota(jnp.int32, (rows, rows), 0)
            == lax.broadcasted_iota(jnp.int32, (rows, rows), 1)
        ).astype(F32)
        for j in range(col_slots):
            here = slice(j * rows, (j + 1) * rows)

            def one(k, carry, here=here, j=j):
                spot = pl.ds(pl.multiple_of(k * rows, rows), rows)
                part = s_ref[here, spot]
                by_row = jnp.exp(part - row_level[:, spot])
                by_col = jnp.exp(part - col_level[here, :])
                pair = (by_row + by_col).astype(BF16).astype(F32)
                hard = by_row.astype(BF16).astype(F32)
                weight = pair + hard * c_ref[here, spot].astype(F32)
                if j == 0:
                    weight = weight - unit * jnp.where(k == 0, 2.0, 0.0)
                high = weight.astype(BF16)
                hi_ref[here, spot] = high
                lo_ref[here, spot] = (weight - high.astype(F32)).astype(BF16)
                return carry

            lax.fori_loop(0, row_slots, one, 0)
        query_scale = F16_TOP / jnp.maximum(query_most[:, :1] * (tall * 1.02 + 8.0), 1e-30)
        passage_scale = F16_TOP / jnp.maximum(
            passage_most[:, :1] * (2 * wide * 1.02 + 8.0), 1e-30
        )
        for j in range(col_slots):
            here = slice(j * rows, (j + 1) * rows)
            part = jnp.dot(hi_ref[here, :], q_all[...], preferred_element_type=F32)
            part = part + jnp.dot(lo_ref[here, :], q_all[...], preferred_element_type=F32)
            if j == 0:
                own_ref[...] = part
            else:
                out_refs[j - 1][...] = part * query_scale
        diagonal = jnp.sum(unit * s_ref[:rows, :rows], axis=0, keepdims=True)
        losses = row_level[:, :rows] + columns[:, :rows] - 2.0 * diagonal
        info_ref[...] = jnp.zeros_like(info_ref)
        info_ref[0:1, :] = jnp.broadcast_to(jnp.sum(losses, axis=1, keepdims=True), (1, rows))
        info_ref[1:2, :] = jnp.broadcast_to(query_scale, (1, rows))
        info_ref[2:3, :] = jnp.broadcast_to(passage_scale, (1, rows))

    block = jax.ShapeDtypeStruct((rows, width), F32)
    return call(
        kernel,
        (
            jax.ShapeDtypeStruct((wide, tall), BF16),
            jax.ShapeDtypeStruct((wide, tall), BF16),
            block,
            *[block] * (col_slots - 1),
            jax.ShapeDtypeStruct((8, rows), F32),
        ),
        [
            pltpu.VMEM((tall, width), BF16),
            pltpu.VMEM((1, tall), F32),
            pltpu.VMEM((wide, rows), F32),
        ],
        (4 * tall * wide * width, tall * wide * 10),
        scores,
        counts,
        *row_stats,
        *col_stats,
        *query_slots,
    )


def query_sweep(high, low, passage_slots):
    rows, width = passage_slots[0].shape
    wide, tall = high.shape
    row_slots, col_slots = tall // rows, wide // rows

    def kernel(*refs):
        hi_ref, lo_ref, refs = refs[0], refs[1], refs[2:]
        p_refs, refs = refs[:col_slots], refs[col_slots:]
        even_ref, odd_ref, p_all = refs
        for j in range(col_slots):
            p_all[j * rows : (j + 1) * rows, :] = p_refs[j][...]

        def one(m, carry):
            spot = pl.ds(pl.multiple_of(m * 2 * rows, 2 * rows), 2 * rows)
            dims = (((0,), (0,)), ((), ()))
            part = lax.dot_general(
                hi_ref[:, spot], p_all[...], dims, preferred_element_type=F32
            ) + lax.dot_general(lo_ref[:, spot], p_all[...], dims, preferred_element_type=F32)
            even_ref[m] = part[:rows]
            odd_ref[m] = part[rows:]
            return carry

        lax.fori_loop(0, row_slots // 2, one, 0)

    half = jax.ShapeDtypeStruct((row_slots // 2, rows, width), F32)
    return call(
        kernel,
        (half, half),
        [pltpu.VMEM((wide, width), BF16)],
        (4 * tall * wide * width, tall * wide * 4 + tall * width * 4),
        high,
        low,
        *passage_slots,
    )


def per_device(queries, passages, hard_ids, list_lengths):
    rows, width = queries.shape
    listed = hard_ids.shape[1]
    across = lax.axis_size("pa")
    down = lax.axis_size("pb")
    query_own = queries.astype(BF16)
    passage_own = passages.astype(BF16)

    live = jnp.arange(listed, dtype=jnp.int32)[None, :] < list_lengths[:, None]
    keys = jnp.where(live, hard_ids, -1).T
    keys = lax.all_gather(keys, "pa")
    place = jnp.stack([lax.axis_index("pb"), lax.axis_index("pa")]).astype(jnp.int32)
    counts = count_listed(keys, across, down, rows, across, place)

    passage_slots = [passage_own] + [exchange(passage_own, "pb", j) for j in range(1, down)]
    even = [query_own] + [exchange(query_own, "pa", k) for k in range(2, across, 2)]
    odd = [exchange(part, "pa", 1) for part in even]
    query_slots = [part for pair in zip(even, odd) for part in pair]

    scores, row_message, col_message = score_sweep(query_slots, passage_slots, counts)
    col_stats = [col_message] + [exchange(col_message, "pb", j) for j in range(1, down)]
    pair_message = join_pair(row_message, exchange(row_message, "pa", 1), rows)
    row_turns = list(range(0, across, 2))
    row_stats = [pair_message] + [exchange(pair_message, "pa", k) for k in row_turns[1:]]

    high, low, *blocks, info = weight_sweep(
        scores, counts, row_stats, row_turns, col_stats, list(range(down)), query_slots
    )
    passage_sum, sent = blocks[0], blocks[1:]
    arrived = [
        exchange(part.astype(jnp.float16), "pb", j) for j, part in enumerate(sent, start=1)
    ]
    even_sum, odd_sum = query_sweep(high, low, passage_slots)
    even_sum = even_sum + exchange(odd_sum, "pa", 1)
    passage_scale = info[2, 0]
    query_scale = info[1, 0]
    returned = [
        exchange((even_sum[k // 2] * passage_scale).astype(jnp.float16), "pa", k)
        for k in row_turns[1:]
    ]
    loss = info[0, 0]
    for axis, size in (("pa", across), ("pb", down)):
        turn = 1
        while turn < size:
            loss = loss + exchange(loss, axis, turn)
            turn *= 2
    loss = loss / (2.0 * rows * across * down)
    back = 0.5 / query_scale
    grad_passages = 0.5 * passage_sum + sum(part.astype(F32) for part in arrived) * back
    back = 0.5 / passage_scale
    grad_queries = 0.5 * even_sum[0] + sum(part.astype(F32) for part in returned) * back
    return (loss, grad_queries, grad_passages)


def solution(mesh):
    return jax.shard_map(
        per_device,
        mesh=mesh,
        in_specs=(
            P(("pb", "pa"), None),
            P(("pb", "pa"), None),
            P(("pb", "pa"), None),
            P(("pb", "pa")),
        ),
        out_specs=(P(), P(("pb", "pa"), None), P(("pb", "pa"), None)),
        check_vma=False,
    )
```

time: 649 us -> 124 us (0.19)
  blocking collectives: 436 us -> 10.2 us
  local copies, waits for them, and re-layouts: 89.7 us -> 4.09 us
  other arithmetic: 61 us -> 9.1 us
  Pallas kernels: 0 us -> 30.8 us
  starting transfers between devices: 14.7 us -> 44 us
  matrix products: 22.9 us -> 0 us
  waiting for transfers between devices: 5.74 us -> 18.7 us
  between operations: 17.2 us -> 6.86 us
    all_gather x5 -> x1, blocking collectives: 230 us -> 10.2 us  [per_device(): keys = lax.all_gather(keys, 'pa')]
    psum x1 -> x0, blocking collectives: 206 us -> none  [per_device(): loss = lax.psum(partial_loss, ('pb', 'pa')) / (2.0 * row_count * devices)]
    gather x2 -> x0, local copies, waits for them, and re-layouts: 45.4 us -> none  [the longest x1 23.3 us: per_device(): fetched.reshape(devices * capacity, feature_width)[slot_place]]
    ppermute x0 -> x29, starting transfers between devices: none -> 44 us  [exchange(): return lax.ppermute(value, axis, [(i, i ^ turn) for i in range(size)])]
    scatter x2 -> x0, local copies, waits for them, and re-layouts: 40.2 us -> none  [the longest x1 24.7 us: per_device(): contribution = jnp.zeros((devices * capacity, feature_width), jnp.float32...]
    scatter-add x1 -> x0, other arithmetic: 36.7 us -> none  [per_device(): hard_passage = jnp.zeros((row_count, feature_width), jnp.float32).at[aske...]
    pallas_call x0 -> x5, Pallas kernels: none -> 30.8 us  [call(): pl.pallas_call(kernel, out_shape=out_shape, in_specs=spaces, out_specs=ja...]
    dot_general x8 -> x0, matrix products: 22.9 us -> none  [the longest x2 5.55 us: query_piece_work(): return jnp.dot(weights, passage_block, preferred_element_type=jnp.float32)]
  transfers between devices with their start and end apart: 6 -> 29, of which waited for: 1 -> 10; matrix products, arithmetic and copies ran while one was open for 4% -> 7% of each run, Pallas kernels for 0% -> 9%
where the time goes in v1:
time: 124 us
  starting transfers between devices  44 us (35%)
  Pallas kernels  30.8 us (25%)
  waiting for transfers between devices  18.7 us (15%)
  blocking collectives  10.2 us (8%)
  other arithmetic  9.1 us (7%)
  between operations  6.86 us (6%)
  local copies, waits for them, and re-layouts  4.09 us (3%)
    ppermute x29, starting transfers between devices, exchange(): return lax.ppermute(value, axis, [(i, i ^ turn) for i in range(size)])  44 us
    pallas_call x5, Pallas kernels, call(): pl.pallas_call(kernel, out_shape=out_shape, in_specs=spaces, out_specs=ja...  30.8 us
    ppermute x29, waiting for transfers between devices, exchange(): return lax.ppermute(value, axis, [(i, i ^ turn) for i in range(size)])  18.7 us
    all_gather x1, blocking collectives, per_device(): keys = lax.all_gather(keys, 'pa')  10.2 us
    unnamed x48, local copies, waits for them, and re-layouts  2.7 us
  transfers between devices with their start and end apart: 29, of which 10 were waited for; matrix products, arithmetic and copies ran while one was open for 7% of the time, Pallas kernels for 9%

profile of v1, /device:TPU:0, one launch (start us, length us, event | category | flops | bytes accessed | tf_op | source)
XLA Modules:
  0.0 123.8 jit_solution(10779971948958858767)
XLA Ops:
  0.6 1.0 convert_element_type.52.refs_8_.refs_2_
  1.7 5.1 %collective-permute-start.9 = (bf16[128,768]{1,0:T(8,128)(2,1)S(1)}, bf16[128,768]{1,0:T(8,128)(2,1)S(1)}, u32[]{:S(2)}, u32[]{:S(2)}) collective-permute-start(bf16[128,768]{1,0:T(8,128)(2,1)S(1)} %convert_element_type.52.refs_8_.refs_2_), channel_id=1, source_target_pairs={{0,24},{8,16},{16,8},{24,0},{1,25},{9,17},{17,9},{25,1},{2,26},{10... | collective-permute-start | bytes 589832 | tf_op jit(solution)/shard_map/ppermute | solution.py:16
  6.8 1.0 convert_element_type.51.refs_0_.refs_10_
  7.8 2.5 %collective-permute-start.5 = (bf16[128,768]{1,0:T(8,128)(2,1)S(1)}, bf16[128,768]{1,0:T(8,128)(2,1)S(1)}, u32[]{:S(2)}, u32[]{:S(2)}) collective-permute-start(bf16[128,768]{1,0:T(8,128)(2,1)S(1)} %convert_element_type.51.refs_0_.refs_10_), channel_id=1, source_target_pairs={{0,6},{1,7},{2,4},{3,5},{4,2},{5,3},{6,0},{7,1},{8,14},{9,15},{10,... | collective-permute-start | bytes 589832 | tf_op jit(solution)/shard_map/ppermute | solution.py:16
  11.4 1.2 %collective-permute-done.9.refs_11_.refs_5_ = bf16[128,768]{1,0:T(8,128)(2,1)S(1)} collective-permute-done((bf16[128,768]{1,0:T(8,128)(2,1)S(1)}, bf16[128,768]{1,0:T(8,128)(2,1)S(1)}, u32[]{:S(2)}, u32[]{:S(2)}) %collective-permute-start.9) | collective-permute-done | bytes 196640 | tf_op jit(solution)/shard_map/ppermute | solution.py:16
  12.6 8.2 %collective-permute-start.7 = (bf16[128,768]{1,0:T(8,128)(2,1)S(1)}, bf16[128,768]{1,0:T(8,128)(2,1)S(1)}, u32[]{:S(2)}, u32[]{:S(2)}) collective-permute-start(bf16[128,768]{1,0:T(8,128)(2,1)S(1)} %convert_element_type.52.refs_8_.refs_2_), channel_id=1, source_target_pairs={{0,8},{8,0},{16,24},{24,16},{1,9},{9,1},{17,25},{25,17},{2,10},{10... | collective-permute-start | bytes 589832 | tf_op jit(solution)/shard_map/ppermute | solution.py:16
  20.8 2.8 %collective-permute-done.8.refs_10_.refs_4_ = bf16[128,768]{1,0:T(8,128)(2,1)S(1)} collective-permute-done((bf16[128,768]{1,0:T(8,128)(2,1)S(1)}, bf16[128,768]{1,0:T(8,128)(2,1)S(1)}, u32[]{:S(2)}, u32[]{:S(2)}) %collective-permute-start.8) | collective-permute-done | bytes 196640 | tf_op jit(solution)/shard_map/ppermute | solution.py:16
  25.3 10.2 %all-gather = s32[256,128]{1,0:T(8,128)} all-gather(s32[32,128]{1,0:T(8,128)S(1)} %select_bitcast_fusion), channel_id=2, replica_groups=mesh['pb'=4,'pa'=8] {'pa'}, dimensions={0}, use_global_device_ids=true | all-gather | bytes 147456 | tf_op jit(solution)/shard_map/all_gather | solution.py:330
  36.2 9.9 %shard_map.67.refs_12_.refs_1_ = bf16[512,1024]{1,0:T(8,128)(2,1)} custom-call(s32[2]{0:T(128)} %pad_add_fusion.place_ref, s32[8,32,128]{2,1,0:T(8,128)} %bitcast.18), custom_call_target="tpu_custom_call" | custom-call | flops 50331648 | bytes 1048576 | tf_op jit(solution)/shard_map/pallas_call | solution.py:23
  47.7 6.7 %shard_map.68 = (f32[512,1024]{1,0:T(8,128)}, f32[8,1024]{1,0:T(8,128)}, f32[8,512]{1,0:T(8,128)}) custom-call(bf16[128,768]{1,0:T(8,128)(2,1)} %copy-done.2, bf16[128,768]{1,0:T(8,128)(2,1)} %copy-done.13, bf16[128,768]{1,0:T(8,128)(2,1)} %copy-done.12, bf16[128,768]{1,0:T(8,128)(2,1)} %copy-done.16, bf16[128,768]{1,0:T(8,128)(2,1)} %copy-done.11, ...), custom_call_target="tpu_custom_call" | custom-call | flops 805306368 | bytes 3145728 | tf_op jit(solution)/shard_map/pallas_call | solution.py:23
  54.7 2.5 %collective-permute-start.16 = (f32[8,512]{1,0:T(8,128)}, f32[8,512]{1,0:T(8,128)S(1)}, u32[]{:S(2)}, u32[]{:S(2)}) collective-permute-start(f32[8,512]{1,0:T(8,128)} %get-tuple-element.17.refs_6_), channel_id=1, source_target_pairs={{0,24},{8,16},{16,8},{24,0},{1,25},{9,17},{17,9},{25,1},{2,26},{10... | collective-permute-start | bytes 49160 | tf_op jit(solution)/shard_map/ppermute | solution.py:16
  57.8 1.4 %shard_map.69.refs_2_ = f32[8,1024]{1,0:T(8,128)} custom-call(f32[8,1024]{1,0:T(8,128)} %get-tuple-element.16.own_ref, f32[8,1024]{1,0:T(8,128)} %copy-done.17), custom_call_target="tpu_custom_call" | custom-call | flops 32768 | bytes 65536 | tf_op jit(solution)/shard_map/pallas_call | solution.py:23
  59.2 1.4 %collective-permute-start.13 = (f32[8,1024]{1,0:T(8,128)}, f32[8,1024]{1,0:T(8,128)S(1)}, u32[]{:S(2)}, u32[]{:S(2)}) collective-permute-start(f32[8,1024]{1,0:T(8,128)} %shard_map.69.refs_2_), channel_id=1, source_target_pairs={{0,6},{1,7},{2,4},{3,5},{4,2},{5,3},{6,0},{7,1},{8,14},{9,15},{10,... | collective-permute-start | bytes 98312 | tf_op jit(solution)/shard_map/ppermute | solution.py:16
  60.7 1.5 %collective-permute-start.12 = (f32[8,1024]{1,0:T(8,128)}, f32[8,1024]{1,0:T(8,128)S(1)}, u32[]{:S(2)}, u32[]{:S(2)}) collective-permute-start(f32[8,1024]{1,0:T(8,128)} %shard_map.69.refs_2_), channel_id=1, source_target_pairs={{0,4},{1,5},{2,6},{3,7},{4,0},{5,1},{6,2},{7,3},{8,12},{9,13},{10,... | collective-permute-start | bytes 98312 | tf_op jit(solution)/shard_map/ppermute | solution.py:16
  62.7 1.9 %collective-permute-start.14 = (f32[8,512]{1,0:T(8,128)}, f32[8,512]{1,0:T(8,128)S(1)}, u32[]{:S(2)}, u32[]{:S(2)}) collective-permute-start(f32[8,512]{1,0:T(8,128)} %get-tuple-element.17.refs_6_), channel_id=1, source_target_pairs={{0,8},{8,0},{16,24},{24,16},{1,9},{9,1},{17,25},{25,17},{2,10},{10... | collective-permute-start | bytes 49160 | tf_op jit(solution)/shard_map/ppermute | solution.py:16
  64.6 2.9 %collective-permute-done.15.refs_8_ = f32[8,512]{1,0:T(8,128)S(1)} collective-permute-done((f32[8,512]{1,0:T(8,128)}, f32[8,512]{1,0:T(8,128)S(1)}, u32[]{:S(2)}, u32[]{:S(2)}) %collective-permute-start.15) | collective-permute-done | bytes 16416 | tf_op jit(solution)/shard_map/ppermute | solution.py:16
  68.2 6.8 %shard_map.70 = (bf16[512,1024]{1,0:T(8,128)(2,1)}, bf16[512,1024]{1,0:T(8,128)(2,1)}, f32[128,768]{1,0:T(8,128)}, f32[128,768]{1,0:T(8,128)}, f32[128,768]{1,0:...) custom-call(f32[512,1024]{1,0:T(8,128)} %get-tuple-element.15.refs_0_, bf16[512,1024]{1,0:T(8,128)(2,1)} %shard_map.67.refs_12_.refs_1_, ...), custom_call_target="tpu_custom_call" | custom-call | flops 1610612736 | bytes 5242880 | tf_op jit(solution)/shard_map/pallas_call | solution.py:23
  75.0 6.0 %shard_map.71 = (f32[4,128,768]{2,1,0:T(8,128)}, f32[4,128,768]{2,1,0:T(8,128)}) custom-call(bf16[512,1024]{1,0:T(8,128)(2,1)} %get-tuple-element.19.refs_0_, bf16[512,1024]{1,0:T(8,128)(2,1)} %get-tuple-element.20.refs_1_, bf16[128,768]{1,0:T(8,128)(2,1)} %copy-done.1, bf16[128,768]{1,0:T(8,128)(2,1)} %copy-done.9, bf16[128,768]{1,0:T(8,128)(2,1)} %copy-done.8, ...), custom_call_target="tpu_custom_call" | custom-call | flops 1610612736 | bytes 5242880 | tf_op jit(solution)/shard_map/pallas_call | solution.py:23
  81.0 1.4 %fusion.8 = (f32[1,1]{1,0:T(1,128)}, f32[1,1]{1,0:T(1,128)}, f32[1,1]{1,0:T(1,128)}) fusion(f32[8,128]{1,0:T(8,128)} %get-tuple-element.18), kind=kLoop, calls=%fused_computation.16 | loop fusion | bytes 24 | tf_op jit(solution)/shard_map/slice | solution.py:355
  85.0 1.5 %collective-permute-start.28 = (f16[128,768]{1,0:T(8,128)(2,1)}, f16[128,768]{1,0:T(8,128)(2,1)S(1)}, u32[]{:S(2)}, u32[]{:S(2)}) collective-permute-start(f16[128,768]{1,0:T(8,128)(2,1)} %convert_element_type.66), channel_id=1, source_target_pairs={{0,24},{8,16},{16,8},{24,0},{1,25},{9,17},{17,9},{25,1},{2,26},{10... | collective-permute-start | bytes 589832 | tf_op jit(solution)/shard_map/ppermute | solution.py:16
  87.5 1.9 %collective-permute-start.26 = (f16[128,768]{1,0:T(8,128)(2,1)}, f16[128,768]{1,0:T(8,128)(2,1)}, u32[]{:S(2)}, u32[]{:S(2)}) collective-permute-start(f16[128,768]{1,0:T(8,128)(2,1)} %convert_element_type.62), channel_id=1, source_target_pairs={{0,8},{8,0},{16,24},{24,16},{1,9},{9,1},{17,25},{25,17},{2,10},{10... | collective-permute-start | bytes 589832 | tf_op jit(solution)/shard_map/ppermute | solution.py:16
  92.0 2.8 %collective-permute-start.18 = (f32[]{:T(128)}, f32[]{:T(128)}, u32[]{:S(2)}, u32[]{:S(2)}) collective-permute-start(f32[]{:T(128)} %add.36), channel_id=1, source_target_pairs={{0,2},{1,3},{2,0},{3,1},{4,6},{5,7},{6,4},{7,5},{8,10},{9,11},{10,... | collective-permute-start | bytes 20 | tf_op jit(solution)/shard_map/ppermute | solution.py:16
  96.2 2.8 %collective-permute-start.19 = (f32[]{:T(128)}, f32[]{:T(128)}, u32[]{:S(2)}, u32[]{:S(2)}) collective-permute-start(f32[]{:T(128)} %add.37), channel_id=1, source_target_pairs={{0,4},{1,5},{2,6},{3,7},{4,0},{5,1},{6,2},{7,3},{8,12},{9,13},{10,... | collective-permute-start | bytes 20 | tf_op jit(solution)/shard_map/ppermute | solution.py:16
  100.5 1.5 %collective-permute-start.20 = (f32[]{:T(128)}, f32[]{:T(128)}, u32[]{:S(2)}, u32[]{:S(2)}) collective-permute-start(f32[]{:T(128)} %add.38), channel_id=1, source_target_pairs={{0,8},{8,0},{16,24},{24,16},{1,9},{9,1},{17,25},{25,17},{2,10},{10... | collective-permute-start | bytes 20 | tf_op jit(solution)/shard_map/ppermute | solution.py:16
  102.0 2.3 %collective-permute-done.20 = f32[]{:T(128)} collective-permute-done((f32[]{:T(128)}, f32[]{:T(128)}, u32[]{:S(2)}, u32[]{:S(2)}) %collective-permute-start.20) | collective-permute-done | bytes 36 | tf_op jit(solution)/shard_map/ppermute | solution.py:16
  104.8 2.4 %collective-permute-start.21 = (f32[]{:T(128)}, f32[]{:T(128)}, u32[]{:S(2)}, u32[]{:S(2)}) collective-permute-start(f32[]{:T(128)} %add.39), channel_id=1, source_target_pairs={{0,16},{8,24},{16,0},{24,8},{1,17},{9,25},{17,1},{25,9},{2,18},{10... | collective-permute-start | bytes 20 | tf_op jit(solution)/shard_map/ppermute | solution.py:16
  107.2 2.2 %collective-permute-done.21 = f32[]{:T(128)} collective-permute-done((f32[]{:T(128)}, f32[]{:T(128)}, u32[]{:S(2)}, u32[]{:S(2)}) %collective-permute-start.21) | collective-permute-done | bytes 36 | tf_op jit(solution)/shard_map/ppermute | solution.py:16
  111.0 1.5 %collective-permute-start.23 = (f16[128,768]{1,0:T(8,128)(2,1)S(1)}, f16[128,768]{1,0:T(8,128)(2,1)S(1)}, u32[]{:S(2)}, u32[]{:S(2)}) collective-permute-start(f16[128,768]{1,0:T(8,128)(2,1)S(1)} %get-tuple-element.27), channel_id=1, source_target_pairs={{0,2},{1,3},{2,0},{3,1},{4,6},{5,7},{6,4},{7,5},{8,10},{9,11},{10,... | collective-permute-start | bytes 589832 | tf_op jit(solution)/shard_map/ppermute | solution.py:16
  112.6 1.5 %collective-permute-start.25 = (f16[128,768]{1,0:T(8,128)(2,1)S(1)}, f16[128,768]{1,0:T(8,128)(2,1)S(1)}, u32[]{:S(2)}, u32[]{:S(2)}) collective-permute-start(f16[128,768]{1,0:T(8,128)(2,1)S(1)} %get-tuple-element.28), channel_id=1, source_target_pairs={{0,6},{1,7},{2,4},{3,5},{4,2},{5,3},{6,0},{7,1},{8,14},{9,15},{10,... | collective-permute-start | bytes 589832 | tf_op jit(solution)/shard_map/ppermute | solution.py:16
  114.6 1.8 %multiply_add_fusion = f32[128,768]{1,0:T(8,128)} fusion(f16[128,768]{1,0:T(8,128)(2,1)S(1)} %collective-permute-done.28, f16[128,768]{1,0:T(8,128)(2,1)S(1)} %collective-permute-done.27, f16[128,768]{1,0:T(8,128)(2,1)} %collective-permute-done.26, f32[128,768]{1,0:T(8,128)S(1)} %copy-done.6, f32[]{:T(128)} %bitcast.10), kind=kLoop, calls=%fused_computation.9 | loop fusion | flops 786432 | bytes 1376260 | tf_op jit(solution)/shard_map/add | solution.py:368
  116.8 3.1 %collective-permute-done.25 = f16[128,768]{1,0:T(8,128)(2,1)S(1)} collective-permute-done((f16[128,768]{1,0:T(8,128)(2,1)S(1)}, f16[128,768]{1,0:T(8,128)(2,1)S(1)}, u32[]{:S(2)}, u32[]{:S(2)}) %collective-permute-start.25) | collective-permute-done | bytes 196640 | tf_op jit(solution)/shard_map/ppermute | solution.py:16
  119.9 1.9 %collective-permute-done.24 = f16[128,768]{1,0:T(8,128)(2,1)S(1)} collective-permute-done((f16[128,768]{1,0:T(8,128)(2,1)S(1)}, f16[128,768]{1,0:T(8,128)(2,1)S(1)}, u32[]{:S(2)}, u32[]{:S(2)}) %collective-permute-start.24) | collective-permute-done | bytes 196640 | tf_op jit(solution)/shard_map/ppermute | solution.py:16
  (92 shorter events, 15.2 us)
Async XLA Ops:
  1.7 44.5 %copy-start.1 = (bf16[128,768]{1,0:T(8,128)(2,1)}, bf16[128,768]{1,0:T(8,128)(2,1)S(1)}, u32[]{:S(2)}) copy-start(bf16[128,768]{1,0:T(8,128)(2,1)S(1)} %convert_element_type.52.refs_8_.refs_2_) | copy-start | bytes 589828
  1.7 10.9 %collective-permute-start.9 = (bf16[128,768]{1,0:T(8,128)(2,1)S(1)}, bf16[128,768]{1,0:T(8,128)(2,1)S(1)}, u32[]{:S(2)}, u32[]{:S(2)}) collective-permute-start(bf16[128,768]{1,0:T(8,128)(2,1)S(1)} %convert_element_type.52.refs_8_.refs_2_), channel_id=1, source_target_pairs={{0,24},{8,16},{16,8},{24,0},{1,25},{9,17},{17,9},{25,1},{2,26},{10... | collective-permute-start | bytes 589832 | tf_op jit(solution)/shard_map/ppermute | solution.py:16
  6.8 16.8 %collective-permute-start.8 = (bf16[128,768]{1,0:T(8,128)(2,1)S(1)}, bf16[128,768]{1,0:T(8,128)(2,1)S(1)}, u32[]{:S(2)}, u32[]{:S(2)}) collective-permute-start(bf16[128,768]{1,0:T(8,128)(2,1)S(1)} %convert_element_type.52.refs_8_.refs_2_), channel_id=1, source_target_pairs={{0,16},{8,24},{16,0},{24,8},{1,17},{9,25},{17,1},{25,9},{2,18},{10... | collective-permute-start | bytes 589832 | tf_op jit(solution)/shard_map/ppermute | solution.py:16
  7.8 38.4 %copy-start.2 = (bf16[128,768]{1,0:T(8,128)(2,1)}, bf16[128,768]{1,0:T(8,128)(2,1)S(1)}, u32[]{:S(2)}) copy-start(bf16[128,768]{1,0:T(8,128)(2,1)S(1)} %convert_element_type.51.refs_0_.refs_10_) | copy-start | bytes 589828
  7.8 15.8 %collective-permute-start.5 = (bf16[128,768]{1,0:T(8,128)(2,1)S(1)}, bf16[128,768]{1,0:T(8,128)(2,1)S(1)}, u32[]{:S(2)}, u32[]{:S(2)}) collective-permute-start(bf16[128,768]{1,0:T(8,128)(2,1)S(1)} %convert_element_type.51.refs_0_.refs_10_), channel_id=1, source_target_pairs={{0,6},{1,7},{2,4},{3,5},{4,2},{5,3},{6,0},{7,1},{8,14},{9,15},{10,... | collective-permute-start | bytes 589832 | tf_op jit(solution)/shard_map/ppermute | solution.py:16
  10.3 13.8 %collective-permute-start.3 = (bf16[128,768]{1,0:T(8,128)(2,1)S(1)}, bf16[128,768]{1,0:T(8,128)(2,1)S(1)}, u32[]{:S(2)}, u32[]{:S(2)}) collective-permute-start(bf16[128,768]{1,0:T(8,128)(2,1)S(1)} %convert_element_type.51.refs_0_.refs_10_), channel_id=1, source_target_pairs={{0,4},{1,5},{2,6},{3,7},{4,0},{5,1},{6,2},{7,3},{8,12},{9,13},{10,... | collective-permute-start | bytes 589832 | tf_op jit(solution)/shard_map/ppermute | solution.py:16
  10.8 13.4 %collective-permute-start.1 = (bf16[128,768]{1,0:T(8,128)(2,1)S(1)}, bf16[128,768]{1,0:T(8,128)(2,1)S(1)}, u32[]{:S(2)}, u32[]{:S(2)}) collective-permute-start(bf16[128,768]{1,0:T(8,128)(2,1)S(1)} %convert_element_type.51.refs_0_.refs_10_), channel_id=1, source_target_pairs={{0,2},{1,3},{2,0},{3,1},{4,6},{5,7},{6,4},{7,5},{8,10},{9,11},{10,... | collective-permute-start | bytes 589832 | tf_op jit(solution)/shard_map/ppermute | solution.py:16
  12.6 33.6 %copy-start.7 = (bf16[128,768]{1,0:T(8,128)(2,1)}, bf16[128,768]{1,0:T(8,128)(2,1)S(1)}, u32[]{:S(2)}) copy-start(bf16[128,768]{1,0:T(8,128)(2,1)S(1)} %collective-permute-done.9.refs_11_.refs_5_) | copy-start | bytes 589828
  12.6 33.5 %collective-permute-start.7 = (bf16[128,768]{1,0:T(8,128)(2,1)S(1)}, bf16[128,768]{1,0:T(8,128)(2,1)S(1)}, u32[]{:S(2)}, u32[]{:S(2)}) collective-permute-start(bf16[128,768]{1,0:T(8,128)(2,1)S(1)} %convert_element_type.52.refs_8_.refs_2_), channel_id=1, source_target_pairs={{0,8},{8,0},{16,24},{24,16},{1,9},{9,1},{17,25},{25,17},{2,10},{10... | collective-permute-start | bytes 589832 | tf_op jit(solution)/shard_map/ppermute | solution.py:16
  23.6 22.5 %collective-permute-start = (bf16[128,768]{1,0:T(8,128)(2,1)S(1)}, bf16[128,768]{1,0:T(8,128)(2,1)S(1)}, u32[]{:S(2)}, u32[]{:S(2)}) collective-permute-start(bf16[128,768]{1,0:T(8,128)(2,1)S(1)} %convert_element_type.51.refs_0_.refs_10_), channel_id=1, source_target_pairs={{0,1},{1,0},{2,3},{3,2},{4,5},{5,4},{6,7},{7,6},{8,9},{9,8},{10,11... | collective-permute-start | bytes 589832 | tf_op jit(solution)/shard_map/ppermute | solution.py:16
  23.6 22.5 %collective-permute-start.6 = (bf16[128,768]{1,0:T(8,128)(2,1)S(1)}, bf16[128,768]{1,0:T(8,128)(2,1)S(1)}, u32[]{:S(2)}, u32[]{:S(2)}) collective-permute-start(bf16[128,768]{1,0:T(8,128)(2,1)S(1)} %collective-permute-done.5.refs_6_.refs_16_), channel_id=1, source_target_pairs={{0,1},{1,0},{2,3},{3,2},{4,5},{5,4},{6,7},{7,6},{8,9},{9,8},{10,11... | collective-permute-start | bytes 589832 | tf_op jit(solution)/shard_map/ppermute | solution.py:16
  24.1 22.0 %collective-permute-start.4 = (bf16[128,768]{1,0:T(8,128)(2,1)S(1)}, bf16[128,768]{1,0:T(8,128)(2,1)S(1)}, u32[]{:S(2)}, u32[]{:S(2)}) collective-permute-start(bf16[128,768]{1,0:T(8,128)(2,1)S(1)} %collective-permute-done.3.refs_4_.refs_14_), channel_id=1, source_target_pairs={{0,1},{1,0},{2,3},{3,2},{4,5},{5,4},{6,7},{7,6},{8,9},{9,8},{10,11... | collective-permute-start | bytes 589832 | tf_op jit(solution)/shard_map/ppermute | solution.py:16
  24.2 22.0 %collective-permute-start.2 = (bf16[128,768]{1,0:T(8,128)(2,1)S(1)}, bf16[128,768]{1,0:T(8,128)(2,1)S(1)}, u32[]{:S(2)}, u32[]{:S(2)}) collective-permute-start(bf16[128,768]{1,0:T(8,128)(2,1)S(1)} %collective-permute-done.1.refs_2_.refs_12_), channel_id=1, source_target_pairs={{0,1},{1,0},{2,3},{3,2},{4,5},{5,4},{6,7},{7,6},{8,9},{9,8},{10,11... | collective-permute-start | bytes 589832 | tf_op jit(solution)/shard_map/ppermute | solution.py:16
  54.4 2.8 %collective-permute-start.10 = (f32[8,1024]{1,0:T(8,128)}, f32[8,1024]{1,0:T(8,128)S(1)}, u32[]{:S(2)}, u32[]{:S(2)}) collective-permute-start(f32[8,1024]{1,0:T(8,128)} %get-tuple-element.16.own_ref), channel_id=1, source_target_pairs={{0,1},{1,0},{2,3},{3,2},{4,5},{5,4},{6,7},{7,6},{8,9},{9,8},{10,11... | collective-permute-start | bytes 98312 | tf_op jit(solution)/shard_map/ppermute | solution.py:16
  54.7 8.0 %collective-permute-start.16 = (f32[8,512]{1,0:T(8,128)}, f32[8,512]{1,0:T(8,128)S(1)}, u32[]{:S(2)}, u32[]{:S(2)}) collective-permute-start(f32[8,512]{1,0:T(8,128)} %get-tuple-element.17.refs_6_), channel_id=1, source_target_pairs={{0,24},{8,16},{16,8},{24,0},{1,25},{9,17},{17,9},{25,1},{2,26},{10... | collective-permute-start | bytes 49160 | tf_op jit(solution)/shard_map/ppermute | solution.py:16
  59.2 8.3 %collective-permute-start.13 = (f32[8,1024]{1,0:T(8,128)}, f32[8,1024]{1,0:T(8,128)S(1)}, u32[]{:S(2)}, u32[]{:S(2)}) collective-permute-start(f32[8,1024]{1,0:T(8,128)} %shard_map.69.refs_2_), channel_id=1, source_target_pairs={{0,6},{1,7},{2,4},{3,5},{4,2},{5,3},{6,0},{7,1},{8,14},{9,15},{10,... | collective-permute-start | bytes 98312 | tf_op jit(solution)/shard_map/ppermute | solution.py:16
  60.7 6.9 %collective-permute-start.12 = (f32[8,1024]{1,0:T(8,128)}, f32[8,1024]{1,0:T(8,128)S(1)}, u32[]{:S(2)}, u32[]{:S(2)}) collective-permute-start(f32[8,1024]{1,0:T(8,128)} %shard_map.69.refs_2_), channel_id=1, source_target_pairs={{0,4},{1,5},{2,6},{3,7},{4,0},{5,1},{6,2},{7,3},{8,12},{9,13},{10,... | collective-permute-start | bytes 98312 | tf_op jit(solution)/shard_map/ppermute | solution.py:16
  62.1 5.5 %collective-permute-start.11 = (f32[8,1024]{1,0:T(8,128)}, f32[8,1024]{1,0:T(8,128)S(1)}, u32[]{:S(2)}, u32[]{:S(2)}) collective-permute-start(f32[8,1024]{1,0:T(8,128)} %shard_map.69.refs_2_), channel_id=1, source_target_pairs={{0,2},{1,3},{2,0},{3,1},{4,6},{5,7},{6,4},{7,5},{8,10},{9,11},{10,... | collective-permute-start | bytes 98312 | tf_op jit(solution)/shard_map/ppermute | solution.py:16
  62.7 4.8 %collective-permute-start.15 = (f32[8,512]{1,0:T(8,128)}, f32[8,512]{1,0:T(8,128)S(1)}, u32[]{:S(2)}, u32[]{:S(2)}) collective-permute-start(f32[8,512]{1,0:T(8,128)} %get-tuple-element.17.refs_6_), channel_id=1, source_target_pairs={{0,16},{8,24},{16,0},{24,8},{1,17},{9,25},{17,1},{25,9},{2,18},{10... | collective-permute-start | bytes 49160 | tf_op jit(solution)/shard_map/ppermute | solution.py:16
  62.7 4.8 %collective-permute-start.14 = (f32[8,512]{1,0:T(8,128)}, f32[8,512]{1,0:T(8,128)S(1)}, u32[]{:S(2)}, u32[]{:S(2)}) collective-permute-start(f32[8,512]{1,0:T(8,128)} %get-tuple-element.17.refs_6_), channel_id=1, source_target_pairs={{0,8},{8,0},{16,24},{24,16},{1,9},{9,1},{17,25},{25,17},{2,10},{10... | collective-permute-start | bytes 49160 | tf_op jit(solution)/shard_map/ppermute | solution.py:16
  81.0 29.0 %collective-permute-start.22 = (f32[4,128,768]{2,1,0:T(8,128)}, f32[4,128,768]{2,1,0:T(8,128)S(1)}, u32[]{:S(2)}, u32[]{:S(2)}) collective-permute-start(f32[4,128,768]{2,1,0:T(8,128)} %get-tuple-element.22), channel_id=1, source_target_pairs={{0,1},{1,0},{2,3},{3,2},{4,5},{5,4},{6,7},{7,6},{8,9},{9,8},{10,11... | collective-permute-start | bytes 4718600 | tf_op jit(solution)/shard_map/ppermute | solution.py:16
  82.4 8.4 %collective-permute-start.17 = (f32[]{:T(128)}, f32[]{:T(128)}, u32[]{:S(2)}, u32[]{:S(2)}) collective-permute-start(f32[]{:T(128)} %bitcast.4), channel_id=1, source_target_pairs={{0,1},{1,0},{2,3},{3,2},{4,5},{5,4},{6,7},{7,6},{8,9},{9,8},{10,11... | collective-permute-start | bytes 20 | tf_op jit(solution)/shard_map/ppermute | solution.py:16
  85.0 29.0 %collective-permute-start.28 = (f16[128,768]{1,0:T(8,128)(2,1)}, f16[128,768]{1,0:T(8,128)(2,1)S(1)}, u32[]{:S(2)}, u32[]{:S(2)}) collective-permute-start(f16[128,768]{1,0:T(8,128)(2,1)} %convert_element_type.66), channel_id=1, source_target_pairs={{0,24},{8,16},{16,8},{24,0},{1,25},{9,17},{17,9},{25,1},{2,26},{10... | collective-permute-start | bytes 589832 | tf_op jit(solution)/shard_map/ppermute | solution.py:16
  86.5 28.1 %collective-permute-start.27 = (f16[128,768]{1,0:T(8,128)(2,1)}, f16[128,768]{1,0:T(8,128)(2,1)S(1)}, u32[]{:S(2)}, u32[]{:S(2)}) collective-permute-start(f16[128,768]{1,0:T(8,128)(2,1)} %convert_element_type.64), channel_id=1, source_target_pairs={{0,16},{8,24},{16,0},{24,8},{1,17},{9,25},{17,1},{25,9},{2,18},{10... | collective-permute-start | bytes 589832 | tf_op jit(solution)/shard_map/ppermute | solution.py:16
  87.5 27.1 %collective-permute-start.26 = (f16[128,768]{1,0:T(8,128)(2,1)}, f16[128,768]{1,0:T(8,128)(2,1)}, u32[]{:S(2)}, u32[]{:S(2)}) collective-permute-start(f16[128,768]{1,0:T(8,128)(2,1)} %convert_element_type.62), channel_id=1, source_target_pairs={{0,8},{8,0},{16,24},{24,16},{1,9},{9,1},{17,25},{25,17},{2,10},{10... | collective-permute-start | bytes 589832 | tf_op jit(solution)/shard_map/ppermute | solution.py:16
  92.0 3.7 %collective-permute-start.18 = (f32[]{:T(128)}, f32[]{:T(128)}, u32[]{:S(2)}, u32[]{:S(2)}) collective-permute-start(f32[]{:T(128)} %add.36), channel_id=1, source_target_pairs={{0,2},{1,3},{2,0},{3,1},{4,6},{5,7},{6,4},{7,5},{8,10},{9,11},{10,... | collective-permute-start | bytes 20 | tf_op jit(solution)/shard_map/ppermute | solution.py:16
  96.2 3.7 %collective-permute-start.19 = (f32[]{:T(128)}, f32[]{:T(128)}, u32[]{:S(2)}, u32[]{:S(2)}) collective-permute-start(f32[]{:T(128)} %add.37), channel_id=1, source_target_pairs={{0,4},{1,5},{2,6},{3,7},{4,0},{5,1},{6,2},{7,3},{8,12},{9,13},{10,... | collective-permute-start | bytes 20 | tf_op jit(solution)/shard_map/ppermute | solution.py:16
  100.5 3.8 %collective-permute-start.20 = (f32[]{:T(128)}, f32[]{:T(128)}, u32[]{:S(2)}, u32[]{:S(2)}) collective-permute-start(f32[]{:T(128)} %add.38), channel_id=1, source_target_pairs={{0,8},{8,0},{16,24},{24,16},{1,9},{9,1},{17,25},{25,17},{2,10},{10... | collective-permute-start | bytes 20 | tf_op jit(solution)/shard_map/ppermute | solution.py:16
  104.8 4.6 %collective-permute-start.21 = (f32[]{:T(128)}, f32[]{:T(128)}, u32[]{:S(2)}, u32[]{:S(2)}) collective-permute-start(f32[]{:T(128)} %add.39), channel_id=1, source_target_pairs={{0,16},{8,24},{16,0},{24,8},{1,17},{9,25},{17,1},{25,9},{2,18},{10... | collective-permute-start | bytes 20 | tf_op jit(solution)/shard_map/ppermute | solution.py:16
  111.0 5.7 %collective-permute-start.23 = (f16[128,768]{1,0:T(8,128)(2,1)S(1)}, f16[128,768]{1,0:T(8,128)(2,1)S(1)}, u32[]{:S(2)}, u32[]{:S(2)}) collective-permute-start(f16[128,768]{1,0:T(8,128)(2,1)S(1)} %get-tuple-element.27), channel_id=1, source_target_pairs={{0,2},{1,3},{2,0},{3,1},{4,6},{5,7},{6,4},{7,5},{8,10},{9,11},{10,... | collective-permute-start | bytes 589832 | tf_op jit(solution)/shard_map/ppermute | solution.py:16
  112.6 7.3 %collective-permute-start.25 = (f16[128,768]{1,0:T(8,128)(2,1)S(1)}, f16[128,768]{1,0:T(8,128)(2,1)S(1)}, u32[]{:S(2)}, u32[]{:S(2)}) collective-permute-start(f16[128,768]{1,0:T(8,128)(2,1)S(1)} %get-tuple-element.28), channel_id=1, source_target_pairs={{0,6},{1,7},{2,4},{3,5},{4,2},{5,3},{6,0},{7,1},{8,14},{9,15},{10,... | collective-permute-start | bytes 589832 | tf_op jit(solution)/shard_map/ppermute | solution.py:16
  114.0 7.8 %collective-permute-start.24 = (f16[128,768]{1,0:T(8,128)(2,1)S(1)}, f16[128,768]{1,0:T(8,128)(2,1)S(1)}, u32[]{:S(2)}, u32[]{:S(2)}) collective-permute-start(f16[128,768]{1,0:T(8,128)(2,1)S(1)} %get-tuple-element.29), channel_id=1, source_target_pairs={{0,4},{1,5},{2,6},{3,7},{4,0},{5,1},{6,2},{7,3},{8,12},{9,13},{10,... | collective-permute-start | bytes 589832 | tf_op jit(solution)/shard_map/ppermute | solution.py:16
  (21 other events, 160.8 us)

commit v2 on v1

v2 whole, which is shorter than its diff:
```python
import math

import jax
import jax.numpy as jnp
from jax import lax
from jax.experimental import pallas as pl
from jax.experimental.pallas import tpu as pltpu
from jax.sharding import PartitionSpec as P

F32 = jnp.float32
BF16 = jnp.bfloat16
VMEM_SPARE = 4 * 1024 * 1024
CODE_SPAN = 2.0**20
CODE_STEPS = 32000.0 / math.asinh(CODE_SPAN)
LOSS_UNIT = 1.0 / 4096.0
DIGIT = 2.0**15


def exchange(value, axis, turn):
    size = lax.axis_size(axis)
    return lax.ppermute(value, axis, [(i, i ^ turn) for i in range(size)])


def call(kernel, out_shape, scratch_shapes, *operands, spare=()):
    size = sum(x.size * x.dtype.itemsize for x in (*operands, *jax.tree.leaves(out_shape)))
    held = [x for x in scratch_shapes if hasattr(x, "memory_space") and x.memory_space == pltpu.VMEM]
    size += sum(math.prod(x.shape) * jnp.dtype(x.dtype).itemsize for x in held)
    spaces = [pl.BlockSpec(memory_space=pltpu.VMEM)] * len(operands)
    spaces += [pl.BlockSpec(memory_space=pl.ANY)] * len(spare)
    return pl.pallas_call(
        kernel,
        out_shape=out_shape,
        in_specs=spaces,
        out_specs=jax.tree.map(lambda _: pl.BlockSpec(memory_space=pltpu.VMEM), out_shape),
        scratch_shapes=scratch_shapes,
        compiler_params=pltpu.CompilerParams(vmem_limit_bytes=2 * size + VMEM_SPARE),
        cost_estimate=pl.CostEstimate(flops=1, bytes_accessed=1, transcendentals=0),
    )(*operands, *spare)


def first_messages(queries, passages, hard_ids, list_lengths):
    rows, width = queries.shape
    listed = hard_ids.shape[1]
    groups = listed // 16
    operands = (passages, hard_ids.T, list_lengths.reshape(1, rows), queries)

    def kernel(*refs):
        here, (p_out, q_out), refs = refs[:4], refs[4:6], refs[6:]
        p_ref, ids_ref, len_ref, q_ref = refs[:4]
        copies = [
            pltpu.make_async_copy(src, dst, refs[4].at[n])
            for n, (src, dst) in enumerate(zip(here, refs[:4]))
        ]
        for copy in copies:
            copy.start()
        for copy in copies:
            copy.wait()
        p_out[...] = p_ref[...].astype(BF16)
        q_out[:rows, :] = q_ref[...].astype(BF16)
        ids = ids_ref[...].astype(F32)
        live = lax.broadcasted_iota(jnp.int32, (listed, rows), 0) < len_ref[...]
        block = jnp.floor((ids + 0.5) * (1.0 / rows))
        inside = (ids - block * rows).astype(BF16)
        block = jnp.where(live, block, -1.0).astype(BF16)
        q_out[rows:, :] = jnp.zeros((16, width), BF16)
        for g in range(groups):
            part = slice(g * 16, (g + 1) * 16)
            q_out[rows:, g * rows : (g + 1) * rows] = block[part, :]
            q_out[rows:, (groups + g) * rows : (groups + g + 1) * rows] = inside[part, :]

    return call(
        kernel,
        (
            jax.ShapeDtypeStruct((rows, width), BF16),
            jax.ShapeDtypeStruct((rows + 16, width), BF16),
        ),
        [pltpu.VMEM(x.shape, x.dtype) for x in operands] + [pltpu.SemaphoreType.DMA((4,))],
        spare=operands,
    )


def tally(tail, rows, listed, col_slots, fields):
    groups = listed // 16
    down, across = lax.axis_index("pb"), lax.axis_index("pa")
    row_axis_size = lax.axis_size("pa")
    digits = [tail[:, g * rows : (g + 1) * rows].astype(F32) for g in range(2 * groups)]
    block = jnp.concatenate(digits[:groups], axis=0).astype(jnp.int32)
    inside = jnp.concatenate(digits[groups:], axis=0).astype(jnp.int32)
    steps = lax.broadcasted_iota(jnp.int32, (rows, rows), 0)
    for g in range(0, col_slots, 4):
        unit = jnp.zeros((listed, rows), jnp.int32)
        for j in range(g, min(g + 4, col_slots)):
            mine = (down ^ j) * row_axis_size + across
            unit = jnp.where(block == mine, 1 << (8 * (j - g)), unit)
        total = jnp.zeros((rows, rows), jnp.int32)
        for h in range(listed):
            total = total + jnp.where(inside[h : h + 1, :] == steps, unit[h : h + 1, :], 0)
        fields[g // 4] = total


def count_at(ref, m, j):
    return ((ref[m, j // 4] >> (8 * (j % 4))) & 255).astype(F32)


def gather_even(messages, col_slots, listed, after):
    slots = len(messages)
    tall, width = messages[0].shape
    rows = tall - 16

    def kernel(*refs):
        m_refs, (out_ref, count_ref) = refs[:slots], refs[-2:]
        for m in range(slots):
            out_ref[m] = m_refs[m][...]
            tally(m_refs[m][rows:, :], rows, listed, col_slots, count_ref.at[m])

    return call(
        kernel,
        (
            jax.ShapeDtypeStruct((slots, tall, width), BF16),
            jax.ShapeDtypeStruct((slots, -(-col_slots // 4), rows, rows), jnp.int32),
        ),
        [],
        *messages,
        spare=after,
    )


def count_odd(messages, col_slots, listed):
    slots, tall, width = messages.shape
    rows = tall - 16

    def kernel(m_ref, count_ref):
        for m in range(slots):
            tally(m_ref[m, rows:, :], rows, listed, col_slots, count_ref.at[m])

    return call(
        kernel,
        jax.ShapeDtypeStruct((slots, -(-col_slots // 4), rows, rows), jnp.int32),
        [],
        messages,
    )


def score_sweep(even, odd, passage_slots, even_counts, odd_counts):
    row_slots, col_slots = 2 * even.shape[0], len(passage_slots)
    rows, width = passage_slots[0].shape
    tall, wide = row_slots * rows, col_slots * rows

    def most_of(part):
        most = jnp.max(jnp.abs(part.astype(F32)), axis=0, keepdims=True)
        return jnp.max(most, axis=1, keepdims=True)

    def kernel(*refs):
        q_refs, refs = refs[:2], refs[2:]
        p_refs, refs = refs[:col_slots], refs[col_slots:]
        even_ref, odd_ref, s_ref, row_ref, col_ref, p_all, top_acc = refs
        row_ref[...] = jnp.zeros_like(row_ref)
        col_ref[...] = jnp.zeros_like(col_ref)
        passage_most = jnp.zeros((1, 1), F32)
        for j in range(col_slots):
            part = p_refs[j][...]
            p_all[j * rows : (j + 1) * rows, :] = part
            passage_most = jnp.maximum(passage_most, most_of(part))
        query_most = jnp.zeros((1, 1), F32)
        for m in range(row_slots // 2):
            both = jnp.concatenate([q[m, :rows, :] for q in q_refs], axis=0)
            query_most = jnp.maximum(query_most, most_of(both))
            spot = slice(2 * m * rows, 2 * (m + 1) * rows)
            s_ref[:, spot] = lax.dot_general(
                p_all[...], both, (((1,), (1,)), ((), ())), preferred_element_type=F32
            )
        row_ref[2:3, :] = jnp.broadcast_to(passage_most, (1, tall))
        unit = lax.broadcasted_iota(jnp.int32, (rows, rows), 0) == lax.broadcasted_iota(
            jnp.int32, (rows, rows), 1
        )
        pairs = jnp.sum(jnp.where(unit, s_ref[:rows, :rows], 0.0), axis=0, keepdims=True)
        row_ref[3:4, :] = jnp.broadcast_to(jnp.sum(pairs, axis=1, keepdims=True), (1, tall))
        col_ref[2:3, :] = jnp.broadcast_to(query_most, (1, wide))
        for k in range(row_slots):
            spot = slice(k * rows, (k + 1) * rows)
            c_ref = (even_ref, odd_ref)[k % 2]
            top = jnp.full((1, rows), -jnp.inf, F32)
            for j in range(col_slots):
                here = slice(j * rows, (j + 1) * rows)
                part = s_ref[here, spot]
                top = jnp.maximum(top, jnp.max(part, axis=0, keepdims=True))
                if k == 0:
                    top_acc[here, :] = part
                else:
                    top_acc[here, :] = jnp.maximum(top_acc[here, :], part)
            total = jnp.zeros((1, rows), F32)
            for j in range(col_slots):
                here = slice(j * rows, (j + 1) * rows)
                times = 1.0 + count_at(c_ref, k // 2, j)
                total = total + jnp.sum(
                    jnp.exp(s_ref[here, spot] - top) * times, axis=0, keepdims=True
                )
            row_ref[0:1, spot] = top
            row_ref[1:2, spot] = total
        for j in range(col_slots):
            here = slice(j * rows, (j + 1) * rows)
            acc = top_acc[here, :]
            col_ref[0:1, here] = jnp.max(acc.T, axis=0, keepdims=True)
            top = jnp.max(acc, axis=1, keepdims=True)
            total = jnp.zeros((rows, rows), F32)
            for k in range(row_slots):
                total = total + jnp.exp(s_ref[here, k * rows : (k + 1) * rows] - top)
            col_ref[1:2, here] = jnp.sum(total.T, axis=0, keepdims=True)

    return call(
        kernel,
        (
            jax.ShapeDtypeStruct((wide, tall), F32),
            jax.ShapeDtypeStruct((8, tall), F32),
            jax.ShapeDtypeStruct((8, wide), F32),
        ),
        [pltpu.VMEM((wide, width), BF16), pltpu.VMEM((wide, rows), F32)],
        even,
        odd,
        *passage_slots,
        even_counts,
        odd_counts,
    )


def turned(value, turn, rows):
    slots = value.shape[1] // rows
    return jnp.concatenate(
        [value[:, (k ^ turn) * rows : ((k ^ turn) + 1) * rows] for k in range(slots)], axis=1
    )


def tree(combine, values):
    while len(values) > 1:
        values = [combine(a, b) for a, b in zip(values[::2], values[1::2])]
    return values[0]


def join(own, other, turn, rows):
    def kernel(own_ref, other_ref, out_ref):
        one, two = own_ref[...], turned(other_ref[...], turn, rows)
        top = jnp.maximum(one[0:1], two[0:1])
        out_ref[0:1, :] = top
        out_ref[1:2, :] = one[1:2] * jnp.exp(one[0:1] - top) + two[1:2] * jnp.exp(two[0:1] - top)
        out_ref[2:3, :] = jnp.maximum(one[2:3], two[2:3])
        out_ref[3:, :] = one[3:] + two[3:]

    return call(kernel, jax.ShapeDtypeStruct(own.shape, F32), [], own, other)


def coded(value, inverse):
    size = jnp.abs(value) * (inverse * CODE_SPAN)
    steps = jnp.log(size + jnp.sqrt(size * size + 1.0)) * CODE_STEPS
    return jnp.round(jnp.where(value < 0.0, -steps, steps)).astype(jnp.int32).astype(jnp.int16)


def decoded(code, bound):
    grown = jnp.exp(code.astype(F32) * (1.0 / CODE_STEPS))
    return (grown - 1.0 / grown) * (bound * (0.5 / CODE_SPAN))


def write_term(ref, value):
    rows = ref.shape[0] - 16
    ref[rows:, :] = jnp.zeros((16, ref.shape[1]), jnp.int16)
    left = value[:, :1] * LOSS_UNIT
    for n in range(3):
        digit = jnp.round(left)
        left = (left - digit) * DIGIT
        ref[rows:, n * 128 : (n + 1) * 128] = (
            jnp.broadcast_to(digit, (16, 128)).astype(jnp.int32).astype(jnp.int16)
        )


def read_term(ref):
    rows = ref.shape[0] - 16
    one, two, three = [
        ref[rows:, n * 128 : (n + 1) * 128].astype(F32)[:1, :1] for n in range(3)
    ]
    return (one + (two + three * (1.0 / DIGIT)) * (1.0 / DIGIT)) * (1.0 / LOSS_UNIT)


def weight_sweep(scores, even_counts, odd_counts, row_stats, col_stats, even, odd):
    rows = even_counts.shape[2]
    width = even.shape[2]
    wide, tall = scores.shape
    row_slots, col_slots = tall // rows, wide // rows

    def kernel(*refs):
        (s_ref, even_ref, odd_ref), refs = refs[:3], refs[3:]
        (row_ref, col_ref), refs = refs[:2], refs[2:]
        q_refs, refs = refs[:2], refs[2:]
        (hi_ref, lo_ref), refs = refs[:2], refs[2:]
        out_refs, refs = refs[:col_slots], refs[col_slots:]
        info_ref, q_all, row_level, col_level = refs
        for k in range(row_slots):
            q_all[k * rows : (k + 1) * rows, :] = q_refs[k % 2][k // 2, :rows, :]
        row_level[...] = row_ref[0:1, :] + jnp.log(row_ref[1:2, :])
        columns = col_ref[0:1, :] + jnp.log(col_ref[1:2, :])
        query_most = col_ref[2:3, :]
        passage_most, pairs = row_ref[2:3, :], row_ref[3:4, :]
        for j in range(col_slots):
            here = slice(j * rows, (j + 1) * rows)
            col_level[here, :] = jnp.broadcast_to(columns[:, here], (rows, rows)).T
        unit = (
            lax.broadcasted_iota(jnp.int32, (rows, rows), 0)
            == lax.broadcasted_iota(jnp.int32, (rows, rows), 1)
        ).astype(F32)
        query_bound = jnp.maximum(query_most[:, :1] * (tall * 1.02 + 8.0), 1e-30)
        passage_bound = jnp.maximum(passage_most[:, :1] * (2 * wide * 1.02 + 8.0), 1e-30)
        inverse = 1.0 / query_bound
        for j in reversed(range(col_slots)):
            here = slice(j * rows, (j + 1) * rows)
            for k in range(row_slots):
                spot = slice(k * rows, (k + 1) * rows)
                c_ref = (even_ref, odd_ref)[k % 2]
                part = s_ref[here, spot]
                by_row = jnp.exp(part - row_level[:, spot])
                by_col = jnp.exp(part - col_level[here, :])
                pair = (by_row + by_col).astype(BF16).astype(F32)
                hard = by_row.astype(BF16).astype(F32)
                weight = pair + hard * count_at(c_ref, k // 2, j)
                if j == 0 and k == 0:
                    weight = weight - 2.0 * unit
                high = weight.astype(BF16)
                hi_ref[here, spot] = high
                lo_ref[here, spot] = (weight - high.astype(F32)).astype(BF16)
            part = jnp.dot(hi_ref[here, :], q_all[...], preferred_element_type=F32)
            part = part + jnp.dot(lo_ref[here, :], q_all[...], preferred_element_type=F32)
            if j % 2 == 0:
                out_refs[j][...] = part
            else:
                out_refs[j][:rows, :] = coded(part, inverse)

        def summed(level):
            parts = [
                jnp.sum(level[:, g * rows : (g + 1) * rows], axis=1, keepdims=True)
                for g in range(level.shape[1] // rows)
            ]
            return tree(jnp.add, parts)

        row_term = summed(row_level[...]) - 2.0 * pairs[:, :1]
        info_ref[...] = jnp.zeros_like(info_ref)
        for n, value in enumerate((row_term, summed(columns), query_bound, passage_bound)):
            info_ref[n : n + 1, :] = jnp.broadcast_to(value, (1, rows))
        for j in range(1, col_slots, 2):
            write_term(out_refs[j], row_term)

    return call(
        kernel,
        (
            jax.ShapeDtypeStruct((wide, tall), BF16),
            jax.ShapeDtypeStruct((wide, tall), BF16),
            *[
                jax.ShapeDtypeStruct((rows, width), F32),
                jax.ShapeDtypeStruct((rows + 16, width), jnp.int16),
            ]
            * (col_slots // 2),
            jax.ShapeDtypeStruct((8, rows), F32),
        ),
        [
            pltpu.VMEM((tall, width), BF16),
            pltpu.VMEM((1, tall), F32),
            pltpu.VMEM((wide, rows), F32),
        ],
        scores,
        even_counts,
        odd_counts,
        row_stats,
        col_stats,
        even,
        odd,
    )


def query_sweep(high, low, passage_slots, info):
    rows, width = passage_slots[0].shape
    wide, tall = high.shape
    row_slots, col_slots = tall // rows, wide // rows
    half = row_slots // 2 * rows

    def kernel(*refs):
        (hi_ref, lo_ref), refs = refs[:2], refs[2:]
        p_refs, refs = refs[:col_slots], refs[col_slots:]
        info_ref, even_ref, odd_ref, p_all = refs
        for j in range(col_slots):
            p_all[j * rows : (j + 1) * rows, :] = p_refs[j][...]
        for m in range(row_slots // 2):
            spot = slice(m * 2 * rows, (m + 1) * 2 * rows)
            dims = (((0,), (0,)), ((), ()))
            part = lax.dot_general(
                hi_ref[:, spot], p_all[...], dims, preferred_element_type=F32
            ) + lax.dot_general(lo_ref[:, spot], p_all[...], dims, preferred_element_type=F32)
            even_ref[m * rows : (m + 1) * rows, :] = part[:rows]
            odd_ref[m * rows : (m + 1) * rows, :] = part[rows:]
        odd_ref[half:, :] = jnp.zeros((8, width), F32)
        odd_ref[half : half + 8, :rows] = info_ref[...]

    return call(
        kernel,
        (
            jax.ShapeDtypeStruct((half, width), F32),
            jax.ShapeDtypeStruct((half + 8, width), F32),
        ),
        [pltpu.VMEM((wide, width), BF16)],
        high,
        low,
        *passage_slots,
        info,
    )


def middle(even, other, info, halves, relayed):
    rows = info.shape[1]
    half, width = even.shape
    slots = half // rows
    passed = len(relayed)

    def kernel(even_ref, other_ref, info_ref, *refs):
        half_refs, relay_refs, refs = refs[:passed], refs[passed : 2 * passed], refs[2 * passed :]
        own_ref, term_ref, refs = refs[0], refs[1], refs[2:]
        query_bound = info_ref[2:3, :1]
        inverse = 1.0 / query_bound
        row_term = info_ref[0:1, :1]
        if passed:
            for half_ref, relay_ref, out_ref in zip(half_refs, relay_refs, refs):
                total = half_ref[...] + decoded(relay_ref[:rows, :], query_bound)
                out_ref[:rows, :] = coded(total, inverse)
            row_term = row_term + read_term(relay_refs[0])
            for out_ref in refs[:passed]:
                write_term(out_ref, row_term)
        inverse = 1.0 / info_ref[3:4, :1]
        own_ref[...] = even_ref[:rows, :] + other_ref[:rows, :]
        col_term = info_ref[1:2, :1] + other_ref[half + 1 : half + 2, :1]
        for m in range(1, slots):
            here = slice(m * rows, (m + 1) * rows)
            out_ref = refs[passed + m - 1]
            out_ref[:rows, :] = coded(even_ref[here, :] + other_ref[here, :], inverse)
            write_term(out_ref, col_term)
        term_ref[...] = jnp.zeros_like(term_ref)
        term_ref[0:1, :] = jnp.broadcast_to(row_term, (1, rows))
        term_ref[1:2, :] = jnp.broadcast_to(col_term, (1, rows))

    return call(
        kernel,
        (
            jax.ShapeDtypeStruct((rows, width), F32),
            jax.ShapeDtypeStruct((8, rows), F32),
            *[jax.ShapeDtypeStruct((rows + 16, width), jnp.int16)] * (passed + slots - 1),
        ),
        [],
        even,
        other,
        info,
        *halves,
        *relayed,
    )


def finish(own, arrived, info, row):
    rows, width = own.shape

    def kernel(own_ref, info_ref, *refs):
        bound = info_ref[row : row + 1, :1]
        total = own_ref[...]
        for a in refs[:-1]:
            total = total + decoded(a[:rows, :], bound)
        refs[-1][...] = 0.5 * total

    return call(kernel, jax.ShapeDtypeStruct((rows, width), F32), [], own, info, *arrived)


def mean_loss(term, across, along, devices):
    rows = term.shape[1]

    def kernel(term_ref, *refs):
        sides = [term_ref[1:2, :1]] + [read_term(a) for a in refs[: len(across)]]
        lines = [term_ref[0:1, :1]] + [read_term(a) for a in refs[len(across) : -1]]
        loss = tree(jnp.add, sides) + tree(jnp.add, lines)
        refs[-1][...] = loss * (1.0 / (2.0 * rows * devices))

    return call(kernel, jax.ShapeDtypeStruct((1, 1), F32), [], term, *across, *along)


def per_device(queries, passages, hard_ids, list_lengths):
    rows, width = queries.shape
    listed = hard_ids.shape[1]
    across = lax.axis_size("pa")
    down = lax.axis_size("pb")
    passage_own, message = first_messages(queries, passages, hard_ids, list_lengths)
    far = [exchange(passage_own, "pb", j) for j in range(2, down, 2)]
    near = exchange(passage_own, "pb", 1)
    row_turns = list(range(0, across, 2))
    even = [message] + [exchange(message, "pa", k) for k in row_turns[1:]]
    even, even_counts = gather_even(even, down, listed, far + [near])
    passage_slots = [passage_own, near]
    for part in far:
        passage_slots += [part, exchange(part, "pb", 1)]
    odd = exchange(even, "pa", 1)
    odd_counts = count_odd(odd, down, listed)

    scores, row_stats, col_stats = score_sweep(
        even, odd, passage_slots, even_counts, odd_counts
    )
    turn = 1
    while turn < max(across, down):
        if turn < across:
            row_stats = join(row_stats, exchange(row_stats, "pa", turn), turn, rows)
        if turn < down:
            col_stats = join(col_stats, exchange(col_stats, "pb", turn), turn, rows)
        turn *= 2

    high, low, *blocks, info = weight_sweep(
        scores, even_counts, odd_counts, row_stats, col_stats, even, odd
    )
    even_sum, odd_sum = query_sweep(high, low, passage_slots, info)
    halves = blocks[2::2]
    relayed = [exchange(part, "pb", 1) for part in blocks[3::2]]
    query_sum, term, *sent = middle(
        even_sum, exchange(odd_sum, "pa", 1), info, halves, relayed
    )
    along = [
        exchange(part, "pb", j) for part, j in zip(sent, range(2, down, 2))
    ]
    side = [exchange(part, "pa", k) for part, k in zip(sent[len(along) :], row_turns[1:])]
    near = exchange(blocks[1], "pb", 1)
    grad_passages = finish(blocks[0], along + [near], info, 2)
    grad_queries = finish(query_sum, side, info, 3)
    loss = mean_loss(term, side, along, across * down)
    return (loss.reshape(()), grad_queries, grad_passages)


def solution(mesh):
    return jax.shard_map(
        per_device,
        mesh=mesh,
        in_specs=(
            P(("pb", "pa"), None),
            P(("pb", "pa"), None),
            P(("pb", "pa"), None),
            P(("pb", "pa")),
        ),
        out_specs=(P(), P(("pb", "pa"), None), P(("pb", "pa"), None)),
        check_vma=False,
    )
```

time: 124 us -> 76.2 us (0.61)
  starting transfers between devices: 44 us -> 21.8 us
  waiting for transfers between devices: 18.7 us -> 35.3 us
  Pallas kernels: 30.8 us -> 14.7 us
  blocking collectives: 10.2 us -> 0 us
  other arithmetic: 9.1 us -> 0 us
  between operations: 6.86 us -> 0.73 us
    ppermute x29 -> x19, starting transfers between devices: 44 us -> 21.8 us  [exchange(): return lax.ppermute(value, axis, [(i, i ^ turn) for i in range(size)])]
    ppermute x29 -> x19, waiting for transfers between devices: 18.7 us -> 35.3 us  [exchange(): return lax.ppermute(value, axis, [(i, i ^ turn) for i in range(size)])]
    pallas_call x5 -> x15, Pallas kernels: 30.8 us -> 14.7 us  [call(): pl.pallas_call(kernel, out_shape=out_shape, in_specs=spaces, out_specs=ja...]
    all_gather x1 -> x0, blocking collectives: 10.2 us -> none  [per_device(): keys = lax.all_gather(keys, 'pa')]
    convert_element_type x6 -> x0, other arithmetic: 4.95 us -> none  [the longest x3 2.09 us: per_device(): part.astype(jnp.float16)]
    add x3 -> x0, other arithmetic: 2.84 us -> none  [the longest x1 1.78 us: per_device(): 0.5 * passage_sum + sum((part.astype(F32) for part in arrived)) * back]
    slice x1 -> x0, local copies, waits for them, and re-layouts: 1.39 us -> none  [per_device(): query_scale = info[1, 0]]
    unnamed x48 -> x8, local copies, waits for them, and re-layouts: 2.7 us -> 3.36 us
  transfers between devices with their start and end apart: 29 -> 19, of which waited for: 10 -> 11; matrix products, arithmetic and copies ran while one was open for 7% -> 0% of each run, Pallas kernels for 9% -> 4%
where the time goes in v2:
time: 76.2 us; the launch traced here: 75.9 us
  waiting for transfers between devices  35.3 us (46%)
  starting transfers between devices  21.8 us (29%)
  Pallas kernels  14.7 us (19%)
  local copies, waits for them, and re-layouts  3.36 us (4%)
    ppermute x19, waiting for transfers between devices, exchange(): return lax.ppermute(value, axis, [(i, i ^ turn) for i in range(size)])  35.3 us
    ppermute x19, starting transfers between devices, exchange(): return lax.ppermute(value, axis, [(i, i ^ turn) for i in range(size)])  21.8 us
    pallas_call x15, Pallas kernels, call(): pl.pallas_call(kernel, out_shape=out_shape, in_specs=spaces, out_specs=ja...  14.7 us
    unnamed x8, local copies, waits for them, and re-layouts  3.36 us
  transfers between devices with their start and end apart: 19, of which 11 were waited for; matrix products, arithmetic and copies ran while one was open for 0% of the time, Pallas kernels for 4%

profile of v2, /device:TPU:0, one launch (start us, length us, event | category | flops | bytes accessed | tf_op | source)
XLA Modules:
  0.0 75.9 jit_solution(14972920140877567083)
XLA Ops:
  0.6 1.0 %copy-done = f32[128,768]{1,0:T(8,128)S(1)} copy-done((f32[128,768]{1,0:T(8,128)S(1)}, f32[128,768]{1,0:T(8,128)}, u32[]{:S(2)}) %copy-start) | copy-done | bytes 393240
  1.6 1.0 %copy-done.1 = f32[128,768]{1,0:T(8,128)S(1)} copy-done((f32[128,768]{1,0:T(8,128)S(1)}, f32[128,768]{1,0:T(8,128)}, u32[]{:S(2)}) %copy-start.1) | copy-done | bytes 393240
  2.6 0.7 copy-done.2
  4.5 4.0 %collective-permute-start.2 = (bf16[144,768]{1,0:T(8,128)(2,1)S(1)}, bf16[144,768]{1,0:T(8,128)(2,1)S(1)}, u32[]{:S(2)}, u32[]{:S(2)}) collective-permute-start(bf16[144,768]{1,0:T(8,128)(2,1)S(1)} %get-tuple-element.25.refs_0_), channel_id=1, source_target_pairs={{0,6},{1,7},{2,4},{3,5},{4,2},{5,3},{6,0},{7,1},{8,14},{9,15},{10,... | collective-permute-start | bytes 663560 | tf_op jit(solution)/shard_map/ppermute | solution.py:21
  9.1 2.0 %collective-permute-start.4 = (bf16[128,768]{1,0:T(8,128)(2,1)S(1)}, bf16[128,768]{1,0:T(8,128)(2,1)S(1)}, u32[]{:S(2)}, u32[]{:S(2)}) collective-permute-start(bf16[128,768]{1,0:T(8,128)(2,1)S(1)} %get-tuple-element.26.refs_2_), channel_id=1, source_target_pairs={{0,8},{8,0},{16,24},{24,16},{1,9},{9,1},{17,25},{25,17},{2,10},{10... | collective-permute-start | bytes 589832 | tf_op jit(solution)/shard_map/ppermute | solution.py:21
  11.1 2.6 %collective-permute-start.3 = (bf16[128,768]{1,0:T(8,128)(2,1)S(1)}, bf16[128,768]{1,0:T(8,128)(2,1)S(1)}, u32[]{:S(2)}, u32[]{:S(2)}) collective-permute-start(bf16[128,768]{1,0:T(8,128)(2,1)S(1)} %get-tuple-element.26.refs_2_), channel_id=1, source_target_pairs={{0,16},{8,24},{16,0},{24,8},{1,17},{9,25},{17,1},{25,9},{2,18},{10... | collective-permute-start | bytes 589832 | tf_op jit(solution)/shard_map/ppermute | solution.py:21
  13.7 5.3 %collective-permute-done.4.refs_5_.refs_3_ = bf16[128,768]{1,0:T(8,128)(2,1)S(1)} collective-permute-done((bf16[128,768]{1,0:T(8,128)(2,1)S(1)}, bf16[128,768]{1,0:T(8,128)(2,1)S(1)}, u32[]{:S(2)}, u32[]{:S(2)}) %collective-permute-start.4) | collective-permute-done | bytes 196640 | tf_op jit(solution)/shard_map/ppermute | solution.py:21
  19.0 2.8 %collective-permute-done.3.refs_4_ = bf16[128,768]{1,0:T(8,128)(2,1)S(1)} collective-permute-done((bf16[128,768]{1,0:T(8,128)(2,1)S(1)}, bf16[128,768]{1,0:T(8,128)(2,1)S(1)}, u32[]{:S(2)}, u32[]{:S(2)}) %collective-permute-start.3) | collective-permute-done | bytes 196640 | tf_op jit(solution)/shard_map/ppermute | solution.py:21
  21.8 1.2 %shard_map.68 = (bf16[4,144,768]{2,1,0:T(8,128)(2,1)S(1)}, s32[4,1,128,128]{3,2,1,0:T(8,128)S(1)}) custom-call(bf16[144,768]{1,0:T(8,128)(2,1)S(1)} %get-tuple-element.25.refs_0_, bf16[144,768]{1,0:T(8,128)(2,1)S(1)} %collective-permute-done.refs_1_, bf16[144,768]{1,0:T(8,128)(2,1)S(1)} %collective-permute-done.1.refs_2_, ...), custom_call_target="tpu_custom_call" | custom-call | flops 1 | bytes 1 | tf_op jit(solution)/shard_map/pallas_call | solution.py:30
  23.5 1.9 %collective-permute-done.5.m_ref.refs_1_.refs_6_ = bf16[4,144,768]{2,1,0:T(8,128)(2,1)S(1)} collective-permute-done((bf16[4,144,768]{2,1,0:T(8,128)(2,1)S(1)}, bf16[4,144,768]{2,1,0:T(8,128)(2,1)S(1)}, u32[]{:S(2)}, u32[]{:S(2)}) %collective-permute-start.5) | collective-permute-done | bytes 884768 | tf_op jit(solution)/shard_map/ppermute | solution.py:21
  25.4 1.2 %shard_map.69.refs_7_.refs_2_ = s32[4,1,128,128]{3,2,1,0:T(8,128)S(1)} custom-call(bf16[4,144,768]{2,1,0:T(8,128)(2,1)S(1)} %collective-permute-done.5.m_ref.refs_1_.refs_6_), custom_call_target="tpu_custom_call" | custom-call | flops 1 | bytes 1 | tf_op jit(solution)/shard_map/pallas_call | solution.py:30
  26.6 3.7 %collective-permute-done.6.refs_5_ = bf16[128,768]{1,0:T(8,128)(2,1)S(1)} collective-permute-done((bf16[128,768]{1,0:T(8,128)(2,1)S(1)}, bf16[128,768]{1,0:T(8,128)(2,1)S(1)}, u32[]{:S(2)}, u32[]{:S(2)}) %collective-permute-start.6) | collective-permute-done | bytes 196640 | tf_op jit(solution)/shard_map/ppermute | solution.py:21
  30.3 2.1 %shard_map.70 = (f32[512,1024]{1,0:T(8,128)S(1)}, f32[8,1024]{1,0:T(8,128)S(1)}, f32[8,512]{1,0:T(8,128)S(1)}) custom-call(bf16[4,144,768]{2,1,0:T(8,128)(2,1)S(1)} %get-tuple-element.27.refs_0_.refs_5_, bf16[4,144,768]{2,1,0:T(8,128)(2,1)S(1)} %collective-permute-done.5.m_ref.refs_1_.refs_6_, bf16[128,768]{1,0:T(8,128)(2,1)S(1)} %get-tuple-element.26.refs_2_, ...), custom_call_target="tpu_custom_call" | custom-call | flops 1 | bytes 1 | tf_op jit(solution)/shard_map/pallas_call | solution.py:30
  32.5 1.2 %collective-permute-done.7.other_ref = f32[8,1024]{1,0:T(8,128)S(1)} collective-permute-done((f32[8,1024]{1,0:T(8,128)S(1)}, f32[8,1024]{1,0:T(8,128)S(1)}, u32[]{:S(2)}, u32[]{:S(2)}) %collective-permute-start.7) | collective-permute-done | bytes 32800 | tf_op jit(solution)/shard_map/ppermute | solution.py:21
  33.7 1.6 %collective-permute-start.8 = (f32[8,1024]{1,0:T(8,128)S(1)}, f32[8,1024]{1,0:T(8,128)S(1)}, u32[]{:S(2)}, u32[]{:S(2)}) collective-permute-start(f32[8,1024]{1,0:T(8,128)S(1)} %shard_map.71.own_ref), channel_id=1, source_target_pairs={{0,2},{1,3},{2,0},{3,1},{4,6},{5,7},{6,4},{7,5},{8,10},{9,11},{10,... | collective-permute-start | bytes 98312 | tf_op jit(solution)/shard_map/ppermute | solution.py:21
  35.7 2.0 %collective-permute-done.8.other_ref = f32[8,1024]{1,0:T(8,128)S(1)} collective-permute-done((f32[8,1024]{1,0:T(8,128)S(1)}, f32[8,1024]{1,0:T(8,128)S(1)}, u32[]{:S(2)}, u32[]{:S(2)}) %collective-permute-start.8) | collective-permute-done | bytes 32800 | tf_op jit(solution)/shard_map/ppermute | solution.py:21
  37.7 1.6 %collective-permute-start.9 = (f32[8,1024]{1,0:T(8,128)S(1)}, f32[8,1024]{1,0:T(8,128)S(1)}, u32[]{:S(2)}, u32[]{:S(2)}) collective-permute-start(f32[8,1024]{1,0:T(8,128)S(1)} %shard_map.72.own_ref), channel_id=1, source_target_pairs={{0,4},{1,5},{2,6},{3,7},{4,0},{5,1},{6,2},{7,3},{8,12},{9,13},{10,... | collective-permute-start | bytes 98312 | tf_op jit(solution)/shard_map/ppermute | solution.py:21
  39.3 1.3 %collective-permute-start.11 = (f32[8,512]{1,0:T(8,128)S(1)}, f32[8,512]{1,0:T(8,128)S(1)}, u32[]{:S(2)}, u32[]{:S(2)}) collective-permute-start(f32[8,512]{1,0:T(8,128)S(1)} %shard_map.74.own_ref), channel_id=1, source_target_pairs={{0,16},{8,24},{16,0},{24,8},{1,17},{9,25},{17,1},{25,9},{2,18},{10... | collective-permute-start | bytes 49160 | tf_op jit(solution)/shard_map/ppermute | solution.py:21
  40.7 3.4 %collective-permute-done.11.other_ref = f32[8,512]{1,0:T(8,128)S(1)} collective-permute-done((f32[8,512]{1,0:T(8,128)S(1)}, f32[8,512]{1,0:T(8,128)S(1)}, u32[]{:S(2)}, u32[]{:S(2)}) %collective-permute-start.11) | collective-permute-done | bytes 16416 | tf_op jit(solution)/shard_map/ppermute | solution.py:21
  44.2 3.1 %shard_map.76 = (bf16[512,1024]{1,0:T(8,128)(2,1)S(1)}, bf16[512,1024]{1,0:T(8,128)(2,1)S(1)}, f32[128,768]{1,0:T(8,128)S(1)}, s16[144,768]{1,0:T(8,128)(2,1)S(1...) custom-call(f32[512,1024]{1,0:T(8,128)S(1)} %get-tuple-element.29.refs_0_, ...), custom_call_target="tpu_custom_call" | custom-call | flops 1 | bytes 1 | tf_op jit(solution)/shard_map/pallas_call | solution.py:30
  47.3 1.8 %shard_map.77 = (f32[512,768]{1,0:T(8,128)S(1)}, f32[520,768]{1,0:T(8,128)S(1)}) custom-call(bf16[512,1024]{1,0:T(8,128)(2,1)S(1)} %get-tuple-element.32.refs_0_, bf16[512,1024]{1,0:T(8,128)(2,1)S(1)} %get-tuple-element.33.refs_1_, bf16[128,768]{1,0:T(8,128)(2,1)S(1)} %get-tuple-element.26.refs_2_, ...), custom_call_target="tpu_custom_call" | custom-call | flops 1 | bytes 1 | tf_op jit(solution)/shard_map/pallas_call | solution.py:30
  49.7 7.4 %collective-permute-done.13.refs_1_ = s16[144,768]{1,0:T(8,128)(2,1)S(1)} collective-permute-done((s16[144,768]{1,0:T(8,128)(2,1)S(1)}, s16[144,768]{1,0:T(8,128)(2,1)S(1)}, u32[]{:S(2)}, u32[]{:S(2)}) %collective-permute-start.13) | collective-permute-done | bytes 221216 | tf_op jit(solution)/shard_map/ppermute | solution.py:21
  57.0 2.0 %shard_map.78 = (f32[128,768]{1,0:T(8,128)S(1)}, f32[8,128]{1,0:T(8,128)S(1)}, s16[144,768]{1,0:T(8,128)(2,1)S(1)}, s16[144,768]{1,0:T(8,128)(2,1)S(1)}, s16[144...) custom-call(f32[512,768]{1,0:T(8,128)S(1)} %get-tuple-element.35.even_ref, ...), custom_call_target="tpu_custom_call" | custom-call | flops 1 | bytes 1 | tf_op jit(solution)/shard_map/pallas_call | solution.py:30
  59.1 1.5 %collective-permute-start.14 = (s16[144,768]{1,0:T(8,128)(2,1)S(1)}, s16[144,768]{1,0:T(8,128)(2,1)S(1)}, u32[]{:S(2)}, u32[]{:S(2)}) collective-permute-start(s16[144,768]{1,0:T(8,128)(2,1)S(1)} %get-tuple-element.40), channel_id=1, source_target_pairs={{0,2},{1,3},{2,0},{3,1},{4,6},{5,7},{6,4},{7,5},{8,10},{9,11},{10,... | collective-permute-start | bytes 663560 | tf_op jit(solution)/shard_map/ppermute | solution.py:21
  61.1 1.5 %collective-permute-start.16 = (s16[144,768]{1,0:T(8,128)(2,1)S(1)}, s16[144,768]{1,0:T(8,128)(2,1)S(1)}, u32[]{:S(2)}, u32[]{:S(2)}) collective-permute-start(s16[144,768]{1,0:T(8,128)(2,1)S(1)} %get-tuple-element.42), channel_id=1, source_target_pairs={{0,6},{1,7},{2,4},{3,5},{4,2},{5,3},{6,0},{7,1},{8,14},{9,15},{10,... | collective-permute-start | bytes 663560 | tf_op jit(solution)/shard_map/ppermute | solution.py:21
  62.6 1.2 %collective-permute-start.17 = (s16[144,768]{1,0:T(8,128)(2,1)S(1)}, s16[144,768]{1,0:T(8,128)(2,1)S(1)}, u32[]{:S(2)}, u32[]{:S(2)}) collective-permute-start(s16[144,768]{1,0:T(8,128)(2,1)S(1)} %get-tuple-element.43), channel_id=1, source_target_pairs={{0,16},{8,24},{16,0},{24,8},{1,17},{9,25},{17,1},{25,9},{2,18},{10... | collective-permute-start | bytes 663560 | tf_op jit(solution)/shard_map/ppermute | solution.py:21
  63.9 1.8 %collective-permute-start.18 = (s16[144,768]{1,0:T(8,128)(2,1)S(1)}, s16[144,768]{1,0:T(8,128)(2,1)S(1)}, u32[]{:S(2)}, u32[]{:S(2)}) collective-permute-start(s16[144,768]{1,0:T(8,128)(2,1)S(1)} %get-tuple-element.46), channel_id=1, source_target_pairs={{0,8},{8,0},{16,24},{24,16},{1,9},{9,1},{17,25},{25,17},{2,10},{10... | collective-permute-start | bytes 663560 | tf_op jit(solution)/shard_map/ppermute | solution.py:21
  65.6 1.9 %collective-permute-done.14.refs_0_ = s16[144,768]{1,0:T(8,128)(2,1)S(1)} collective-permute-done((s16[144,768]{1,0:T(8,128)(2,1)S(1)}, s16[144,768]{1,0:T(8,128)(2,1)S(1)}, u32[]{:S(2)}, u32[]{:S(2)}) %collective-permute-start.14) | collective-permute-done | bytes 221216 | tf_op jit(solution)/shard_map/ppermute | solution.py:21
  67.5 4.6 %collective-permute-done.15.refs_1_ = s16[144,768]{1,0:T(8,128)(2,1)S(1)} collective-permute-done((s16[144,768]{1,0:T(8,128)(2,1)S(1)}, s16[144,768]{1,0:T(8,128)(2,1)S(1)}, u32[]{:S(2)}, u32[]{:S(2)}) %collective-permute-start.15) | collective-permute-done | bytes 221216 | tf_op jit(solution)/shard_map/ppermute | solution.py:21
  72.1 1.2 %shard_map.80 = f32[128,768]{1,0:T(8,128)} custom-call(f32[128,768]{1,0:T(8,128)S(1)} %get-tuple-element.44.own_ref, f32[8,128]{1,0:T(8,128)S(1)} %get-tuple-element.34.refs_6_.info_ref, s16[144,768]{1,0:T(8,128)(2,1)S(1)} %collective-permute-done.14.refs_0_, s16[144,768]{1,0:T(8,128)(2,1)S(1)} %collective-permute-done.15.refs_1_, ...), custom_call_target="tpu_custom_call" | custom-call | flops 1 | bytes 1 | tf_op jit(solution)/shard_map/pallas_call | solution.py:30
  73.2 1.1 %collective-permute-done.17.refs_3_.refs_0_ = s16[144,768]{1,0:T(8,128)(2,1)S(1)} collective-permute-done((s16[144,768]{1,0:T(8,128)(2,1)S(1)}, s16[144,768]{1,0:T(8,128)(2,1)S(1)}, u32[]{:S(2)}, u32[]{:S(2)}) %collective-permute-start.17) | collective-permute-done | bytes 221216 | tf_op jit(solution)/shard_map/ppermute | solution.py:21
  74.9 1.0 %shard_map.81 = f32[128,768]{1,0:T(8,128)} custom-call(f32[128,768]{1,0:T(8,128)S(1)} %get-tuple-element.45.own_ref, f32[8,128]{1,0:T(8,128)S(1)} %get-tuple-element.34.refs_6_.info_ref, s16[144,768]{1,0:T(8,128)(2,1)S(1)} %collective-permute-done.17.refs_3_.refs_0_, s16[144,768]{1,0:T(8,128)(2,1)S(1)} %collective-permute-done.18.refs_1_), custom_call_target="tpu_custom_call" | custom-call | flops 1 | bytes 1 | tf_op jit(solution)/shard_map/pallas_call | solution.py:30
  (29 shorter events, 4.6 us)
Async XLA Ops:
  0.6 1.0 %copy-start = (f32[128,768]{1,0:T(8,128)S(1)}, f32[128,768]{1,0:T(8,128)}, u32[]{:S(2)}) copy-start(f32[128,768]{1,0:T(8,128)} %refs_0_.1) | copy-start | bytes 1179652
  1.6 1.0 %copy-start.1 = (f32[128,768]{1,0:T(8,128)S(1)}, f32[128,768]{1,0:T(8,128)}, u32[]{:S(2)}) copy-start(f32[128,768]{1,0:T(8,128)} %refs_3_.1) | copy-start | bytes 1179652
  2.6 0.7 copy-start.2
  3.3 0.7 copy-start.3
  4.5 17.3 %collective-permute-start.2 = (bf16[144,768]{1,0:T(8,128)(2,1)S(1)}, bf16[144,768]{1,0:T(8,128)(2,1)S(1)}, u32[]{:S(2)}, u32[]{:S(2)}) collective-permute-start(bf16[144,768]{1,0:T(8,128)(2,1)S(1)} %get-tuple-element.25.refs_0_), channel_id=1, source_target_pairs={{0,6},{1,7},{2,4},{3,5},{4,2},{5,3},{6,0},{7,1},{8,14},{9,15},{10,... | collective-permute-start | bytes 663560 | tf_op jit(solution)/shard_map/ppermute | solution.py:21
  8.4 13.3 %collective-permute-start.1 = (bf16[144,768]{1,0:T(8,128)(2,1)S(1)}, bf16[144,768]{1,0:T(8,128)(2,1)S(1)}, u32[]{:S(2)}, u32[]{:S(2)}) collective-permute-start(bf16[144,768]{1,0:T(8,128)(2,1)S(1)} %get-tuple-element.25.refs_0_), channel_id=1, source_target_pairs={{0,4},{1,5},{2,6},{3,7},{4,0},{5,1},{6,2},{7,3},{8,12},{9,13},{10,... | collective-permute-start | bytes 663560 | tf_op jit(solution)/shard_map/ppermute | solution.py:21
  9.0 12.8 %collective-permute-start = (bf16[144,768]{1,0:T(8,128)(2,1)S(1)}, bf16[144,768]{1,0:T(8,128)(2,1)S(1)}, u32[]{:S(2)}, u32[]{:S(2)}) collective-permute-start(bf16[144,768]{1,0:T(8,128)(2,1)S(1)} %get-tuple-element.25.refs_0_), channel_id=1, source_target_pairs={{0,2},{1,3},{2,0},{3,1},{4,6},{5,7},{6,4},{7,5},{8,10},{9,11},{10,... | collective-permute-start | bytes 663560 | tf_op jit(solution)/shard_map/ppermute | solution.py:21
  9.1 9.9 %collective-permute-start.4 = (bf16[128,768]{1,0:T(8,128)(2,1)S(1)}, bf16[128,768]{1,0:T(8,128)(2,1)S(1)}, u32[]{:S(2)}, u32[]{:S(2)}) collective-permute-start(bf16[128,768]{1,0:T(8,128)(2,1)S(1)} %get-tuple-element.26.refs_2_), channel_id=1, source_target_pairs={{0,8},{8,0},{16,24},{24,16},{1,9},{9,1},{17,25},{25,17},{2,10},{10... | collective-permute-start | bytes 589832 | tf_op jit(solution)/shard_map/ppermute | solution.py:21
  11.1 10.7 %collective-permute-start.3 = (bf16[128,768]{1,0:T(8,128)(2,1)S(1)}, bf16[128,768]{1,0:T(8,128)(2,1)S(1)}, u32[]{:S(2)}, u32[]{:S(2)}) collective-permute-start(bf16[128,768]{1,0:T(8,128)(2,1)S(1)} %get-tuple-element.26.refs_2_), channel_id=1, source_target_pairs={{0,16},{8,24},{16,0},{24,8},{1,17},{9,25},{17,1},{25,9},{2,18},{10... | collective-permute-start | bytes 589832 | tf_op jit(solution)/shard_map/ppermute | solution.py:21
  22.9 2.5 %collective-permute-start.5 = (bf16[4,144,768]{2,1,0:T(8,128)(2,1)S(1)}, bf16[4,144,768]{2,1,0:T(8,128)(2,1)S(1)}, u32[]{:S(2)}, u32[]{:S(2)}) collective-permute-start(bf16[4,144,768]{2,1,0:T(8,128)(2,1)S(1)} %get-tuple-element.27.refs_0_.refs_5_), channel_id=1, source_target_pairs={{0,1},{1,0},{2,3},{3,2},{4,5},{5,4},{6,7},{7,6},{8,9},{9,8},{10,11... | collective-permute-start | bytes 2654216 | tf_op jit(solution)/shard_map/ppermute | solution.py:21
  23.0 7.3 %collective-permute-start.6 = (bf16[128,768]{1,0:T(8,128)(2,1)S(1)}, bf16[128,768]{1,0:T(8,128)(2,1)S(1)}, u32[]{:S(2)}, u32[]{:S(2)}) collective-permute-start(bf16[128,768]{1,0:T(8,128)(2,1)S(1)} %collective-permute-done.3.refs_4_), channel_id=1, source_target_pairs={{0,8},{8,0},{16,24},{24,16},{1,9},{9,1},{17,25},{25,17},{2,10},{10... | collective-permute-start | bytes 589832 | tf_op jit(solution)/shard_map/ppermute | solution.py:21
  32.4 1.3 %collective-permute-start.7 = (f32[8,1024]{1,0:T(8,128)S(1)}, f32[8,1024]{1,0:T(8,128)S(1)}, u32[]{:S(2)}, u32[]{:S(2)}) collective-permute-start(f32[8,1024]{1,0:T(8,128)S(1)} %get-tuple-element.30.own_ref), channel_id=1, source_target_pairs={{0,1},{1,0},{2,3},{3,2},{4,5},{5,4},{6,7},{7,6},{8,9},{9,8},{10,11... | collective-permute-start | bytes 98312 | tf_op jit(solution)/shard_map/ppermute | solution.py:21
  33.7 4.0 %collective-permute-start.8 = (f32[8,1024]{1,0:T(8,128)S(1)}, f32[8,1024]{1,0:T(8,128)S(1)}, u32[]{:S(2)}, u32[]{:S(2)}) collective-permute-start(f32[8,1024]{1,0:T(8,128)S(1)} %shard_map.71.own_ref), channel_id=1, source_target_pairs={{0,2},{1,3},{2,0},{3,1},{4,6},{5,7},{6,4},{7,5},{8,10},{9,11},{10,... | collective-permute-start | bytes 98312 | tf_op jit(solution)/shard_map/ppermute | solution.py:21
  35.3 4.0 %collective-permute-start.10 = (f32[8,512]{1,0:T(8,128)S(1)}, f32[8,512]{1,0:T(8,128)S(1)}, u32[]{:S(2)}, u32[]{:S(2)}) collective-permute-start(f32[8,512]{1,0:T(8,128)S(1)} %get-tuple-element.31.own_ref), channel_id=1, source_target_pairs={{0,8},{8,0},{16,24},{24,16},{1,9},{9,1},{17,25},{25,17},{2,10},{10... | collective-permute-start | bytes 49160 | tf_op jit(solution)/shard_map/ppermute | solution.py:21
  37.7 6.4 %collective-permute-start.9 = (f32[8,1024]{1,0:T(8,128)S(1)}, f32[8,1024]{1,0:T(8,128)S(1)}, u32[]{:S(2)}, u32[]{:S(2)}) collective-permute-start(f32[8,1024]{1,0:T(8,128)S(1)} %shard_map.72.own_ref), channel_id=1, source_target_pairs={{0,4},{1,5},{2,6},{3,7},{4,0},{5,1},{6,2},{7,3},{8,12},{9,13},{10,... | collective-permute-start | bytes 98312 | tf_op jit(solution)/shard_map/ppermute | solution.py:21
  39.3 4.8 %collective-permute-start.11 = (f32[8,512]{1,0:T(8,128)S(1)}, f32[8,512]{1,0:T(8,128)S(1)}, u32[]{:S(2)}, u32[]{:S(2)}) collective-permute-start(f32[8,512]{1,0:T(8,128)S(1)} %shard_map.74.own_ref), channel_id=1, source_target_pairs={{0,16},{8,24},{16,0},{24,8},{1,17},{9,25},{17,1},{25,9},{2,18},{10... | collective-permute-start | bytes 49160 | tf_op jit(solution)/shard_map/ppermute | solution.py:21
  49.1 7.9 %collective-permute-start.12 = (f32[520,768]{1,0:T(8,128)S(1)}, f32[520,768]{1,0:T(8,128)S(1)}, u32[]{:S(2)}, u32[]{:S(2)}) collective-permute-start(f32[520,768]{1,0:T(8,128)S(1)} %get-tuple-element.36), channel_id=1, source_target_pairs={{0,1},{1,0},{2,3},{3,2},{4,5},{5,4},{6,7},{7,6},{8,9},{9,8},{10,11... | collective-permute-start | bytes 4792328 | tf_op jit(solution)/shard_map/ppermute | solution.py:21
  49.2 7.8 %collective-permute-start.13 = (s16[144,768]{1,0:T(8,128)(2,1)S(1)}, s16[144,768]{1,0:T(8,128)(2,1)S(1)}, u32[]{:S(2)}, u32[]{:S(2)}) collective-permute-start(s16[144,768]{1,0:T(8,128)(2,1)S(1)} %get-tuple-element.38), channel_id=1, source_target_pairs={{0,8},{8,0},{16,24},{24,16},{1,9},{9,1},{17,25},{25,17},{2,10},{10... | collective-permute-start | bytes 663560 | tf_op jit(solution)/shard_map/ppermute | solution.py:21
  59.1 8.4 %collective-permute-start.14 = (s16[144,768]{1,0:T(8,128)(2,1)S(1)}, s16[144,768]{1,0:T(8,128)(2,1)S(1)}, u32[]{:S(2)}, u32[]{:S(2)}) collective-permute-start(s16[144,768]{1,0:T(8,128)(2,1)S(1)} %get-tuple-element.40), channel_id=1, source_target_pairs={{0,2},{1,3},{2,0},{3,1},{4,6},{5,7},{6,4},{7,5},{8,10},{9,11},{10,... | collective-permute-start | bytes 663560 | tf_op jit(solution)/shard_map/ppermute | solution.py:21
  60.6 11.5 %collective-permute-start.15 = (s16[144,768]{1,0:T(8,128)(2,1)S(1)}, s16[144,768]{1,0:T(8,128)(2,1)S(1)}, u32[]{:S(2)}, u32[]{:S(2)}) collective-permute-start(s16[144,768]{1,0:T(8,128)(2,1)S(1)} %get-tuple-element.41), channel_id=1, source_target_pairs={{0,4},{1,5},{2,6},{3,7},{4,0},{5,1},{6,2},{7,3},{8,12},{9,13},{10,... | collective-permute-start | bytes 663560 | tf_op jit(solution)/shard_map/ppermute | solution.py:21
  61.1 10.9 %collective-permute-start.16 = (s16[144,768]{1,0:T(8,128)(2,1)S(1)}, s16[144,768]{1,0:T(8,128)(2,1)S(1)}, u32[]{:S(2)}, u32[]{:S(2)}) collective-permute-start(s16[144,768]{1,0:T(8,128)(2,1)S(1)} %get-tuple-element.42), channel_id=1, source_target_pairs={{0,6},{1,7},{2,4},{3,5},{4,2},{5,3},{6,0},{7,1},{8,14},{9,15},{10,... | collective-permute-start | bytes 663560 | tf_op jit(solution)/shard_map/ppermute | solution.py:21
  62.6 11.7 %collective-permute-start.17 = (s16[144,768]{1,0:T(8,128)(2,1)S(1)}, s16[144,768]{1,0:T(8,128)(2,1)S(1)}, u32[]{:S(2)}, u32[]{:S(2)}) collective-permute-start(s16[144,768]{1,0:T(8,128)(2,1)S(1)} %get-tuple-element.43), channel_id=1, source_target_pairs={{0,16},{8,24},{16,0},{24,8},{1,17},{9,25},{17,1},{25,9},{2,18},{10... | collective-permute-start | bytes 663560 | tf_op jit(solution)/shard_map/ppermute | solution.py:21
  63.9 11.0 %collective-permute-start.18 = (s16[144,768]{1,0:T(8,128)(2,1)S(1)}, s16[144,768]{1,0:T(8,128)(2,1)S(1)}, u32[]{:S(2)}, u32[]{:S(2)}) collective-permute-start(s16[144,768]{1,0:T(8,128)(2,1)S(1)} %get-tuple-element.46), channel_id=1, source_target_pairs={{0,8},{8,0},{16,24},{24,16},{1,9},{9,1},{17,25},{25,17},{2,10},{10... | collective-permute-start | bytes 663560 | tf_op jit(solution)/shard_map/ppermute | solution.py:21

commit v3 on v0

v3 whole, which is shorter than its diff:
```python
import math

import jax
import jax.numpy as jnp
from jax import lax
from jax.experimental import pallas as pl
from jax.experimental.pallas import tpu as pltpu
from jax.sharding import PartitionSpec as P

F32 = jnp.float32
BF16 = jnp.bfloat16
TIME_BYTES = 3.6e6
VMEM_SPARE = 4 * 1024 * 1024
VMEM_MOST = 56 * 1024 * 1024
CODE_SPAN = 2.0**28
CODE_STEPS = 32000.0 / 28.0
LOSS_UNIT = 1.0 / 4096.0
DIGIT = 2.0**15


def exchange(value, axis, turn):
    size = lax.axis_size(axis)
    return lax.ppermute(value, axis, [(i, i ^ turn) for i in range(size)])


def call(kernel, out_shape, scratch_shapes, *operands, spare=(), room=None, time=0.1):
    size = sum(x.size * x.dtype.itemsize for x in (*operands, *jax.tree.leaves(out_shape)))
    held = [x for x in scratch_shapes if hasattr(x, "memory_space") and x.memory_space == pltpu.VMEM]
    size += sum(math.prod(x.shape) * jnp.dtype(x.dtype).itemsize for x in held)
    spaces = [pl.BlockSpec(memory_space=pltpu.VMEM)] * len(operands)
    spaces += [pl.BlockSpec(memory_space=pl.ANY)] * len(spare)
    return pl.pallas_call(
        kernel,
        out_shape=out_shape,
        in_specs=spaces,
        out_specs=jax.tree.map(lambda _: pl.BlockSpec(memory_space=pltpu.VMEM), out_shape),
        scratch_shapes=scratch_shapes,
        compiler_params=pltpu.CompilerParams(vmem_limit_bytes=room or 2 * size + VMEM_SPARE),
        cost_estimate=pl.CostEstimate(
            flops=1, bytes_accessed=int(time * TIME_BYTES), transcendentals=0
        ),
    )(*operands, *spare)


def put(ref, value):
    rows = value.shape[0]
    for g in range(value.shape[1] // 128):
        ref[g * rows : (g + 1) * rows, :] = value[:, g * 128 : (g + 1) * 128]


def get(ref, rows, width):
    return jnp.concatenate(
        [ref[g * rows : (g + 1) * rows, :] for g in range(width // 128)], axis=1
    )


def first_messages(queries, passages, hard_ids, list_lengths):
    rows, width = queries.shape
    listed = hard_ids.shape[1]
    body = width // 128 * rows
    operands = (passages, hard_ids.T, list_lengths.reshape(1, rows), queries)

    def kernel(*refs):
        sources, (q_out, near_out, far_out), held, sems = refs[:4], refs[4:7], refs[7:11], refs[11]
        copies = [
            pltpu.make_async_copy(src, dst, sems.at[n])
            for n, (src, dst) in enumerate(zip(sources, held))
        ]
        for copy in copies:
            copy.start()
        p_ref, ids_ref, len_ref, q_ref = held
        for copy in copies:
            copy.wait()
        part = p_ref[...].astype(BF16)
        for out in (near_out, far_out):
            put(out, part)
            out[body:, :] = jnp.zeros((out.shape[0] - body, 128), BF16)
        put(q_out, q_ref[...].astype(BF16))
        ids = ids_ref[...].astype(F32)
        live = lax.broadcasted_iota(jnp.int32, (listed, rows), 0) < len_ref[...]
        block = jnp.floor((ids + 0.5) * (1.0 / rows))
        number = (ids - block * rows + 128.0) * jnp.exp2(block - 64.0)
        q_out[body:, :] = jnp.where(live, number, 0.0).astype(BF16)

    return call(
        kernel,
        [jax.ShapeDtypeStruct((body + listed + more, 128), BF16) for more in (0, 0, 16)],
        [pltpu.VMEM(x.shape, x.dtype) for x in operands] + [pltpu.SemaphoreType.DMA((4,))],
        spare=operands,
        room=VMEM_MOST,
        time=2.0,
    )


def count_listed(message, listed, col_slots, after=()):
    body = message.shape[0] - listed
    rows = 128
    row_axis_size = lax.axis_size("pa")

    def kernel(m_ref, *refs):
        count_ref = refs[-1]
        if after:
            refs[-2][...] = m_ref[...]
        down, across = lax.axis_index("pb"), lax.axis_index("pa")
        number = m_ref[body:, :].astype(F32)
        live = number > 0.0
        block = jnp.floor(jnp.log2(jnp.where(live, number, 1.0)) + 57.002)
        inside = (number * jnp.exp2(64.0 - block) - 127.5).astype(jnp.int32)
        block = jnp.where(live, block, -1.0).astype(jnp.int32)
        steps = lax.broadcasted_iota(jnp.int32, (rows, rows), 0)
        for g in range(0, col_slots, 4):
            unit = jnp.zeros((listed, rows), jnp.int32)
            for j in range(g, min(g + 4, col_slots)):
                mine = (down ^ j) * row_axis_size + across
                unit = jnp.where(block == mine, 1 << (8 * (j - g)), unit)
            total = jnp.zeros((rows, rows), jnp.int32)
            for h in range(listed):
                total = total + jnp.where(inside[h : h + 1, :] == steps, unit[h : h + 1, :], 0)
            count_ref[g // 4] = total

    counts = jax.ShapeDtypeStruct((-(-col_slots // 4), rows, rows), jnp.int32)
    if not len(after):
        return message, call(kernel, counts, [], message, time=0.3)
    copied = jax.ShapeDtypeStruct(message.shape, message.dtype)
    return call(kernel, (copied, counts), [], message, spare=after, time=0.3)


def count_at(ref, j):
    return ((ref[j // 4] >> (8 * (j % 4))) & 255).astype(F32)


def score_sweep(messages, passage_slots, counts, rows, width):
    row_slots, col_slots = len(messages), len(passage_slots)
    tall, wide = row_slots * rows, col_slots * rows

    def most_of(part):
        most = jnp.max(jnp.abs(part.astype(F32)), axis=0, keepdims=True)
        return jnp.max(most, axis=1, keepdims=True)

    def kernel(*refs):
        q_refs, refs = refs[:row_slots], refs[row_slots:]
        p_refs, refs = refs[:col_slots], refs[col_slots:]
        c_refs, refs = refs[:row_slots], refs[row_slots:]
        s_ref, stat_ref, q_all, p_all, top_acc = refs
        stat_ref[...] = jnp.zeros_like(stat_ref)
        passage_most = jnp.zeros((1, 1), F32)
        for j in range(col_slots):
            part = get(p_refs[j], rows, width)
            p_all[j * rows : (j + 1) * rows, :] = part
            passage_most = jnp.maximum(passage_most, most_of(part))
        query_most = jnp.zeros((1, 1), F32)
        for m in range(row_slots // 2):
            both = [get(q, rows, width) for q in q_refs[2 * m : 2 * m + 2]]
            both = jnp.concatenate(both, axis=0)
            query_most = jnp.maximum(query_most, most_of(both))
            spot = slice(2 * m * rows, 2 * (m + 1) * rows)
            q_all[spot, :] = both
            s_ref[:, spot] = lax.dot_general(
                p_all[...], both, (((1,), (1,)), ((), ())), preferred_element_type=F32
            )
        stat_ref[2:3, :tall] = jnp.broadcast_to(passage_most, (1, tall))
        stat_ref[2:3, tall:] = jnp.broadcast_to(query_most, (1, wide))
        unit = lax.broadcasted_iota(jnp.int32, (rows, rows), 0) == lax.broadcasted_iota(
            jnp.int32, (rows, rows), 1
        )
        pairs = jnp.sum(jnp.where(unit, s_ref[:rows, :rows], 0.0), axis=0, keepdims=True)
        stat_ref[3:4, :tall] = jnp.broadcast_to(
            jnp.sum(pairs, axis=1, keepdims=True), (1, tall)
        )
        for k in range(row_slots):
            spot = slice(k * rows, (k + 1) * rows)
            top = jnp.full((1, rows), -jnp.inf, F32)
            for j in range(col_slots):
                here = slice(j * rows, (j + 1) * rows)
                part = s_ref[here, spot]
                top = jnp.maximum(top, jnp.max(part, axis=0, keepdims=True))
                if k == 0:
                    top_acc[here, :] = part
                else:
                    top_acc[here, :] = jnp.maximum(top_acc[here, :], part)
            total = jnp.zeros((1, rows), F32)
            for j in range(col_slots):
                here = slice(j * rows, (j + 1) * rows)
                times = 1.0 + count_at(c_refs[k], j)
                total = total + jnp.sum(
                    jnp.exp(s_ref[here, spot] - top) * times, axis=0, keepdims=True
                )
            stat_ref[0:1, spot] = top
            stat_ref[1:2, spot] = total
        for j in range(col_slots):
            here = slice(j * rows, (j + 1) * rows)
            there = slice(tall + j * rows, tall + (j + 1) * rows)
            acc = top_acc[here, :]
            stat_ref[0:1, there] = jnp.max(acc.T, axis=0, keepdims=True)
            top = jnp.max(acc, axis=1, keepdims=True)
            total = jnp.zeros((rows, rows), F32)
            for k in range(row_slots):
                total = total + jnp.exp(s_ref[here, k * rows : (k + 1) * rows] - top)
            stat_ref[1:2, there] = jnp.sum(total.T, axis=0, keepdims=True)

    return call(
        kernel,
        (
            jax.ShapeDtypeStruct((wide, tall), F32),
            jax.ShapeDtypeStruct((8, tall + wide), F32),
            jax.ShapeDtypeStruct((tall, width), BF16),
            jax.ShapeDtypeStruct((wide, width), BF16),
        ),
        [pltpu.VMEM((wide, rows), F32)],
        *messages,
        *passage_slots,
        *counts,
        time=2.0,
    )


def turned(value, turn, rows):
    slots = value.shape[1] // rows
    return jnp.concatenate(
        [value[:, (k ^ turn) * rows : ((k ^ turn) + 1) * rows] for k in range(slots)], axis=1
    )


def tree(combine, values):
    while len(values) > 1:
        values = [combine(a, b) for a, b in zip(values[::2], values[1::2])]
    return values[0]


def joined(one, two):
    top = jnp.maximum(one[0:1], two[0:1])
    total = one[1:2] * jnp.exp(one[0:1] - top) + two[1:2] * jnp.exp(two[0:1] - top)
    most = jnp.maximum(one[2:3], two[2:3])
    return jnp.concatenate([top, total, most, one[3:] + two[3:]], axis=0)


def share_out(own, other, tall, wide, rows, after):
    def kernel(own_ref, other_ref, after_ref, out_ref):
        first = lax.axis_index("pa") % 2 == 0
        by_row = joined(own_ref[:, :tall], turned(other_ref[:, :tall], 1, rows))
        by_col = jnp.concatenate([own_ref[:, tall:], other_ref[:, tall:]], axis=1)
        out_ref[...] = jnp.where(first, by_row, by_col)

    return call(kernel, jax.ShapeDtypeStruct((8, tall), F32), [], own, other, spare=[after])


def share_all(own, others, rows):
    def kernel(own_ref, *refs):
        first = lax.axis_index("pa") % 2 == 0
        parts = [own_ref[...]]
        for t, ref in enumerate(refs[:-1], start=1):
            there = ref[...]
            parts.append(jnp.where(first, turned(there, 2 * t, rows), turned(there, t, rows)))
        refs[-1][...] = tree(joined, parts)

    return call(kernel, jax.ShapeDtypeStruct(own.shape, F32), [], own, *others)


def levels(own, other, wide, rows):
    tall = own.shape[1]

    def kernel(own_ref, other_ref, row_ref, col_ref, info_ref):
        first = lax.axis_index("pa") % 2 == 0
        own_v, other_v = own_ref[...], other_ref[...]
        by_row = jnp.where(first, own_v, turned(other_v, 1, rows))
        by_col = jnp.where(first, other_v, own_v)
        mine = jnp.where(first, by_col[:, wide:], by_col[:, :wide])
        row_level = by_row[0:1] + jnp.log(by_row[1:2])
        both = by_col[0:1] + jnp.log(by_col[1:2])
        row_ref[...] = jnp.broadcast_to(row_level, row_ref.shape)
        columns = mine[0:1] + jnp.log(mine[1:2])
        for j in range(wide // rows):
            here = slice(j * rows, (j + 1) * rows)
            col_ref[here, :] = jnp.broadcast_to(columns[:, here], (rows, rows)).T

        def summed(level):
            parts = [
                jnp.sum(level[:, g * rows : (g + 1) * rows], axis=1, keepdims=True)
                for g in range(level.shape[1] // rows)
            ]
            return tree(jnp.add, parts)

        row_term = summed(row_level) - 2.0 * by_row[3:4, :1]
        query_bound = jnp.maximum(mine[2:3, :1] * (tall * 1.02 + 8.0), 1e-30)
        passage_bound = jnp.maximum(by_row[2:3, :1] * (2 * wide * 1.02 + 8.0), 1e-30)
        info_ref[...] = jnp.zeros_like(info_ref)
        for n, value in enumerate((row_term, summed(both), query_bound, passage_bound)):
            info_ref[n : n + 1, :] = jnp.broadcast_to(value, (1, rows))

    return call(
        kernel,
        (
            jax.ShapeDtypeStruct((8, tall), F32),
            jax.ShapeDtypeStruct((wide, rows), F32),
            jax.ShapeDtypeStruct((8, rows), F32),
        ),
        [],
        own,
        other,
    )


def coded(value, inverse):
    steps = jnp.log2(jnp.abs(value) * (inverse * CODE_SPAN) + 1.0) * CODE_STEPS + 0.5
    return jnp.where(value < 0.0, -steps, steps).astype(jnp.int32).astype(jnp.int16)


def decoded(code, bound):
    steps = code.astype(F32)
    size = (jnp.exp2(jnp.abs(steps) * (1.0 / CODE_STEPS)) - 1.0) * (bound * (1.0 / CODE_SPAN))
    return jnp.where(steps < 0.0, -size, size)


def write_term(ref, value):
    lanes = lax.broadcasted_iota(jnp.int32, (16, 128), 1)
    left = value[:, :1] * LOSS_UNIT
    digits = jnp.zeros((16, 128), F32)
    for n in range(3):
        digit = jnp.round(left)
        left = (left - digit) * DIGIT
        digits = jnp.where(lanes == n, digit, digits)
    ref[ref.shape[0] - 16 :, :] = digits.astype(jnp.int32).astype(jnp.int16)


def read_term(ref):
    digits = ref[ref.shape[0] - 16 :, :].astype(F32)[:1, :]
    one, two, three = digits[:, 0:1], digits[:, 1:2], digits[:, 2:3]
    return (one + (two + three * (1.0 / DIGIT)) * (1.0 / DIGIT)) * (1.0 / LOSS_UNIT)


def weight_sweep(picked, scores, row_level, col_level, counts):
    wide, tall = scores.shape
    rows = col_level.shape[1]
    row_slots = tall // rows

    def kernel(s_ref, row_ref, col_ref, *refs):
        c_refs, (hi_ref, lo_ref) = refs[:row_slots], refs[row_slots:]
        unit = (
            lax.broadcasted_iota(jnp.int32, (rows, rows), 0)
            == lax.broadcasted_iota(jnp.int32, (rows, rows), 1)
        ).astype(F32)
        for n, j in enumerate(picked):
            here = slice(j * rows, (j + 1) * rows)
            for k in range(row_slots):
                spot = slice(k * rows, (k + 1) * rows)
                part = s_ref[here, spot]
                by_row = jnp.exp(part - row_ref[0:1, spot])
                by_col = jnp.exp(part - col_ref[here, :])
                pair = (by_row + by_col).astype(BF16).astype(F32)
                hard = by_row.astype(BF16).astype(F32)
                weight = pair + hard * count_at(c_refs[k], j)
                if j == 0 and k == 0:
                    weight = weight - 2.0 * unit
                high = weight.astype(BF16)
                hi_ref[n, :, spot] = high
                lo_ref[n, :, spot] = (weight - high.astype(F32)).astype(BF16)

    weights = jax.ShapeDtypeStruct((len(picked), rows, tall), BF16)
    return call(
        kernel,
        (weights, weights),
        [],
        scores,
        row_level,
        col_level,
        *counts,
        time=0.45 * len(picked),
    )


def passage_sweep(picked, held, weights, q_all, info, term=False):
    high, low = weights
    rows, width = info.shape[1], q_all.shape[1]
    body = width // 128 * rows
    odd = [j for j in picked if j % 2]
    even = [j for j in picked if j % 2 == 0]

    def kernel(hi_ref, lo_ref, q_ref, info_ref, *out_refs):
        inverse = 1.0 / info_ref[2:3, :1]
        if term:
            write_term(out_refs[-1], info_ref[0:1, :])
        for j in picked:
            n = held.index(j)
            part = jnp.dot(hi_ref[n], q_ref[...], preferred_element_type=F32)
            part = part + jnp.dot(lo_ref[n], q_ref[...], preferred_element_type=F32)
            if j % 2:
                first = odd.index(j) * body
                put(out_refs[-1].at[first : first + body, :], coded(part, inverse))
            else:
                put(out_refs[even.index(j)], part)

    outs = [jax.ShapeDtypeStruct((body, 128), F32)] * len(even)
    if odd:
        outs.append(jax.ShapeDtypeStruct((len(odd) * body + 16 * term, 128), jnp.int16))
    return call(kernel, outs, [], high, low, q_all, info, time=0.4 * len(picked))


def flipped(block):
    def kernel(in_ref, out_ref):
        out_ref[...] = in_ref[...].astype(F32).T.astype(BF16)

    shape = jax.ShapeDtypeStruct(block.shape[::-1], BF16)
    return call(kernel, shape, [], block, time=0.3)


def query_sweep(pairs, weights, picked, passages, info):
    width, rows = passages.shape[0], info.shape[1]
    slots = sorted((j, 2 * i, n) for i, part in enumerate(picked) for n, j in enumerate(part))

    def kernel(*refs):
        w_refs, (p_ref, info_ref, *even_refs, odd_ref) = refs[: len(weights)], refs[len(weights) :]
        for i, (m, even_ref) in enumerate(zip(pairs, even_refs)):
            spot = slice(2 * m * rows, 2 * (m + 1) * rows)
            total = jnp.zeros((width, 2 * rows), F32)
            for side in range(2):
                weight = [w_refs[g + side][n, :, spot] for _, g, n in slots]
                weight = jnp.concatenate(weight, axis=0)
                total = total + jnp.dot(p_ref[...], weight, preferred_element_type=F32)
            even_ref[...] = total[:, :rows]
            odd_ref[i * width : (i + 1) * width, :] = coded(
                total[:, rows:], 1.0 / info_ref[3:4, :1]
            )

    blocks = [jax.ShapeDtypeStruct((width, rows), F32)] * len(pairs)
    blocks.append(jax.ShapeDtypeStruct((len(pairs) * width, rows), jnp.int16))
    return call(kernel, blocks, [], *weights, passages, info, time=0.6 * len(pairs))


def send_on(own, arrived, info, bound_row, term_row, part=0, longer=0, after=()):
    body = own.shape[0]

    def kernel(own_ref, arrived_ref, info_ref, *refs):
        out_ref = refs[-1]
        bound = info_ref[bound_row : bound_row + 1, :1]
        total = own_ref[...] + decoded(arrived_ref[part * body : (part + 1) * body, :], bound)
        out_ref[:body, :] = coded(total, 1.0 / bound)
        out_ref[body:, :] = jnp.zeros((16 + longer, 128), jnp.int16)
        term = info_ref[term_row : term_row + 1, :1]
        if arrived.shape[0] % body:
            term = term + read_term(arrived_ref)
        write_term(out_ref, term)

    return call(
        kernel,
        jax.ShapeDtypeStruct((body + 16 + longer, 128), jnp.int16),
        [],
        own,
        arrived,
        info,
        spare=after,
        time=0.5,
    )


def added(own, arrived, info, bound_row, after=()):
    body = own.shape[0]

    def kernel(own_ref, info_ref, *refs):
        bound = info_ref[bound_row : bound_row + 1, :1]
        total = own_ref[...]
        for (_, part), ref in zip(arrived, refs):
            total = total + decoded(ref[part * body : (part + 1) * body, :], bound)
        refs[-1][...] = total

    block = jax.ShapeDtypeStruct(own.shape, F32)
    messages = [message for message, _ in arrived]
    return call(kernel, block, [], own, info, *messages, spare=after, time=0.3)


def finish_passages(own, arrived, info, width, after):
    body = own.shape[0]
    rows = body * 128 // width

    def kernel(own_ref, info_ref, *refs):
        bound = info_ref[2:3, :1]
        total = own_ref[...]
        for ref in refs[: len(arrived)]:
            total = total + decoded(ref[:body, :], bound)
        refs[-2][...] = 0.5 * get(total, rows, width)
        refs[-1][...] = info_ref[...]

    outs = (jax.ShapeDtypeStruct((rows, width), F32), jax.ShapeDtypeStruct(info.shape, F32))
    return call(kernel, outs, [], own, info, *arrived, spare=after, time=1.0)


def finish_queries(own, late, side, near, along, info, devices, after):
    body, rows = own.shape

    def kernel(own_ref, info_ref, term_ref, *refs):
        s_refs, refs = refs[: len(side)], refs[len(side) :]
        a_refs, (loss_ref, out_ref) = refs[: len(along)], refs[-2:]
        bound = info_ref[3:4, :1]
        total = own_ref[...]
        for ref in s_refs[:late]:
            total = total + decoded(ref[:body, :], bound)
        for g in range(body // 128):
            here = slice(g * 128, (g + 1) * 128)
            out_ref[:, here] = 0.5 * total[here, :].T
        sides = [info_ref[1:2, :1]] + [read_term(ref) for ref in s_refs]
        lines = [info_ref[0:1, :1] + read_term(term_ref)] + [read_term(ref) for ref in a_refs]
        loss = tree(jnp.add, sides) + tree(jnp.add, lines)
        loss_ref[...] = loss * (1.0 / (2.0 * rows * devices))

    outs = (jax.ShapeDtypeStruct((1, 1), F32), jax.ShapeDtypeStruct((rows, body), F32))
    return call(kernel, outs, [], own, info, near, *side, *along, spare=[after], time=1.0)


def per_device(queries, passages, hard_ids, list_lengths):
    rows, width = queries.shape
    listed = hard_ids.shape[1]
    across = lax.axis_size("pa")
    down = lax.axis_size("pb")
    tall, wide = across * rows, down * rows

    message, near_message, far_message = first_messages(
        queries, passages, hard_ids, list_lengths
    )
    far = [exchange(far_message, "pb", j) for j in range(2, down, 2)]
    near = exchange(near_message, "pb", 1)
    passage_slots = [near_message, near]
    for part in far:
        passage_slots += [part, exchange(part, "pb", 1)]
    row_turns = list(range(0, across, 2))
    messages, counts = [], []
    for k in row_turns:
        part = exchange(message, "pa", k) if k else message
        part, count = count_listed(part, listed, down, [near, *far, counts[0]] if k else [])
        other, other_count = count_listed(exchange(part, "pa", 1), listed, down)
        messages += [part, other]
        counts += [count, other_count]

    scores, stats, q_all, p_all = score_sweep(messages, passage_slots, counts, rows, width)
    passages = flipped(p_all)
    stats = share_out(stats, exchange(stats, "pa", 1), tall, wide, rows, passages)
    others = []
    for t in range(1, down):
        pairs = []
        for i in range(across * down):
            z, c = divmod(i, across)
            pairs.append((i, z * across + (c ^ 2 * t) if c % 2 == 0 else (z ^ t) * across + c))
        others.append(lax.ppermute(stats, ("pb", "pa"), pairs))
    stats = share_all(stats, others, rows)
    row_level, col_level, info = levels(stats, exchange(stats, "pa", 1), wide, rows)

    swept = (scores, row_level, col_level, counts)
    onward = list(range(3, down, 2))
    staying = [*range(2, down, 2), 1, 0]
    first = weight_sweep(onward, *swept)
    (near,) = passage_sweep(onward, onward, first, q_all, info, True)
    near = exchange(near, "pb", 1)
    second = weight_sweep(staying, *swept)
    weights = [*first, *second]
    blocks = passage_sweep(staying[:-2], staying, second, q_all, info)
    along = [
        exchange(send_on(own, near, info, 2, 0, part, 16), "pb", 2 * (part + 1))
        for part, own in enumerate(blocks)
    ]
    (last,) = passage_sweep([1], staying, second, q_all, info)
    last = exchange(last, "pb", 1)
    (passage_sum,) = passage_sweep([0], staying, second, q_all, info)

    side = []
    for m in range(across // 2):
        own, other = query_sweep([m], weights, [onward, staying], passages, info)
        other = exchange(other, "pa", 1)
        if m:
            after = [last] if m == 2 else []
            side.append(exchange(send_on(own, other, info, 3, 1, after=after), "pa", 2 * m))
        else:
            query_sum, core = own, other
    query_sum = added(query_sum, [(core, 0), (side[-1], 0)], info, 3)
    grad_passages, after = finish_passages(
        passage_sum, [last, *along], info, width, [query_sum]
    )
    loss, grad_queries = finish_queries(
        query_sum, len(side) - 1, side, near, along, info, across * down, after
    )
    return (loss.reshape(()), grad_queries, grad_passages)


def solution(mesh):
    return jax.shard_map(
        per_device,
        mesh=mesh,
        in_specs=(
            P(("pb", "pa"), None),
            P(("pb", "pa"), None),
            P(("pb", "pa"), None),
            P(("pb", "pa")),
        ),
        out_specs=(P(), P(("pb", "pa"), None), P(("pb", "pa"), None)),
        check_vma=False,
    )
```

time: 649 us -> 60.9 us (0.09)
  blocking collectives: 436 us -> 0 us
  local copies, waits for them, and re-layouts: 89.7 us -> 0.94 us
  other arithmetic: 61 us -> 0 us
  matrix products: 22.9 us -> 0 us
  Pallas kernels: 0 us -> 18 us
  between operations: 17.2 us -> 0.88 us
  starting transfers between devices: 14.7 us -> 25.9 us
  waiting for transfers between devices: 5.74 us -> 14.9 us
    all_gather x5 -> x0, blocking collectives: 230 us -> none  [the longest x1 189 us: per_device(): passage_block = lax.all_gather(passage_own, 'pb', axis=0, tiled=True)]
    psum x1 -> x0, blocking collectives: 206 us -> none  [per_device(): loss = lax.psum(partial_loss, ('pb', 'pa')) / (2.0 * row_count * devices)]
    gather x2 -> x0, local copies, waits for them, and re-layouts: 45.4 us -> none  [the longest x1 23.3 us: per_device(): fetched.reshape(devices * capacity, feature_width)[slot_place]]
    scatter x2 -> x0, local copies, waits for them, and re-layouts: 40.2 us -> none  [the longest x1 24.7 us: per_device(): contribution = jnp.zeros((devices * capacity, feature_width), jnp.float32...]
    scatter-add x1 -> x0, other arithmetic: 36.7 us -> none  [per_device(): hard_passage = jnp.zeros((row_count, feature_width), jnp.float32).at[aske...]
    ppermute x0 -> x25, starting transfers between devices: none -> 25.9 us  [the longest x22 22.4 us: exchange(): return lax.ppermute(value, axis, [(i, i ^ turn) for i in range(size)])]
    dot_general x8 -> x0, matrix products: 22.9 us -> none  [the longest x2 5.55 us: query_piece_work(): return jnp.dot(weights, passage_block, preferred_element_type=jnp.float32)]
    pallas_call x0 -> x31, Pallas kernels: none -> 18 us  [call(): pl.pallas_call(kernel, out_shape=out_shape, in_specs=spaces, out_specs=ja...]
  transfers between devices with their start and end apart: 6 -> 25, of which waited for: 1 -> 14; matrix products, arithmetic and copies ran while one was open for 4% -> 0% of each run, Pallas kernels for 0% -> 19%
where the time goes in v3:
time: 60.9 us; the launch traced here: 60.7 us
  starting transfers between devices  25.9 us (43%)
  Pallas kernels  18 us (30%)
  waiting for transfers between devices  14.9 us (24%)
  local copies, waits for them, and re-layouts  0.94 us (2%)
  between operations  0.88 us (1%)
    ppermute x22, starting transfers between devices, exchange(): return lax.ppermute(value, axis, [(i, i ^ turn) for i in range(size)])  22.4 us
    pallas_call x31, Pallas kernels, call(): pl.pallas_call(kernel, out_shape=out_shape, in_specs=spaces, out_specs=ja...  18 us
    ppermute x22, waiting for transfers between devices, exchange(): return lax.ppermute(value, axis, [(i, i ^ turn) for i in range(size)])  11.9 us
    ppermute x3, starting transfers between devices, per_device(): others.append(lax.ppermute(stats, ('pb', 'pa'), pairs))  3.55 us
    ppermute x3, waiting for transfers between devices, per_device(): others.append(lax.ppermute(stats, ('pb', 'pa'), pairs))  3.04 us
  transfers between devices with their start and end apart: 25, of which 14 were waited for; matrix products, arithmetic and copies ran while one was open for 0% of the time, Pallas kernels for 19%

profile of v3, /device:TPU:0, one launch (start us, length us, event | category | flops | bytes accessed | tf_op | source)
XLA Modules:
  0.0 60.7 jit_solution(1464862468967269967)
XLA Ops:
  0.6 2.0 %shard_map.67 = (bf16[800,128]{1,0:T(8,128)(2,1)}, bf16[800,128]{1,0:T(8,128)(2,1)}, bf16[816,128]{1,0:T(8,128)(2,1)}) custom-call(f32[128,768]{1,0:T(8,128)} %refs_0_.1, s32[32,128]{1,0:T(8,128)} %bitcast.3, s32[1,128]{1,0:T(1,128)} %bitcast.4, f32[128,768]{1,0:T(8,128)} %refs_3_.1), custom_call_target="tpu_custom_call" | custom-call | flops 1 | bytes 7200000 | tf_op jit(solution)/shard_map/pallas_call | solution.py:32
  2.7 4.1 %collective-permute-start.3 = (bf16[816,128]{1,0:T(8,128)(2,1)}, bf16[816,128]{1,0:T(8,128)(2,1)S(1)}, u32[]{:S(2)}, u32[]{:S(2)}) collective-permute-start(bf16[816,128]{1,0:T(8,128)(2,1)} %get-tuple-element.37), channel_id=1, source_target_pairs={{0,16},{8,24},{16,0},{24,8},{1,17},{9,25},{17,1},{25,9},{2,18},{10... | collective-permute-start | bytes 626696 | tf_op jit(solution)/shard_map/ppermute | solution.py:23
  6.8 1.6 %collective-permute-start.2 = (bf16[800,128]{1,0:T(8,128)(2,1)}, bf16[800,128]{1,0:T(8,128)(2,1)S(1)}, u32[]{:S(2)}, u32[]{:S(2)}) collective-permute-start(bf16[800,128]{1,0:T(8,128)(2,1)} %get-tuple-element.36.refs_8_), channel_id=1, source_target_pairs={{0,8},{8,0},{16,24},{24,16},{1,9},{9,1},{17,25},{25,17},{2,10},{10... | collective-permute-start | bytes 614408 | tf_op jit(solution)/shard_map/ppermute | solution.py:23
  8.3 1.5 %collective-permute-start.1 = (bf16[800,128]{1,0:T(8,128)(2,1)}, bf16[800,128]{1,0:T(8,128)(2,1)S(1)}, u32[]{:S(2)}, u32[]{:S(2)}) collective-permute-start(bf16[800,128]{1,0:T(8,128)(2,1)} %get-tuple-element.35.m_ref.refs_0_), channel_id=1, source_target_pairs={{0,2},{1,3},{2,0},{3,1},{4,6},{5,7},{6,4},{7,5},{8,10},{9,11},{10,... | collective-permute-start | bytes 614408 | tf_op jit(solution)/shard_map/ppermute | solution.py:23
  9.8 1.5 %collective-permute-start.5 = (bf16[800,128]{1,0:T(8,128)(2,1)}, bf16[800,128]{1,0:T(8,128)(2,1)S(1)}, u32[]{:S(2)}, u32[]{:S(2)}) collective-permute-start(bf16[800,128]{1,0:T(8,128)(2,1)} %get-tuple-element.35.m_ref.refs_0_), channel_id=1, source_target_pairs={{0,4},{1,5},{2,6},{3,7},{4,0},{5,1},{6,2},{7,3},{8,12},{9,13},{10,... | collective-permute-start | bytes 614408 | tf_op jit(solution)/shard_map/ppermute | solution.py:23
  11.8 4.9 %collective-permute-done.3.refs_1_.refs_10_ = bf16[816,128]{1,0:T(8,128)(2,1)S(1)} collective-permute-done((bf16[816,128]{1,0:T(8,128)(2,1)}, bf16[816,128]{1,0:T(8,128)(2,1)S(1)}, u32[]{:S(2)}, u32[]{:S(2)}) %collective-permute-start.3) | collective-permute-done | bytes 208928 | tf_op jit(solution)/shard_map/ppermute | solution.py:23
  16.7 0.7 %collective-permute-start.9 = (bf16[816,128]{1,0:T(8,128)(2,1)S(1)}, bf16[816,128]{1,0:T(8,128)(2,1)S(1)}, u32[]{:S(2)}, u32[]{:S(2)}) collective-permute-start(bf16[816,128]{1,0:T(8,128)(2,1)S(1)} %collective-permute-done.3.refs_1_.refs_10_), channel_id=1, source_target_pairs={{0,8},{8,0},{16,24},{24,16},{1,9},{9,1},{17,25},{25,17},{2,10},{10... | collective-permute-start | bytes 626696 | tf_op jit(solution)/shard_map/ppermute | solution.py:23
  17.4 0.9 %copy-done = bf16[800,128]{1,0:T(8,128)(2,1)S(1)} copy-done((bf16[800,128]{1,0:T(8,128)(2,1)S(1)}, bf16[800,128]{1,0:T(8,128)(2,1)}, u32[]{:S(2)}) %copy-start) | copy-done | bytes 204824
  19.7 0.8 %collective-permute-done.5.m_ref = bf16[800,128]{1,0:T(8,128)(2,1)S(1)} collective-permute-done((bf16[800,128]{1,0:T(8,128)(2,1)}, bf16[800,128]{1,0:T(8,128)(2,1)S(1)}, u32[]{:S(2)}, u32[]{:S(2)}) %collective-permute-start.5) | collective-permute-done | bytes 204832 | tf_op jit(solution)/shard_map/ppermute | solution.py:23
  23.1 2.2 %shard_map.76 = (f32[512,1024]{1,0:T(8,128)S(1)}, f32[8,1536]{1,0:T(8,128)S(1)}, bf16[1024,768]{1,0:T(8,128)(2,1)S(1)}, bf16[512,768]{1,0:T(8,128)(2,1)S(1)}) custom-call(bf16[800,128]{1,0:T(8,128)(2,1)S(1)} %copy-done.1, bf16[800,128]{1,0:T(8,128)(2,1)S(1)} %collective-permute-done.m_ref.refs_1_, bf16[800,128]{1,0:T(8,128)(2,1)S(1)} %get-tuple-element.38.refs_2_, ...), custom_call_target="tpu_custom_call" | custom-call | flops 1 | bytes 7200000 | tf_op jit(solution)/shard_map/pallas_call | solution.py:32
  26.1 0.6 collective-permute-done.10.other_ref
  26.7 2.2 %collective-permute-start.13 = (f32[8,1024]{1,0:T(8,128)S(1)}, f32[8,1024]{1,0:T(8,128)S(1)}, u32[]{:S(2)}, u32[]{:S(2)}) collective-permute-start(f32[8,1024]{1,0:T(8,128)S(1)} %shard_map.78.own_ref), channel_id=1, source_target_pairs={{0,6},{1,25},{2,4},{3,27},{4,2},{5,29},{6,0},{7,31},{8,14},{9,17},... | collective-permute-start | bytes 98312 | tf_op jit(solution)/shard_map/ppermute | solution.py:541
  29.4 0.9 %collective-permute-start.11 = (f32[8,1024]{1,0:T(8,128)S(1)}, f32[8,1024]{1,0:T(8,128)S(1)}, u32[]{:S(2)}, u32[]{:S(2)}) collective-permute-start(f32[8,1024]{1,0:T(8,128)S(1)} %shard_map.78.own_ref), channel_id=1, source_target_pairs={{0,2},{1,9},{2,0},{3,11},{4,6},{5,13},{6,4},{7,15},{8,10},{9,1},{1... | collective-permute-start | bytes 98312 | tf_op jit(solution)/shard_map/ppermute | solution.py:541
  30.3 1.3 %collective-permute-done.13.refs_2_ = f32[8,1024]{1,0:T(8,128)S(1)} collective-permute-done((f32[8,1024]{1,0:T(8,128)S(1)}, f32[8,1024]{1,0:T(8,128)S(1)}, u32[]{:S(2)}, u32[]{:S(2)}) %collective-permute-start.13) | collective-permute-done | bytes 32800 | tf_op jit(solution)/shard_map/ppermute | solution.py:541
  31.6 1.2 %collective-permute-done.12.refs_1_ = f32[8,1024]{1,0:T(8,128)S(1)} collective-permute-done((f32[8,1024]{1,0:T(8,128)S(1)}, f32[8,1024]{1,0:T(8,128)S(1)}, u32[]{:S(2)}, u32[]{:S(2)}) %collective-permute-start.12) | collective-permute-done | bytes 32800 | tf_op jit(solution)/shard_map/ppermute | solution.py:541
  33.4 1.2 %collective-permute-start.14 = (f32[8,1024]{1,0:T(8,128)S(1)}, f32[8,1024]{1,0:T(8,128)S(1)}, u32[]{:S(2)}, u32[]{:S(2)}) collective-permute-start(f32[8,1024]{1,0:T(8,128)S(1)} %shard_map.79.own_ref), channel_id=1, source_target_pairs={{0,1},{1,0},{2,3},{3,2},{4,5},{5,4},{6,7},{7,6},{8,9},{9,8},{10,11... | collective-permute-start | bytes 98312 | tf_op jit(solution)/shard_map/ppermute | solution.py:23
  34.6 0.9 %collective-permute-done.14.other_ref = f32[8,1024]{1,0:T(8,128)S(1)} collective-permute-done((f32[8,1024]{1,0:T(8,128)S(1)}, f32[8,1024]{1,0:T(8,128)S(1)}, u32[]{:S(2)}, u32[]{:S(2)}) %collective-permute-start.14) | collective-permute-done | bytes 32800 | tf_op jit(solution)/shard_map/ppermute | solution.py:23
  36.0 0.7 %shard_map.87 = s16[784,128]{1,0:T(8,128)(2,1)S(1)} custom-call(bf16[1,128,1024]{2,1,0:T(8,128)(2,1)S(1)} %get-tuple-element.49.refs_0_.hi_ref, bf16[1,128,1024]{2,1,0:T(8,128)(2,1)S(1)} %get-tuple-element.50.refs_1_.lo_ref, bf16[1024,768]{1,0:T(8,128)(2,1)S(1)} %get-tuple-element.58.q_ref, f32[8,128]{1,0:T(8,128)S(1)} %get-tuple-element.53.refs_5_.info_ref), custom_call_target="tpu_custom_call" | custom-call | flops 1 | bytes 1440000 | tf_op jit(solution)/shard_map/pallas_call | solution.py:32
  36.7 1.0 %collective-permute-start.18 = (s16[784,128]{1,0:T(8,128)(2,1)S(1)}, s16[784,128]{1,0:T(8,128)(2,1)S(1)}, u32[]{:S(2)}, u32[]{:S(2)}) collective-permute-start(s16[784,128]{1,0:T(8,128)(2,1)S(1)} %shard_map.87), channel_id=1, source_target_pairs={{0,8},{8,0},{16,24},{24,16},{1,9},{9,1},{17,25},{25,17},{2,10},{10... | collective-permute-start | bytes 602120 | tf_op jit(solution)/shard_map/ppermute | solution.py:23
  37.7 1.0 %shard_map.82 = (bf16[3,128,1024]{2,1,0:T(8,128)(2,1)S(1)}, bf16[3,128,1024]{2,1,0:T(8,128)(2,1)S(1)}) custom-call(f32[512,1024]{1,0:T(8,128)S(1)} %get-tuple-element.44.s_ref, f32[8,1024]{1,0:T(8,128)S(1)} %get-tuple-element.47.row_ref, f32[512,128]{1,0:T(8,128)S(1)} %get-tuple-element.48.col_ref, s32[1,128,128]{2,1,0:T(8,128)S(1)} %shard_map.68.refs_2_.refs_12_.refs_0_, ...), custom_call_target="tpu_custom_call" | custom-call | flops 1 | bytes 4860000 | tf_op jit(solution)/shard_map/pallas_call | solution.py:32
  39.5 0.7 %shard_map.91 = s16[768,128]{1,0:T(8,128)(2,1)S(1)} custom-call(bf16[3,128,1024]{2,1,0:T(8,128)(2,1)S(1)} %get-tuple-element.51.refs_2_.hi_ref, bf16[3,128,1024]{2,1,0:T(8,128)(2,1)S(1)} %get-tuple-element.52.refs_3_.lo_ref, bf16[1024,768]{1,0:T(8,128)(2,1)S(1)} %get-tuple-element.58.q_ref, f32[8,128]{1,0:T(8,128)S(1)} %get-tuple-element.53.refs_5_.info_ref), custom_call_target="tpu_custom_call" | custom-call | flops 1 | bytes 1440000 | tf_op jit(solution)/shard_map/pallas_call | solution.py:32
  40.1 0.6 shard_map.90
  40.8 1.2 %collective-permute-start.22 = (s16[768,128]{1,0:T(8,128)(2,1)S(1)}, s16[768,128]{1,0:T(8,128)(2,1)S(1)}, u32[]{:S(2)}, u32[]{:S(2)}) collective-permute-start(s16[768,128]{1,0:T(8,128)(2,1)S(1)} %shard_map.91), channel_id=1, source_target_pairs={{0,8},{8,0},{16,24},{24,16},{1,9},{9,1},{17,25},{25,17},{2,10},{10... | collective-permute-start | bytes 589832 | tf_op jit(solution)/shard_map/ppermute | solution.py:23
  44.5 2.4 %collective-permute-start.24 = (s16[800,128]{1,0:T(8,128)(2,1)S(1)}, s16[800,128]{1,0:T(8,128)(2,1)S(1)}, u32[]{:S(2)}, u32[]{:S(2)}) collective-permute-start(s16[800,128]{1,0:T(8,128)(2,1)S(1)} %shard_map.94), channel_id=1, source_target_pairs={{0,16},{8,24},{16,0},{24,8},{1,17},{9,25},{17,1},{25,9},{2,18},{10... | collective-permute-start | bytes 614408 | tf_op jit(solution)/shard_map/ppermute | solution.py:23
  47.3 2.1 %collective-permute-start.17 = (s16[784,128]{1,0:T(8,128)(2,1)S(1)}, s16[784,128]{1,0:T(8,128)(2,1)S(1)}, u32[]{:S(2)}, u32[]{:S(2)}) collective-permute-start(s16[784,128]{1,0:T(8,128)(2,1)S(1)} %shard_map.85), channel_id=1, source_target_pairs={{0,6},{1,7},{2,4},{3,5},{4,2},{5,3},{6,0},{7,1},{8,14},{9,15},{10,... | collective-permute-start | bytes 602120 | tf_op jit(solution)/shard_map/ppermute | solution.py:23
  49.4 1.5 %collective-permute-done.22.refs_0_ = s16[768,128]{1,0:T(8,128)(2,1)S(1)} collective-permute-done((s16[768,128]{1,0:T(8,128)(2,1)S(1)}, s16[768,128]{1,0:T(8,128)(2,1)S(1)}, u32[]{:S(2)}, u32[]{:S(2)}) %collective-permute-start.22) | collective-permute-done | bytes 196640 | tf_op jit(solution)/shard_map/ppermute | solution.py:23
  51.3 1.6 %collective-permute-start.23 = (s16[784,128]{1,0:T(8,128)(2,1)S(1)}, s16[784,128]{1,0:T(8,128)(2,1)S(1)}, u32[]{:S(2)}, u32[]{:S(2)}) collective-permute-start(s16[784,128]{1,0:T(8,128)(2,1)S(1)} %shard_map.92), channel_id=1, source_target_pairs={{0,4},{1,5},{2,6},{3,7},{4,0},{5,1},{6,2},{7,3},{8,12},{9,13},{10,... | collective-permute-start | bytes 602120 | tf_op jit(solution)/shard_map/ppermute | solution.py:23
  53.3 0.6 %collective-permute-start.20 = (s16[784,128]{1,0:T(8,128)(2,1)S(1)}, s16[784,128]{1,0:T(8,128)(2,1)S(1)}, u32[]{:S(2)}, u32[]{:S(2)}) collective-permute-start(s16[784,128]{1,0:T(8,128)(2,1)S(1)} %shard_map.89), channel_id=1, source_target_pairs={{0,2},{1,3},{2,0},{3,1},{4,6},{5,7},{6,4},{7,5},{8,10},{9,11},{10,... | collective-permute-start | bytes 602120 | tf_op jit(solution)/shard_map/ppermute | solution.py:23
  55.2 0.8 %collective-permute-done.15.refs_0_ = s16[768,128]{1,0:T(8,128)(2,1)S(1)} collective-permute-done((s16[768,128]{1,0:T(8,128)(2,1)S(1)}, s16[768,128]{1,0:T(8,128)(2,1)S(1)}, u32[]{:S(2)}, u32[]{:S(2)}) %collective-permute-start.15) | collective-permute-done | bytes 196640 | tf_op jit(solution)/shard_map/ppermute | solution.py:23
  56.8 1.2 %shard_map.96 = (f32[128,768]{1,0:T(8,128)}, f32[8,128]{1,0:T(8,128)S(1)}) custom-call(f32[768,128]{1,0:T(8,128)S(1)} %shard_map.95.own_ref, f32[8,128]{1,0:T(8,128)S(1)} %get-tuple-element.53.refs_5_.info_ref, s16[768,128]{1,0:T(8,128)(2,1)S(1)} %collective-permute-done.22.refs_0_, s16[800,128]{1,0:T(8,128)(2,1)S(1)} %collective-permute-done.24.refs_1_.refs_3_, ...), custom_call_target="tpu_custom_call" | custom-call | flops 1 | bytes 3600000 | tf_op jit(solution)/shard_map/pallas_call | solution.py:32
  57.9 1.6 %collective-permute-done.23.refs_1_ = s16[784,128]{1,0:T(8,128)(2,1)S(1)} collective-permute-done((s16[784,128]{1,0:T(8,128)(2,1)S(1)}, s16[784,128]{1,0:T(8,128)(2,1)S(1)}, u32[]{:S(2)}, u32[]{:S(2)}) %collective-permute-start.23) | collective-permute-done | bytes 200736 | tf_op jit(solution)/shard_map/ppermute | solution.py:23
  59.6 1.1 %shard_map.97 = (f32[1,1]{1,0:T(1,128)}, f32[128,768]{1,0:T(8,128)}) custom-call(f32[768,128]{1,0:T(8,128)S(1)} %shard_map.86.refs_2_.own_ref, f32[8,128]{1,0:T(8,128)S(1)} %get-tuple-element.53.refs_5_.info_ref, s16[784,128]{1,0:T(8,128)(2,1)S(1)} %collective-permute-done.18.arrived_ref.term_ref, s16[784,128]{1,0:T(8,128)(2,1)S(1)} %collective-permute-done.20.refs_0_, ...), custom_call_target="tpu_custom_call" | custom-call | flops 1 | bytes 3600000 | tf_op jit(solution)/shard_map/pallas_call | solution.py:32
  (55 shorter events, 13.2 us)
Async XLA Ops:
  2.7 14.1 %collective-permute-start.3 = (bf16[816,128]{1,0:T(8,128)(2,1)}, bf16[816,128]{1,0:T(8,128)(2,1)S(1)}, u32[]{:S(2)}, u32[]{:S(2)}) collective-permute-start(bf16[816,128]{1,0:T(8,128)(2,1)} %get-tuple-element.37), channel_id=1, source_target_pairs={{0,16},{8,24},{16,0},{24,8},{1,17},{9,25},{17,1},{25,9},{2,18},{10... | collective-permute-start | bytes 626696 | tf_op jit(solution)/shard_map/ppermute | solution.py:23
  6.8 11.9 %collective-permute-start.2 = (bf16[800,128]{1,0:T(8,128)(2,1)}, bf16[800,128]{1,0:T(8,128)(2,1)S(1)}, u32[]{:S(2)}, u32[]{:S(2)}) collective-permute-start(bf16[800,128]{1,0:T(8,128)(2,1)} %get-tuple-element.36.refs_8_), channel_id=1, source_target_pairs={{0,8},{8,0},{16,24},{24,16},{1,9},{9,1},{17,25},{25,17},{2,10},{10... | collective-permute-start | bytes 614408 | tf_op jit(solution)/shard_map/ppermute | solution.py:23
  8.3 10.4 %collective-permute-start.1 = (bf16[800,128]{1,0:T(8,128)(2,1)}, bf16[800,128]{1,0:T(8,128)(2,1)S(1)}, u32[]{:S(2)}, u32[]{:S(2)}) collective-permute-start(bf16[800,128]{1,0:T(8,128)(2,1)} %get-tuple-element.35.m_ref.refs_0_), channel_id=1, source_target_pairs={{0,2},{1,3},{2,0},{3,1},{4,6},{5,7},{6,4},{7,5},{8,10},{9,11},{10,... | collective-permute-start | bytes 614408 | tf_op jit(solution)/shard_map/ppermute | solution.py:23
  9.8 10.6 %collective-permute-start.5 = (bf16[800,128]{1,0:T(8,128)(2,1)}, bf16[800,128]{1,0:T(8,128)(2,1)S(1)}, u32[]{:S(2)}, u32[]{:S(2)}) collective-permute-start(bf16[800,128]{1,0:T(8,128)(2,1)} %get-tuple-element.35.m_ref.refs_0_), channel_id=1, source_target_pairs={{0,4},{1,5},{2,6},{3,7},{4,0},{5,1},{6,2},{7,3},{8,12},{9,13},{10,... | collective-permute-start | bytes 614408 | tf_op jit(solution)/shard_map/ppermute | solution.py:23
  11.4 9.5 %collective-permute-start.7 = (bf16[800,128]{1,0:T(8,128)(2,1)}, bf16[800,128]{1,0:T(8,128)(2,1)S(1)}, u32[]{:S(2)}, u32[]{:S(2)}) collective-permute-start(bf16[800,128]{1,0:T(8,128)(2,1)} %get-tuple-element.35.m_ref.refs_0_), channel_id=1, source_target_pairs={{0,6},{1,7},{2,4},{3,5},{4,2},{5,3},{6,0},{7,1},{8,14},{9,15},{10,... | collective-permute-start | bytes 614408 | tf_op jit(solution)/shard_map/ppermute | solution.py:23
  16.7 6.3 %collective-permute-start.9 = (bf16[816,128]{1,0:T(8,128)(2,1)S(1)}, bf16[816,128]{1,0:T(8,128)(2,1)S(1)}, u32[]{:S(2)}, u32[]{:S(2)}) collective-permute-start(bf16[816,128]{1,0:T(8,128)(2,1)S(1)} %collective-permute-done.3.refs_1_.refs_10_), channel_id=1, source_target_pairs={{0,8},{8,0},{16,24},{24,16},{1,9},{9,1},{17,25},{25,17},{2,10},{10... | collective-permute-start | bytes 626696 | tf_op jit(solution)/shard_map/ppermute | solution.py:23
  17.4 0.9 %copy-start = (bf16[800,128]{1,0:T(8,128)(2,1)S(1)}, bf16[800,128]{1,0:T(8,128)(2,1)}, u32[]{:S(2)}) copy-start(bf16[800,128]{1,0:T(8,128)(2,1)} %get-tuple-element.35.m_ref.refs_0_) | copy-start | bytes 614404
  18.4 4.7 %copy-start.1 = (bf16[800,128]{1,0:T(8,128)(2,1)S(1)}, bf16[800,128]{1,0:T(8,128)(2,1)}, u32[]{:S(2)}) copy-start(bf16[800,128]{1,0:T(8,128)(2,1)} %get-tuple-element.35.m_ref.refs_0_) | copy-start | bytes 614404
  18.4 4.7 %copy-start.2 = (bf16[800,128]{1,0:T(8,128)(2,1)S(1)}, bf16[800,128]{1,0:T(8,128)(2,1)}, u32[]{:S(2)}) copy-start(bf16[800,128]{1,0:T(8,128)(2,1)} %get-tuple-element.36.refs_8_) | copy-start | bytes 614404
  18.7 3.0 %collective-permute-start = (bf16[800,128]{1,0:T(8,128)(2,1)S(1)}, bf16[800,128]{1,0:T(8,128)(2,1)S(1)}, u32[]{:S(2)}, u32[]{:S(2)}) collective-permute-start(bf16[800,128]{1,0:T(8,128)(2,1)S(1)} %copy-done), channel_id=1, source_target_pairs={{0,1},{1,0},{2,3},{3,2},{4,5},{5,4},{6,7},{7,6},{8,9},{9,8},{10,11... | collective-permute-start | bytes 614408 | tf_op jit(solution)/shard_map/ppermute | solution.py:23
  19.1 2.9 %collective-permute-start.4 = (bf16[800,128]{1,0:T(8,128)(2,1)S(1)}, bf16[800,128]{1,0:T(8,128)(2,1)S(1)}, u32[]{:S(2)}, u32[]{:S(2)}) collective-permute-start(bf16[800,128]{1,0:T(8,128)(2,1)S(1)} %get-tuple-element.38.refs_2_), channel_id=1, source_target_pairs={{0,1},{1,0},{2,3},{3,2},{4,5},{5,4},{6,7},{7,6},{8,9},{9,8},{10,11... | collective-permute-start | bytes 614408 | tf_op jit(solution)/shard_map/ppermute | solution.py:23
  20.7 1.6 %collective-permute-start.6 = (bf16[800,128]{1,0:T(8,128)(2,1)S(1)}, bf16[800,128]{1,0:T(8,128)(2,1)S(1)}, u32[]{:S(2)}, u32[]{:S(2)}) collective-permute-start(bf16[800,128]{1,0:T(8,128)(2,1)S(1)} %get-tuple-element.39.refs_4_), channel_id=1, source_target_pairs={{0,1},{1,0},{2,3},{3,2},{4,5},{5,4},{6,7},{7,6},{8,9},{9,8},{10,11... | collective-permute-start | bytes 614408 | tf_op jit(solution)/shard_map/ppermute | solution.py:23
  21.1 1.6 %collective-permute-start.8 = (bf16[800,128]{1,0:T(8,128)(2,1)S(1)}, bf16[800,128]{1,0:T(8,128)(2,1)S(1)}, u32[]{:S(2)}, u32[]{:S(2)}) collective-permute-start(bf16[800,128]{1,0:T(8,128)(2,1)S(1)} %get-tuple-element.40.refs_6_), channel_id=1, source_target_pairs={{0,1},{1,0},{2,3},{3,2},{4,5},{5,4},{6,7},{7,6},{8,9},{9,8},{10,11... | collective-permute-start | bytes 614408 | tf_op jit(solution)/shard_map/ppermute | solution.py:23
  25.4 1.3 %collective-permute-start.10 = (f32[8,1536]{1,0:T(8,128)S(1)}, f32[8,1536]{1,0:T(8,128)S(1)}, u32[]{:S(2)}, u32[]{:S(2)}) collective-permute-start(f32[8,1536]{1,0:T(8,128)S(1)} %get-tuple-element.45.own_ref), channel_id=1, source_target_pairs={{0,1},{1,0},{2,3},{3,2},{4,5},{5,4},{6,7},{7,6},{8,9},{9,8},{10,11... | collective-permute-start | bytes 147464 | tf_op jit(solution)/shard_map/ppermute | solution.py:23
  26.7 4.9 %collective-permute-start.13 = (f32[8,1024]{1,0:T(8,128)S(1)}, f32[8,1024]{1,0:T(8,128)S(1)}, u32[]{:S(2)}, u32[]{:S(2)}) collective-permute-start(f32[8,1024]{1,0:T(8,128)S(1)} %shard_map.78.own_ref), channel_id=1, source_target_pairs={{0,6},{1,25},{2,4},{3,27},{4,2},{5,29},{6,0},{7,31},{8,14},{9,17},... | collective-permute-start | bytes 98312 | tf_op jit(solution)/shard_map/ppermute | solution.py:541
  28.9 3.9 %collective-permute-start.12 = (f32[8,1024]{1,0:T(8,128)S(1)}, f32[8,1024]{1,0:T(8,128)S(1)}, u32[]{:S(2)}, u32[]{:S(2)}) collective-permute-start(f32[8,1024]{1,0:T(8,128)S(1)} %shard_map.78.own_ref), channel_id=1, source_target_pairs={{0,4},{1,17},{2,6},{3,19},{4,0},{5,21},{6,2},{7,23},{8,12},{9,25},... | collective-permute-start | bytes 98312 | tf_op jit(solution)/shard_map/ppermute | solution.py:541
  29.4 3.9 %collective-permute-start.11 = (f32[8,1024]{1,0:T(8,128)S(1)}, f32[8,1024]{1,0:T(8,128)S(1)}, u32[]{:S(2)}, u32[]{:S(2)}) collective-permute-start(f32[8,1024]{1,0:T(8,128)S(1)} %shard_map.78.own_ref), channel_id=1, source_target_pairs={{0,2},{1,9},{2,0},{3,11},{4,6},{5,13},{6,4},{7,15},{8,10},{9,1},{1... | collective-permute-start | bytes 98312 | tf_op jit(solution)/shard_map/ppermute | solution.py:541
  33.4 2.0 %collective-permute-start.14 = (f32[8,1024]{1,0:T(8,128)S(1)}, f32[8,1024]{1,0:T(8,128)S(1)}, u32[]{:S(2)}, u32[]{:S(2)}) collective-permute-start(f32[8,1024]{1,0:T(8,128)S(1)} %shard_map.79.own_ref), channel_id=1, source_target_pairs={{0,1},{1,0},{2,3},{3,2},{4,5},{5,4},{6,7},{7,6},{8,9},{9,8},{10,11... | collective-permute-start | bytes 98312 | tf_op jit(solution)/shard_map/ppermute | solution.py:23
  36.7 7.3 %collective-permute-start.18 = (s16[784,128]{1,0:T(8,128)(2,1)S(1)}, s16[784,128]{1,0:T(8,128)(2,1)S(1)}, u32[]{:S(2)}, u32[]{:S(2)}) collective-permute-start(s16[784,128]{1,0:T(8,128)(2,1)S(1)} %shard_map.87), channel_id=1, source_target_pairs={{0,8},{8,0},{16,24},{24,16},{1,9},{9,1},{17,25},{25,17},{2,10},{10... | collective-permute-start | bytes 602120 | tf_op jit(solution)/shard_map/ppermute | solution.py:23
  39.4 7.5 %collective-permute-start.16 = (s16[768,128]{1,0:T(8,128)(2,1)S(1)}, s16[768,128]{1,0:T(8,128)(2,1)S(1)}, u32[]{:S(2)}, u32[]{:S(2)}) collective-permute-start(s16[768,128]{1,0:T(8,128)(2,1)S(1)} %get-tuple-element.57), channel_id=1, source_target_pairs={{0,1},{1,0},{2,3},{3,2},{4,5},{5,4},{6,7},{7,6},{8,9},{9,8},{10,11... | collective-permute-start | bytes 589832 | tf_op jit(solution)/shard_map/ppermute | solution.py:23
  40.8 10.1 %collective-permute-start.22 = (s16[768,128]{1,0:T(8,128)(2,1)S(1)}, s16[768,128]{1,0:T(8,128)(2,1)S(1)}, u32[]{:S(2)}, u32[]{:S(2)}) collective-permute-start(s16[768,128]{1,0:T(8,128)(2,1)S(1)} %shard_map.91), channel_id=1, source_target_pairs={{0,8},{8,0},{16,24},{24,16},{1,9},{9,1},{17,25},{25,17},{2,10},{10... | collective-permute-start | bytes 589832 | tf_op jit(solution)/shard_map/ppermute | solution.py:23
  41.9 9.0 %collective-permute-start.21 = (s16[768,128]{1,0:T(8,128)(2,1)S(1)}, s16[768,128]{1,0:T(8,128)(2,1)S(1)}, u32[]{:S(2)}, u32[]{:S(2)}) collective-permute-start(s16[768,128]{1,0:T(8,128)(2,1)S(1)} %get-tuple-element.62), channel_id=1, source_target_pairs={{0,1},{1,0},{2,3},{3,2},{4,5},{5,4},{6,7},{7,6},{8,9},{9,8},{10,11... | collective-permute-start | bytes 589832 | tf_op jit(solution)/shard_map/ppermute | solution.py:23
  42.7 10.2 %collective-permute-start.19 = (s16[768,128]{1,0:T(8,128)(2,1)S(1)}, s16[768,128]{1,0:T(8,128)(2,1)S(1)}, u32[]{:S(2)}, u32[]{:S(2)}) collective-permute-start(s16[768,128]{1,0:T(8,128)(2,1)S(1)} %get-tuple-element.60), channel_id=1, source_target_pairs={{0,1},{1,0},{2,3},{3,2},{4,5},{5,4},{6,7},{7,6},{8,9},{9,8},{10,11... | collective-permute-start | bytes 589832 | tf_op jit(solution)/shard_map/ppermute | solution.py:23
  44.5 12.3 %collective-permute-start.24 = (s16[800,128]{1,0:T(8,128)(2,1)S(1)}, s16[800,128]{1,0:T(8,128)(2,1)S(1)}, u32[]{:S(2)}, u32[]{:S(2)}) collective-permute-start(s16[800,128]{1,0:T(8,128)(2,1)S(1)} %shard_map.94), channel_id=1, source_target_pairs={{0,16},{8,24},{16,0},{24,8},{1,17},{9,25},{17,1},{25,9},{2,18},{10... | collective-permute-start | bytes 614408 | tf_op jit(solution)/shard_map/ppermute | solution.py:23
  47.3 9.1 %collective-permute-start.17 = (s16[784,128]{1,0:T(8,128)(2,1)S(1)}, s16[784,128]{1,0:T(8,128)(2,1)S(1)}, u32[]{:S(2)}, u32[]{:S(2)}) collective-permute-start(s16[784,128]{1,0:T(8,128)(2,1)S(1)} %shard_map.85), channel_id=1, source_target_pairs={{0,6},{1,7},{2,4},{3,5},{4,2},{5,3},{6,0},{7,1},{8,14},{9,15},{10,... | collective-permute-start | bytes 602120 | tf_op jit(solution)/shard_map/ppermute | solution.py:23
  51.3 8.2 %collective-permute-start.23 = (s16[784,128]{1,0:T(8,128)(2,1)S(1)}, s16[784,128]{1,0:T(8,128)(2,1)S(1)}, u32[]{:S(2)}, u32[]{:S(2)}) collective-permute-start(s16[784,128]{1,0:T(8,128)(2,1)S(1)} %shard_map.92), channel_id=1, source_target_pairs={{0,4},{1,5},{2,6},{3,7},{4,0},{5,1},{6,2},{7,3},{8,12},{9,13},{10,... | collective-permute-start | bytes 602120 | tf_op jit(solution)/shard_map/ppermute | solution.py:23
  53.3 6.3 %collective-permute-start.20 = (s16[784,128]{1,0:T(8,128)(2,1)S(1)}, s16[784,128]{1,0:T(8,128)(2,1)S(1)}, u32[]{:S(2)}, u32[]{:S(2)}) collective-permute-start(s16[784,128]{1,0:T(8,128)(2,1)S(1)} %shard_map.89), channel_id=1, source_target_pairs={{0,2},{1,3},{2,0},{3,1},{4,6},{5,7},{6,4},{7,5},{8,10},{9,11},{10,... | collective-permute-start | bytes 602120 | tf_op jit(solution)/shard_map/ppermute | solution.py:23
  54.5 1.5 %collective-permute-start.15 = (s16[768,128]{1,0:T(8,128)(2,1)S(1)}, s16[768,128]{1,0:T(8,128)(2,1)S(1)}, u32[]{:S(2)}, u32[]{:S(2)}) collective-permute-start(s16[768,128]{1,0:T(8,128)(2,1)S(1)} %get-tuple-element.55), channel_id=1, source_target_pairs={{0,1},{1,0},{2,3},{3,2},{4,5},{5,4},{6,7},{7,6},{8,9},{9,8},{10,11... | collective-permute-start | bytes 589832 | tf_op jit(solution)/shard_map/ppermute | solution.py:23

commit v4 on v3

--- a/solution.py
+++ b/solution.py
@@ -14,7 +14,7 @@
 VMEM_MOST = 56 * 1024 * 1024
 CODE_SPAN = 2.0**28
 CODE_STEPS = 32000.0 / 28.0
-LOSS_UNIT = 1.0 / 4096.0
+LOSS_UNIT = 1.0 / 16384.0
 DIGIT = 2.0**15
 
 
@@ -134,7 +134,8 @@
     tall, wide = row_slots * rows, col_slots * rows
 
     def most_of(part):
-        most = jnp.max(jnp.abs(part.astype(F32)), axis=0, keepdims=True)
+        tiles = [jnp.abs(part[n : n + 16, :]) for n in range(0, part.shape[0], 16)]
+        most = jnp.max(tree(jnp.maximum, tiles).astype(F32), axis=0, keepdims=True)
         return jnp.max(most, axis=1, keepdims=True)
 
     def kernel(*refs):
@@ -148,6 +149,26 @@
             part = get(p_refs[j], rows, width)
             p_all[j * rows : (j + 1) * rows, :] = part
             passage_most = jnp.maximum(passage_most, most_of(part))
+        def row_stats(k):
+            spot = slice(k * rows, (k + 1) * rows)
+            tops = []
+            for j in range(col_slots):
+                here = slice(j * rows, (j + 1) * rows)
+                part = s_ref[here, spot]
+                tops.append(jnp.max(part, axis=0, keepdims=True))
+                if k == 0:
+                    top_acc[here, :] = part
+                else:
+                    top_acc[here, :] = jnp.maximum(top_acc[here, :], part)
+            top = tree(jnp.maximum, tops)
+            total = jnp.zeros((rows, rows), F32)
+            for j in range(col_slots):
+                here = slice(j * rows, (j + 1) * rows)
+                times = 1.0 + count_at(c_refs[k], j)
+                total = total + jnp.exp(s_ref[here, spot] - top) * times
+            stat_ref[0:1, spot] = top
+            stat_ref[1:2, spot] = jnp.sum(total, axis=0, keepdims=True)
+
         query_most = jnp.zeros((1, 1), F32)
         for m in range(row_slots // 2):
             both = [get(q, rows, width) for q in q_refs[2 * m : 2 * m + 2]]
@@ -158,35 +179,19 @@
             s_ref[:, spot] = lax.dot_general(
                 p_all[...], both, (((1,), (1,)), ((), ())), preferred_element_type=F32
             )
+            if m:
+                row_stats(2 * m - 2)
+                row_stats(2 * m - 1)
+        row_stats(row_slots - 2)
+        row_stats(row_slots - 1)
         stat_ref[2:3, :tall] = jnp.broadcast_to(passage_most, (1, tall))
         stat_ref[2:3, tall:] = jnp.broadcast_to(query_most, (1, wide))
         unit = lax.broadcasted_iota(jnp.int32, (rows, rows), 0) == lax.broadcasted_iota(
             jnp.int32, (rows, rows), 1
         )
         pairs = jnp.sum(jnp.where(unit, s_ref[:rows, :rows], 0.0), axis=0, keepdims=True)
-        stat_ref[3:4, :tall] = jnp.broadcast_to(
-            jnp.sum(pairs, axis=1, keepdims=True), (1, tall)
-        )
-        for k in range(row_slots):
-            spot = slice(k * rows, (k + 1) * rows)
-            top = jnp.full((1, rows), -jnp.inf, F32)
-            for j in range(col_slots):
-                here = slice(j * rows, (j + 1) * rows)
-                part = s_ref[here, spot]
-                top = jnp.maximum(top, jnp.max(part, axis=0, keepdims=True))
-                if k == 0:
-                    top_acc[here, :] = part
-                else:
-                    top_acc[here, :] = jnp.maximum(top_acc[here, :], part)
-            total = jnp.zeros((1, rows), F32)
-            for j in range(col_slots):
-                here = slice(j * rows, (j + 1) * rows)
-                times = 1.0 + count_at(c_refs[k], j)
-                total = total + jnp.sum(
-                    jnp.exp(s_ref[here, spot] - top) * times, axis=0, keepdims=True
-                )
-            stat_ref[0:1, spot] = top
-            stat_ref[1:2, spot] = total
+        stat_ref[3:4, :rows] = pairs
+        stat_ref[3:4, tall : tall + rows] = pairs
         for j in range(col_slots):
             here = slice(j * rows, (j + 1) * rows)
             there = slice(tall + j * rows, tall + (j + 1) * rows)
@@ -280,11 +285,12 @@
             ]
             return tree(jnp.add, parts)
 
-        row_term = summed(row_level) - 2.0 * by_row[3:4, :1]
+        row_term = summed(row_level - by_row[3:4])
+        col_term = summed(both - by_col[3:4])
         query_bound = jnp.maximum(mine[2:3, :1] * (tall * 1.02 + 8.0), 1e-30)
         passage_bound = jnp.maximum(by_row[2:3, :1] * (2 * wide * 1.02 + 8.0), 1e-30)
         info_ref[...] = jnp.zeros_like(info_ref)
-        for n, value in enumerate((row_term, summed(both), query_bound, passage_bound)):
+        for n, value in enumerate((row_term, col_term, query_bound, passage_bound)):
             info_ref[n : n + 1, :] = jnp.broadcast_to(value, (1, rows))
 
     return call(

time: 60.9 us -> 60.9 us (level)
  no operation moved by 1% of the time
where the time goes in v4:
time: 60.9 us; the launch traced here: 60.7 us
  starting transfers between devices  25.9 us (43%)
  Pallas kernels  18 us (30%)
  waiting for transfers between devices  14.9 us (24%)
  local copies, waits for them, and re-layouts  0.94 us (2%)
  between operations  0.88 us (1%)
    ppermute x22, starting transfers between devices, exchange(): return lax.ppermute(value, axis, [(i, i ^ turn) for i in range(size)])  22.3 us
    pallas_call x31, Pallas kernels, call(): pl.pallas_call(kernel, out_shape=out_shape, in_specs=spaces, out_specs=ja...  18 us
    ppermute x22, waiting for transfers between devices, exchange(): return lax.ppermute(value, axis, [(i, i ^ turn) for i in range(size)])  11.9 us
    ppermute x3, starting transfers between devices, per_device(): others.append(lax.ppermute(stats, ('pb', 'pa'), pairs))  3.55 us
    ppermute x3, waiting for transfers between devices, per_device(): others.append(lax.ppermute(stats, ('pb', 'pa'), pairs))  3.05 us
  transfers between devices with their start and end apart: 25, of which 14 were waited for; matrix products, arithmetic and copies ran while one was open for 0% of the time, Pallas kernels for 19%

profile of v4, /device:TPU:0, one launch (start us, length us, event | category | flops | bytes accessed | tf_op | source)
XLA Modules:
  0.0 60.7 jit_solution(12865415575746616010)
XLA Ops:
  0.6 2.0 %shard_map.67 = (bf16[800,128]{1,0:T(8,128)(2,1)}, bf16[800,128]{1,0:T(8,128)(2,1)}, bf16[816,128]{1,0:T(8,128)(2,1)}) custom-call(f32[128,768]{1,0:T(8,128)} %refs_0_.1, s32[32,128]{1,0:T(8,128)} %bitcast.3, s32[1,128]{1,0:T(1,128)} %bitcast.4, f32[128,768]{1,0:T(8,128)} %refs_3_.1), custom_call_target="tpu_custom_call" | custom-call | flops 1 | bytes 7200000 | tf_op jit(solution)/shard_map/pallas_call | solution.py:32
  2.7 4.1 %collective-permute-start.3 = (bf16[816,128]{1,0:T(8,128)(2,1)}, bf16[816,128]{1,0:T(8,128)(2,1)S(1)}, u32[]{:S(2)}, u32[]{:S(2)}) collective-permute-start(bf16[816,128]{1,0:T(8,128)(2,1)} %get-tuple-element.37), channel_id=1, source_target_pairs={{0,16},{8,24},{16,0},{24,8},{1,17},{9,25},{17,1},{25,9},{2,18},{10... | collective-permute-start | bytes 626696 | tf_op jit(solution)/shard_map/ppermute | solution.py:23
  6.8 1.6 %collective-permute-start.2 = (bf16[800,128]{1,0:T(8,128)(2,1)}, bf16[800,128]{1,0:T(8,128)(2,1)S(1)}, u32[]{:S(2)}, u32[]{:S(2)}) collective-permute-start(bf16[800,128]{1,0:T(8,128)(2,1)} %get-tuple-element.36.refs_8_), channel_id=1, source_target_pairs={{0,8},{8,0},{16,24},{24,16},{1,9},{9,1},{17,25},{25,17},{2,10},{10... | collective-permute-start | bytes 614408 | tf_op jit(solution)/shard_map/ppermute | solution.py:23
  8.3 1.5 %collective-permute-start.1 = (bf16[800,128]{1,0:T(8,128)(2,1)}, bf16[800,128]{1,0:T(8,128)(2,1)S(1)}, u32[]{:S(2)}, u32[]{:S(2)}) collective-permute-start(bf16[800,128]{1,0:T(8,128)(2,1)} %get-tuple-element.35.m_ref.refs_0_), channel_id=1, source_target_pairs={{0,2},{1,3},{2,0},{3,1},{4,6},{5,7},{6,4},{7,5},{8,10},{9,11},{10,... | collective-permute-start | bytes 614408 | tf_op jit(solution)/shard_map/ppermute | solution.py:23
  9.8 1.5 %collective-permute-start.5 = (bf16[800,128]{1,0:T(8,128)(2,1)}, bf16[800,128]{1,0:T(8,128)(2,1)S(1)}, u32[]{:S(2)}, u32[]{:S(2)}) collective-permute-start(bf16[800,128]{1,0:T(8,128)(2,1)} %get-tuple-element.35.m_ref.refs_0_), channel_id=1, source_target_pairs={{0,4},{1,5},{2,6},{3,7},{4,0},{5,1},{6,2},{7,3},{8,12},{9,13},{10,... | collective-permute-start | bytes 614408 | tf_op jit(solution)/shard_map/ppermute | solution.py:23
  11.8 4.9 %collective-permute-done.3.refs_1_.refs_10_ = bf16[816,128]{1,0:T(8,128)(2,1)S(1)} collective-permute-done((bf16[816,128]{1,0:T(8,128)(2,1)}, bf16[816,128]{1,0:T(8,128)(2,1)S(1)}, u32[]{:S(2)}, u32[]{:S(2)}) %collective-permute-start.3) | collective-permute-done | bytes 208928 | tf_op jit(solution)/shard_map/ppermute | solution.py:23
  16.7 0.7 %collective-permute-start.9 = (bf16[816,128]{1,0:T(8,128)(2,1)S(1)}, bf16[816,128]{1,0:T(8,128)(2,1)S(1)}, u32[]{:S(2)}, u32[]{:S(2)}) collective-permute-start(bf16[816,128]{1,0:T(8,128)(2,1)S(1)} %collective-permute-done.3.refs_1_.refs_10_), channel_id=1, source_target_pairs={{0,8},{8,0},{16,24},{24,16},{1,9},{9,1},{17,25},{25,17},{2,10},{10... | collective-permute-start | bytes 626696 | tf_op jit(solution)/shard_map/ppermute | solution.py:23
  17.4 0.9 %copy-done = bf16[800,128]{1,0:T(8,128)(2,1)S(1)} copy-done((bf16[800,128]{1,0:T(8,128)(2,1)S(1)}, bf16[800,128]{1,0:T(8,128)(2,1)}, u32[]{:S(2)}) %copy-start) | copy-done | bytes 204824
  19.7 0.8 %collective-permute-done.5.m_ref = bf16[800,128]{1,0:T(8,128)(2,1)S(1)} collective-permute-done((bf16[800,128]{1,0:T(8,128)(2,1)}, bf16[800,128]{1,0:T(8,128)(2,1)S(1)}, u32[]{:S(2)}, u32[]{:S(2)}) %collective-permute-start.5) | collective-permute-done | bytes 204832 | tf_op jit(solution)/shard_map/ppermute | solution.py:23
  23.1 2.2 %shard_map.76 = (f32[512,1024]{1,0:T(8,128)S(1)}, f32[8,1536]{1,0:T(8,128)S(1)}, bf16[1024,768]{1,0:T(8,128)(2,1)S(1)}, bf16[512,768]{1,0:T(8,128)(2,1)S(1)}) custom-call(bf16[800,128]{1,0:T(8,128)(2,1)S(1)} %copy-done.1, bf16[800,128]{1,0:T(8,128)(2,1)S(1)} %collective-permute-done.m_ref.refs_1_, bf16[800,128]{1,0:T(8,128)(2,1)S(1)} %get-tuple-element.38.refs_2_, ...), custom_call_target="tpu_custom_call" | custom-call | flops 1 | bytes 7200000 | tf_op jit(solution)/shard_map/pallas_call | solution.py:32
  26.0 0.6 collective-permute-done.10.other_ref
  26.7 2.2 %collective-permute-start.13 = (f32[8,1024]{1,0:T(8,128)S(1)}, f32[8,1024]{1,0:T(8,128)S(1)}, u32[]{:S(2)}, u32[]{:S(2)}) collective-permute-start(f32[8,1024]{1,0:T(8,128)S(1)} %shard_map.78.own_ref), channel_id=1, source_target_pairs={{0,6},{1,25},{2,4},{3,27},{4,2},{5,29},{6,0},{7,31},{8,14},{9,17},... | collective-permute-start | bytes 98312 | tf_op jit(solution)/shard_map/ppermute | solution.py:547
  29.4 0.9 %collective-permute-start.11 = (f32[8,1024]{1,0:T(8,128)S(1)}, f32[8,1024]{1,0:T(8,128)S(1)}, u32[]{:S(2)}, u32[]{:S(2)}) collective-permute-start(f32[8,1024]{1,0:T(8,128)S(1)} %shard_map.78.own_ref), channel_id=1, source_target_pairs={{0,2},{1,9},{2,0},{3,11},{4,6},{5,13},{6,4},{7,15},{8,10},{9,1},{1... | collective-permute-start | bytes 98312 | tf_op jit(solution)/shard_map/ppermute | solution.py:547
  30.2 1.3 %collective-permute-done.13.refs_2_ = f32[8,1024]{1,0:T(8,128)S(1)} collective-permute-done((f32[8,1024]{1,0:T(8,128)S(1)}, f32[8,1024]{1,0:T(8,128)S(1)}, u32[]{:S(2)}, u32[]{:S(2)}) %collective-permute-start.13) | collective-permute-done | bytes 32800 | tf_op jit(solution)/shard_map/ppermute | solution.py:547
  31.6 1.2 %collective-permute-done.12.refs_1_ = f32[8,1024]{1,0:T(8,128)S(1)} collective-permute-done((f32[8,1024]{1,0:T(8,128)S(1)}, f32[8,1024]{1,0:T(8,128)S(1)}, u32[]{:S(2)}, u32[]{:S(2)}) %collective-permute-start.12) | collective-permute-done | bytes 32800 | tf_op jit(solution)/shard_map/ppermute | solution.py:547
  33.4 1.2 %collective-permute-start.14 = (f32[8,1024]{1,0:T(8,128)S(1)}, f32[8,1024]{1,0:T(8,128)S(1)}, u32[]{:S(2)}, u32[]{:S(2)}) collective-permute-start(f32[8,1024]{1,0:T(8,128)S(1)} %shard_map.79.own_ref), channel_id=1, source_target_pairs={{0,1},{1,0},{2,3},{3,2},{4,5},{5,4},{6,7},{7,6},{8,9},{9,8},{10,11... | collective-permute-start | bytes 98312 | tf_op jit(solution)/shard_map/ppermute | solution.py:23
  34.6 0.9 %collective-permute-done.14.other_ref = f32[8,1024]{1,0:T(8,128)S(1)} collective-permute-done((f32[8,1024]{1,0:T(8,128)S(1)}, f32[8,1024]{1,0:T(8,128)S(1)}, u32[]{:S(2)}, u32[]{:S(2)}) %collective-permute-start.14) | collective-permute-done | bytes 32800 | tf_op jit(solution)/shard_map/ppermute | solution.py:23
  36.0 0.7 %shard_map.87 = s16[784,128]{1,0:T(8,128)(2,1)S(1)} custom-call(bf16[1,128,1024]{2,1,0:T(8,128)(2,1)S(1)} %get-tuple-element.49.refs_0_.hi_ref, bf16[1,128,1024]{2,1,0:T(8,128)(2,1)S(1)} %get-tuple-element.50.refs_1_.lo_ref, bf16[1024,768]{1,0:T(8,128)(2,1)S(1)} %get-tuple-element.58.q_ref, f32[8,128]{1,0:T(8,128)S(1)} %get-tuple-element.53.refs_5_.info_ref), custom_call_target="tpu_custom_call" | custom-call | flops 1 | bytes 1440000 | tf_op jit(solution)/shard_map/pallas_call | solution.py:32
  36.7 1.0 %collective-permute-start.18 = (s16[784,128]{1,0:T(8,128)(2,1)S(1)}, s16[784,128]{1,0:T(8,128)(2,1)S(1)}, u32[]{:S(2)}, u32[]{:S(2)}) collective-permute-start(s16[784,128]{1,0:T(8,128)(2,1)S(1)} %shard_map.87), channel_id=1, source_target_pairs={{0,8},{8,0},{16,24},{24,16},{1,9},{9,1},{17,25},{25,17},{2,10},{10... | collective-permute-start | bytes 602120 | tf_op jit(solution)/shard_map/ppermute | solution.py:23
  37.7 1.0 %shard_map.82 = (bf16[3,128,1024]{2,1,0:T(8,128)(2,1)S(1)}, bf16[3,128,1024]{2,1,0:T(8,128)(2,1)S(1)}) custom-call(f32[512,1024]{1,0:T(8,128)S(1)} %get-tuple-element.44.s_ref, f32[8,1024]{1,0:T(8,128)S(1)} %get-tuple-element.47.row_ref, f32[512,128]{1,0:T(8,128)S(1)} %get-tuple-element.48.col_ref, s32[1,128,128]{2,1,0:T(8,128)S(1)} %shard_map.68.refs_2_.refs_12_.refs_0_, ...), custom_call_target="tpu_custom_call" | custom-call | flops 1 | bytes 4860000 | tf_op jit(solution)/shard_map/pallas_call | solution.py:32
  38.7 0.6 shard_map.84
  39.4 0.7 %shard_map.91 = s16[768,128]{1,0:T(8,128)(2,1)S(1)} custom-call(bf16[3,128,1024]{2,1,0:T(8,128)(2,1)S(1)} %get-tuple-element.51.refs_2_.hi_ref, bf16[3,128,1024]{2,1,0:T(8,128)(2,1)S(1)} %get-tuple-element.52.refs_3_.lo_ref, bf16[1024,768]{1,0:T(8,128)(2,1)S(1)} %get-tuple-element.58.q_ref, f32[8,128]{1,0:T(8,128)S(1)} %get-tuple-element.53.refs_5_.info_ref), custom_call_target="tpu_custom_call" | custom-call | flops 1 | bytes 1440000 | tf_op jit(solution)/shard_map/pallas_call | solution.py:32
  40.1 0.6 shard_map.90
  40.7 1.2 %collective-permute-start.22 = (s16[768,128]{1,0:T(8,128)(2,1)S(1)}, s16[768,128]{1,0:T(8,128)(2,1)S(1)}, u32[]{:S(2)}, u32[]{:S(2)}) collective-permute-start(s16[768,128]{1,0:T(8,128)(2,1)S(1)} %shard_map.91), channel_id=1, source_target_pairs={{0,8},{8,0},{16,24},{24,16},{1,9},{9,1},{17,25},{25,17},{2,10},{10... | collective-permute-start | bytes 589832 | tf_op jit(solution)/shard_map/ppermute | solution.py:23
  44.5 2.3 %collective-permute-start.24 = (s16[800,128]{1,0:T(8,128)(2,1)S(1)}, s16[800,128]{1,0:T(8,128)(2,1)S(1)}, u32[]{:S(2)}, u32[]{:S(2)}) collective-permute-start(s16[800,128]{1,0:T(8,128)(2,1)S(1)} %shard_map.94), channel_id=1, source_target_pairs={{0,16},{8,24},{16,0},{24,8},{1,17},{9,25},{17,1},{25,9},{2,18},{10... | collective-permute-start | bytes 614408 | tf_op jit(solution)/shard_map/ppermute | solution.py:23
  47.2 2.1 %collective-permute-start.17 = (s16[784,128]{1,0:T(8,128)(2,1)S(1)}, s16[784,128]{1,0:T(8,128)(2,1)S(1)}, u32[]{:S(2)}, u32[]{:S(2)}) collective-permute-start(s16[784,128]{1,0:T(8,128)(2,1)S(1)} %shard_map.85), channel_id=1, source_target_pairs={{0,6},{1,7},{2,4},{3,5},{4,2},{5,3},{6,0},{7,1},{8,14},{9,15},{10,... | collective-permute-start | bytes 602120 | tf_op jit(solution)/shard_map/ppermute | solution.py:23
  49.4 1.5 %collective-permute-done.22.refs_0_ = s16[768,128]{1,0:T(8,128)(2,1)S(1)} collective-permute-done((s16[768,128]{1,0:T(8,128)(2,1)S(1)}, s16[768,128]{1,0:T(8,128)(2,1)S(1)}, u32[]{:S(2)}, u32[]{:S(2)}) %collective-permute-start.22) | collective-permute-done | bytes 196640 | tf_op jit(solution)/shard_map/ppermute | solution.py:23
  51.3 1.6 %collective-permute-start.23 = (s16[784,128]{1,0:T(8,128)(2,1)S(1)}, s16[784,128]{1,0:T(8,128)(2,1)S(1)}, u32[]{:S(2)}, u32[]{:S(2)}) collective-permute-start(s16[784,128]{1,0:T(8,128)(2,1)S(1)} %shard_map.92), channel_id=1, source_target_pairs={{0,4},{1,5},{2,6},{3,7},{4,0},{5,1},{6,2},{7,3},{8,12},{9,13},{10,... | collective-permute-start | bytes 602120 | tf_op jit(solution)/shard_map/ppermute | solution.py:23
  55.2 0.8 %collective-permute-done.15.refs_0_ = s16[768,128]{1,0:T(8,128)(2,1)S(1)} collective-permute-done((s16[768,128]{1,0:T(8,128)(2,1)S(1)}, s16[768,128]{1,0:T(8,128)(2,1)S(1)}, u32[]{:S(2)}, u32[]{:S(2)}) %collective-permute-start.15) | collective-permute-done | bytes 196640 | tf_op jit(solution)/shard_map/ppermute | solution.py:23
  56.7 1.2 %shard_map.96 = (f32[128,768]{1,0:T(8,128)}, f32[8,128]{1,0:T(8,128)S(1)}) custom-call(f32[768,128]{1,0:T(8,128)S(1)} %shard_map.95.own_ref, f32[8,128]{1,0:T(8,128)S(1)} %get-tuple-element.53.refs_5_.info_ref, s16[768,128]{1,0:T(8,128)(2,1)S(1)} %collective-permute-done.22.refs_0_, s16[800,128]{1,0:T(8,128)(2,1)S(1)} %collective-permute-done.24.refs_1_.refs_3_, ...), custom_call_target="tpu_custom_call" | custom-call | flops 1 | bytes 3600000 | tf_op jit(solution)/shard_map/pallas_call | solution.py:32
  57.9 1.6 %collective-permute-done.23.refs_1_ = s16[784,128]{1,0:T(8,128)(2,1)S(1)} collective-permute-done((s16[784,128]{1,0:T(8,128)(2,1)S(1)}, s16[784,128]{1,0:T(8,128)(2,1)S(1)}, u32[]{:S(2)}, u32[]{:S(2)}) %collective-permute-start.23) | collective-permute-done | bytes 200736 | tf_op jit(solution)/shard_map/ppermute | solution.py:23
  59.6 1.1 %shard_map.97 = (f32[1,1]{1,0:T(1,128)}, f32[128,768]{1,0:T(8,128)}) custom-call(f32[768,128]{1,0:T(8,128)S(1)} %shard_map.86.refs_2_.own_ref, f32[8,128]{1,0:T(8,128)S(1)} %get-tuple-element.53.refs_5_.info_ref, s16[784,128]{1,0:T(8,128)(2,1)S(1)} %collective-permute-done.18.arrived_ref.term_ref, s16[784,128]{1,0:T(8,128)(2,1)S(1)} %collective-permute-done.20.refs_0_, ...), custom_call_target="tpu_custom_call" | custom-call | flops 1 | bytes 3600000 | tf_op jit(solution)/shard_map/pallas_call | solution.py:32
  (55 shorter events, 13.2 us)
Async XLA Ops:
  2.7 14.1 %collective-permute-start.3 = (bf16[816,128]{1,0:T(8,128)(2,1)}, bf16[816,128]{1,0:T(8,128)(2,1)S(1)}, u32[]{:S(2)}, u32[]{:S(2)}) collective-permute-start(bf16[816,128]{1,0:T(8,128)(2,1)} %get-tuple-element.37), channel_id=1, source_target_pairs={{0,16},{8,24},{16,0},{24,8},{1,17},{9,25},{17,1},{25,9},{2,18},{10... | collective-permute-start | bytes 626696 | tf_op jit(solution)/shard_map/ppermute | solution.py:23
  6.8 11.9 %collective-permute-start.2 = (bf16[800,128]{1,0:T(8,128)(2,1)}, bf16[800,128]{1,0:T(8,128)(2,1)S(1)}, u32[]{:S(2)}, u32[]{:S(2)}) collective-permute-start(bf16[800,128]{1,0:T(8,128)(2,1)} %get-tuple-element.36.refs_8_), channel_id=1, source_target_pairs={{0,8},{8,0},{16,24},{24,16},{1,9},{9,1},{17,25},{25,17},{2,10},{10... | collective-permute-start | bytes 614408 | tf_op jit(solution)/shard_map/ppermute | solution.py:23
  8.3 10.4 %collective-permute-start.1 = (bf16[800,128]{1,0:T(8,128)(2,1)}, bf16[800,128]{1,0:T(8,128)(2,1)S(1)}, u32[]{:S(2)}, u32[]{:S(2)}) collective-permute-start(bf16[800,128]{1,0:T(8,128)(2,1)} %get-tuple-element.35.m_ref.refs_0_), channel_id=1, source_target_pairs={{0,2},{1,3},{2,0},{3,1},{4,6},{5,7},{6,4},{7,5},{8,10},{9,11},{10,... | collective-permute-start | bytes 614408 | tf_op jit(solution)/shard_map/ppermute | solution.py:23
  9.8 10.6 %collective-permute-start.5 = (bf16[800,128]{1,0:T(8,128)(2,1)}, bf16[800,128]{1,0:T(8,128)(2,1)S(1)}, u32[]{:S(2)}, u32[]{:S(2)}) collective-permute-start(bf16[800,128]{1,0:T(8,128)(2,1)} %get-tuple-element.35.m_ref.refs_0_), channel_id=1, source_target_pairs={{0,4},{1,5},{2,6},{3,7},{4,0},{5,1},{6,2},{7,3},{8,12},{9,13},{10,... | collective-permute-start | bytes 614408 | tf_op jit(solution)/shard_map/ppermute | solution.py:23
  11.4 9.5 %collective-permute-start.7 = (bf16[800,128]{1,0:T(8,128)(2,1)}, bf16[800,128]{1,0:T(8,128)(2,1)S(1)}, u32[]{:S(2)}, u32[]{:S(2)}) collective-permute-start(bf16[800,128]{1,0:T(8,128)(2,1)} %get-tuple-element.35.m_ref.refs_0_), channel_id=1, source_target_pairs={{0,6},{1,7},{2,4},{3,5},{4,2},{5,3},{6,0},{7,1},{8,14},{9,15},{10,... | collective-permute-start | bytes 614408 | tf_op jit(solution)/shard_map/ppermute | solution.py:23
  16.7 6.3 %collective-permute-start.9 = (bf16[816,128]{1,0:T(8,128)(2,1)S(1)}, bf16[816,128]{1,0:T(8,128)(2,1)S(1)}, u32[]{:S(2)}, u32[]{:S(2)}) collective-permute-start(bf16[816,128]{1,0:T(8,128)(2,1)S(1)} %collective-permute-done.3.refs_1_.refs_10_), channel_id=1, source_target_pairs={{0,8},{8,0},{16,24},{24,16},{1,9},{9,1},{17,25},{25,17},{2,10},{10... | collective-permute-start | bytes 626696 | tf_op jit(solution)/shard_map/ppermute | solution.py:23
  17.4 0.9 %copy-start = (bf16[800,128]{1,0:T(8,128)(2,1)S(1)}, bf16[800,128]{1,0:T(8,128)(2,1)}, u32[]{:S(2)}) copy-start(bf16[800,128]{1,0:T(8,128)(2,1)} %get-tuple-element.35.m_ref.refs_0_) | copy-start | bytes 614404
  18.4 4.7 %copy-start.1 = (bf16[800,128]{1,0:T(8,128)(2,1)S(1)}, bf16[800,128]{1,0:T(8,128)(2,1)}, u32[]{:S(2)}) copy-start(bf16[800,128]{1,0:T(8,128)(2,1)} %get-tuple-element.35.m_ref.refs_0_) | copy-start | bytes 614404
  18.4 4.7 %copy-start.2 = (bf16[800,128]{1,0:T(8,128)(2,1)S(1)}, bf16[800,128]{1,0:T(8,128)(2,1)}, u32[]{:S(2)}) copy-start(bf16[800,128]{1,0:T(8,128)(2,1)} %get-tuple-element.36.refs_8_) | copy-start | bytes 614404
  18.7 3.0 %collective-permute-start = (bf16[800,128]{1,0:T(8,128)(2,1)S(1)}, bf16[800,128]{1,0:T(8,128)(2,1)S(1)}, u32[]{:S(2)}, u32[]{:S(2)}) collective-permute-start(bf16[800,128]{1,0:T(8,128)(2,1)S(1)} %copy-done), channel_id=1, source_target_pairs={{0,1},{1,0},{2,3},{3,2},{4,5},{5,4},{6,7},{7,6},{8,9},{9,8},{10,11... | collective-permute-start | bytes 614408 | tf_op jit(solution)/shard_map/ppermute | solution.py:23
  19.1 2.9 %collective-permute-start.4 = (bf16[800,128]{1,0:T(8,128)(2,1)S(1)}, bf16[800,128]{1,0:T(8,128)(2,1)S(1)}, u32[]{:S(2)}, u32[]{:S(2)}) collective-permute-start(bf16[800,128]{1,0:T(8,128)(2,1)S(1)} %get-tuple-element.38.refs_2_), channel_id=1, source_target_pairs={{0,1},{1,0},{2,3},{3,2},{4,5},{5,4},{6,7},{7,6},{8,9},{9,8},{10,11... | collective-permute-start | bytes 614408 | tf_op jit(solution)/shard_map/ppermute | solution.py:23
  20.7 1.6 %collective-permute-start.6 = (bf16[800,128]{1,0:T(8,128)(2,1)S(1)}, bf16[800,128]{1,0:T(8,128)(2,1)S(1)}, u32[]{:S(2)}, u32[]{:S(2)}) collective-permute-start(bf16[800,128]{1,0:T(8,128)(2,1)S(1)} %get-tuple-element.39.refs_4_), channel_id=1, source_target_pairs={{0,1},{1,0},{2,3},{3,2},{4,5},{5,4},{6,7},{7,6},{8,9},{9,8},{10,11... | collective-permute-start | bytes 614408 | tf_op jit(solution)/shard_map/ppermute | solution.py:23
  21.1 1.6 %collective-permute-start.8 = (bf16[800,128]{1,0:T(8,128)(2,1)S(1)}, bf16[800,128]{1,0:T(8,128)(2,1)S(1)}, u32[]{:S(2)}, u32[]{:S(2)}) collective-permute-start(bf16[800,128]{1,0:T(8,128)(2,1)S(1)} %get-tuple-element.40.refs_6_), channel_id=1, source_target_pairs={{0,1},{1,0},{2,3},{3,2},{4,5},{5,4},{6,7},{7,6},{8,9},{9,8},{10,11... | collective-permute-start | bytes 614408 | tf_op jit(solution)/shard_map/ppermute | solution.py:23
  25.3 1.3 %collective-permute-start.10 = (f32[8,1536]{1,0:T(8,128)S(1)}, f32[8,1536]{1,0:T(8,128)S(1)}, u32[]{:S(2)}, u32[]{:S(2)}) collective-permute-start(f32[8,1536]{1,0:T(8,128)S(1)} %get-tuple-element.45.own_ref), channel_id=1, source_target_pairs={{0,1},{1,0},{2,3},{3,2},{4,5},{5,4},{6,7},{7,6},{8,9},{9,8},{10,11... | collective-permute-start | bytes 147464 | tf_op jit(solution)/shard_map/ppermute | solution.py:23
  26.7 4.9 %collective-permute-start.13 = (f32[8,1024]{1,0:T(8,128)S(1)}, f32[8,1024]{1,0:T(8,128)S(1)}, u32[]{:S(2)}, u32[]{:S(2)}) collective-permute-start(f32[8,1024]{1,0:T(8,128)S(1)} %shard_map.78.own_ref), channel_id=1, source_target_pairs={{0,6},{1,25},{2,4},{3,27},{4,2},{5,29},{6,0},{7,31},{8,14},{9,17},... | collective-permute-start | bytes 98312 | tf_op jit(solution)/shard_map/ppermute | solution.py:547
  28.9 3.9 %collective-permute-start.12 = (f32[8,1024]{1,0:T(8,128)S(1)}, f32[8,1024]{1,0:T(8,128)S(1)}, u32[]{:S(2)}, u32[]{:S(2)}) collective-permute-start(f32[8,1024]{1,0:T(8,128)S(1)} %shard_map.78.own_ref), channel_id=1, source_target_pairs={{0,4},{1,17},{2,6},{3,19},{4,0},{5,21},{6,2},{7,23},{8,12},{9,25},... | collective-permute-start | bytes 98312 | tf_op jit(solution)/shard_map/ppermute | solution.py:547
  29.4 3.9 %collective-permute-start.11 = (f32[8,1024]{1,0:T(8,128)S(1)}, f32[8,1024]{1,0:T(8,128)S(1)}, u32[]{:S(2)}, u32[]{:S(2)}) collective-permute-start(f32[8,1024]{1,0:T(8,128)S(1)} %shard_map.78.own_ref), channel_id=1, source_target_pairs={{0,2},{1,9},{2,0},{3,11},{4,6},{5,13},{6,4},{7,15},{8,10},{9,1},{1... | collective-permute-start | bytes 98312 | tf_op jit(solution)/shard_map/ppermute | solution.py:547
  33.4 2.1 %collective-permute-start.14 = (f32[8,1024]{1,0:T(8,128)S(1)}, f32[8,1024]{1,0:T(8,128)S(1)}, u32[]{:S(2)}, u32[]{:S(2)}) collective-permute-start(f32[8,1024]{1,0:T(8,128)S(1)} %shard_map.79.own_ref), channel_id=1, source_target_pairs={{0,1},{1,0},{2,3},{3,2},{4,5},{5,4},{6,7},{7,6},{8,9},{9,8},{10,11... | collective-permute-start | bytes 98312 | tf_op jit(solution)/shard_map/ppermute | solution.py:23
  36.7 7.3 %collective-permute-start.18 = (s16[784,128]{1,0:T(8,128)(2,1)S(1)}, s16[784,128]{1,0:T(8,128)(2,1)S(1)}, u32[]{:S(2)}, u32[]{:S(2)}) collective-permute-start(s16[784,128]{1,0:T(8,128)(2,1)S(1)} %shard_map.87), channel_id=1, source_target_pairs={{0,8},{8,0},{16,24},{24,16},{1,9},{9,1},{17,25},{25,17},{2,10},{10... | collective-permute-start | bytes 602120 | tf_op jit(solution)/shard_map/ppermute | solution.py:23
  39.4 7.5 %collective-permute-start.16 = (s16[768,128]{1,0:T(8,128)(2,1)S(1)}, s16[768,128]{1,0:T(8,128)(2,1)S(1)}, u32[]{:S(2)}, u32[]{:S(2)}) collective-permute-start(s16[768,128]{1,0:T(8,128)(2,1)S(1)} %get-tuple-element.57), channel_id=1, source_target_pairs={{0,1},{1,0},{2,3},{3,2},{4,5},{5,4},{6,7},{7,6},{8,9},{9,8},{10,11... | collective-permute-start | bytes 589832 | tf_op jit(solution)/shard_map/ppermute | solution.py:23
  40.7 10.2 %collective-permute-start.22 = (s16[768,128]{1,0:T(8,128)(2,1)S(1)}, s16[768,128]{1,0:T(8,128)(2,1)S(1)}, u32[]{:S(2)}, u32[]{:S(2)}) collective-permute-start(s16[768,128]{1,0:T(8,128)(2,1)S(1)} %shard_map.91), channel_id=1, source_target_pairs={{0,8},{8,0},{16,24},{24,16},{1,9},{9,1},{17,25},{25,17},{2,10},{10... | collective-permute-start | bytes 589832 | tf_op jit(solution)/shard_map/ppermute | solution.py:23
  41.9 9.0 %collective-permute-start.21 = (s16[768,128]{1,0:T(8,128)(2,1)S(1)}, s16[768,128]{1,0:T(8,128)(2,1)S(1)}, u32[]{:S(2)}, u32[]{:S(2)}) collective-permute-start(s16[768,128]{1,0:T(8,128)(2,1)S(1)} %get-tuple-element.62), channel_id=1, source_target_pairs={{0,1},{1,0},{2,3},{3,2},{4,5},{5,4},{6,7},{7,6},{8,9},{9,8},{10,11... | collective-permute-start | bytes 589832 | tf_op jit(solution)/shard_map/ppermute | solution.py:23
  42.7 10.2 %collective-permute-start.19 = (s16[768,128]{1,0:T(8,128)(2,1)S(1)}, s16[768,128]{1,0:T(8,128)(2,1)S(1)}, u32[]{:S(2)}, u32[]{:S(2)}) collective-permute-start(s16[768,128]{1,0:T(8,128)(2,1)S(1)} %get-tuple-element.60), channel_id=1, source_target_pairs={{0,1},{1,0},{2,3},{3,2},{4,5},{5,4},{6,7},{7,6},{8,9},{9,8},{10,11... | collective-permute-start | bytes 589832 | tf_op jit(solution)/shard_map/ppermute | solution.py:23
  44.5 12.3 %collective-permute-start.24 = (s16[800,128]{1,0:T(8,128)(2,1)S(1)}, s16[800,128]{1,0:T(8,128)(2,1)S(1)}, u32[]{:S(2)}, u32[]{:S(2)}) collective-permute-start(s16[800,128]{1,0:T(8,128)(2,1)S(1)} %shard_map.94), channel_id=1, source_target_pairs={{0,16},{8,24},{16,0},{24,8},{1,17},{9,25},{17,1},{25,9},{2,18},{10... | collective-permute-start | bytes 614408 | tf_op jit(solution)/shard_map/ppermute | solution.py:23
  47.2 9.1 %collective-permute-start.17 = (s16[784,128]{1,0:T(8,128)(2,1)S(1)}, s16[784,128]{1,0:T(8,128)(2,1)S(1)}, u32[]{:S(2)}, u32[]{:S(2)}) collective-permute-start(s16[784,128]{1,0:T(8,128)(2,1)S(1)} %shard_map.85), channel_id=1, source_target_pairs={{0,6},{1,7},{2,4},{3,5},{4,2},{5,3},{6,0},{7,1},{8,14},{9,15},{10,... | collective-permute-start | bytes 602120 | tf_op jit(solution)/shard_map/ppermute | solution.py:23
  51.3 8.2 %collective-permute-start.23 = (s16[784,128]{1,0:T(8,128)(2,1)S(1)}, s16[784,128]{1,0:T(8,128)(2,1)S(1)}, u32[]{:S(2)}, u32[]{:S(2)}) collective-permute-start(s16[784,128]{1,0:T(8,128)(2,1)S(1)} %shard_map.92), channel_id=1, source_target_pairs={{0,4},{1,5},{2,6},{3,7},{4,0},{5,1},{6,2},{7,3},{8,12},{9,13},{10,... | collective-permute-start | bytes 602120 | tf_op jit(solution)/shard_map/ppermute | solution.py:23
  53.3 6.3 %collective-permute-start.20 = (s16[784,128]{1,0:T(8,128)(2,1)S(1)}, s16[784,128]{1,0:T(8,128)(2,1)S(1)}, u32[]{:S(2)}, u32[]{:S(2)}) collective-permute-start(s16[784,128]{1,0:T(8,128)(2,1)S(1)} %shard_map.89), channel_id=1, source_target_pairs={{0,2},{1,3},{2,0},{3,1},{4,6},{5,7},{6,4},{7,5},{8,10},{9,11},{10,... | collective-permute-start | bytes 602120 | tf_op jit(solution)/shard_map/ppermute | solution.py:23
  54.5 1.5 %collective-permute-start.15 = (s16[768,128]{1,0:T(8,128)(2,1)S(1)}, s16[768,128]{1,0:T(8,128)(2,1)S(1)}, u32[]{:S(2)}, u32[]{:S(2)}) collective-permute-start(s16[768,128]{1,0:T(8,128)(2,1)S(1)} %get-tuple-element.55), channel_id=1, source_target_pairs={{0,1},{1,0},{2,3},{3,2},{4,5},{5,4},{6,7},{7,6},{8,9},{9,8},{10,11... | collective-permute-start | bytes 589832 | tf_op jit(solution)/shard_map/ppermute | solution.py:23

commit v5 on v4

--- a/solution.py
+++ b/solution.py
@@ -557,10 +557,6 @@
     second = weight_sweep(staying, *swept)
     weights = [*first, *second]
     blocks = passage_sweep(staying[:-2], staying, second, q_all, info)
-    along = [
-        exchange(send_on(own, near, info, 2, 0, part, 16), "pb", 2 * (part + 1))
-        for part, own in enumerate(blocks)
-    ]
     (last,) = passage_sweep([1], staying, second, q_all, info)
     last = exchange(last, "pb", 1)
     (passage_sum,) = passage_sweep([0], staying, second, q_all, info)
@@ -571,9 +567,14 @@
         other = exchange(other, "pa", 1)
         if m:
             after = [last] if m == 2 else []
-            side.append(exchange(send_on(own, other, info, 3, 1, after=after), "pa", 2 * m))
+            message = send_on(own, other, info, 3, 1, after=after)
+            side.append(exchange(message, "pa", 2 * m))
         else:
             query_sum, core = own, other
+    along = [
+        exchange(send_on(own, near, info, 2, 0, part, 16, [message]), "pb", 2 * (part + 1))
+        for part, own in enumerate(blocks)
+    ]
     query_sum = added(query_sum, [(core, 0), (side[-1], 0)], info, 3)
     grad_passages, after = finish_passages(
         passage_sum, [last, *along], info, width, [query_sum]

time: 60.9 us -> 60.6 us (level)
  transfers between devices with their start and end apart: 25 -> 25, of which waited for: 14 -> 13; matrix products, arithmetic and copies ran while one was open for 0% -> 0% of each run, Pallas kernels for 19% -> 19%
where the time goes in v5:
time: 60.6 us; the launch traced here: 60.5 us
  starting transfers between devices  25.9 us (43%)
  Pallas kernels  18 us (30%)
  waiting for transfers between devices  14.6 us (24%)
  local copies, waits for them, and re-layouts  0.94 us (2%)
  between operations  0.9 us (1%)
    ppermute x22, starting transfers between devices, exchange(): return lax.ppermute(value, axis, [(i, i ^ turn) for i in range(size)])  22.4 us
    pallas_call x31, Pallas kernels, call(): pl.pallas_call(kernel, out_shape=out_shape, in_specs=spaces, out_specs=ja...  18 us
    ppermute x22, waiting for transfers between devices, exchange(): return lax.ppermute(value, axis, [(i, i ^ turn) for i in range(size)])  11.6 us
    ppermute x3, starting transfers between devices, per_device(): others.append(lax.ppermute(stats, ('pb', 'pa'), pairs))  3.55 us
    ppermute x3, waiting for transfers between devices, per_device(): others.append(lax.ppermute(stats, ('pb', 'pa'), pairs))  3.05 us
  transfers between devices with their start and end apart: 25, of which 13 were waited for; matrix products, arithmetic and copies ran while one was open for 0% of the time, Pallas kernels for 19%

profile of v5, /device:TPU:0, one launch (start us, length us, event | category | flops | bytes accessed | tf_op | source)
XLA Modules:
  0.0 60.5 jit_solution(3851966883047299654)
XLA Ops:
  0.6 2.0 %shard_map.67 = (bf16[800,128]{1,0:T(8,128)(2,1)}, bf16[800,128]{1,0:T(8,128)(2,1)}, bf16[816,128]{1,0:T(8,128)(2,1)}) custom-call(f32[128,768]{1,0:T(8,128)} %refs_0_.1, s32[32,128]{1,0:T(8,128)} %bitcast.3, s32[1,128]{1,0:T(1,128)} %bitcast.4, f32[128,768]{1,0:T(8,128)} %refs_3_.1), custom_call_target="tpu_custom_call" | custom-call | flops 1 | bytes 7200000 | tf_op jit(solution)/shard_map/pallas_call | solution.py:32
  2.7 4.1 %collective-permute-start.3 = (bf16[816,128]{1,0:T(8,128)(2,1)}, bf16[816,128]{1,0:T(8,128)(2,1)S(1)}, u32[]{:S(2)}, u32[]{:S(2)}) collective-permute-start(bf16[816,128]{1,0:T(8,128)(2,1)} %get-tuple-element.37), channel_id=1, source_target_pairs={{0,16},{8,24},{16,0},{24,8},{1,17},{9,25},{17,1},{25,9},{2,18},{10... | collective-permute-start | bytes 626696 | tf_op jit(solution)/shard_map/ppermute | solution.py:23
  6.8 1.6 %collective-permute-start.2 = (bf16[800,128]{1,0:T(8,128)(2,1)}, bf16[800,128]{1,0:T(8,128)(2,1)S(1)}, u32[]{:S(2)}, u32[]{:S(2)}) collective-permute-start(bf16[800,128]{1,0:T(8,128)(2,1)} %get-tuple-element.36.refs_8_), channel_id=1, source_target_pairs={{0,8},{8,0},{16,24},{24,16},{1,9},{9,1},{17,25},{25,17},{2,10},{10... | collective-permute-start | bytes 614408 | tf_op jit(solution)/shard_map/ppermute | solution.py:23
  8.3 1.5 %collective-permute-start.1 = (bf16[800,128]{1,0:T(8,128)(2,1)}, bf16[800,128]{1,0:T(8,128)(2,1)S(1)}, u32[]{:S(2)}, u32[]{:S(2)}) collective-permute-start(bf16[800,128]{1,0:T(8,128)(2,1)} %get-tuple-element.35.m_ref.refs_0_), channel_id=1, source_target_pairs={{0,2},{1,3},{2,0},{3,1},{4,6},{5,7},{6,4},{7,5},{8,10},{9,11},{10,... | collective-permute-start | bytes 614408 | tf_op jit(solution)/shard_map/ppermute | solution.py:23
  9.8 1.5 %collective-permute-start.5 = (bf16[800,128]{1,0:T(8,128)(2,1)}, bf16[800,128]{1,0:T(8,128)(2,1)S(1)}, u32[]{:S(2)}, u32[]{:S(2)}) collective-permute-start(bf16[800,128]{1,0:T(8,128)(2,1)} %get-tuple-element.35.m_ref.refs_0_), channel_id=1, source_target_pairs={{0,4},{1,5},{2,6},{3,7},{4,0},{5,1},{6,2},{7,3},{8,12},{9,13},{10,... | collective-permute-start | bytes 614408 | tf_op jit(solution)/shard_map/ppermute | solution.py:23
  11.8 4.9 %collective-permute-done.3.refs_1_.refs_10_ = bf16[816,128]{1,0:T(8,128)(2,1)S(1)} collective-permute-done((bf16[816,128]{1,0:T(8,128)(2,1)}, bf16[816,128]{1,0:T(8,128)(2,1)S(1)}, u32[]{:S(2)}, u32[]{:S(2)}) %collective-permute-start.3) | collective-permute-done | bytes 208928 | tf_op jit(solution)/shard_map/ppermute | solution.py:23
  16.7 0.7 %collective-permute-start.9 = (bf16[816,128]{1,0:T(8,128)(2,1)S(1)}, bf16[816,128]{1,0:T(8,128)(2,1)S(1)}, u32[]{:S(2)}, u32[]{:S(2)}) collective-permute-start(bf16[816,128]{1,0:T(8,128)(2,1)S(1)} %collective-permute-done.3.refs_1_.refs_10_), channel_id=1, source_target_pairs={{0,8},{8,0},{16,24},{24,16},{1,9},{9,1},{17,25},{25,17},{2,10},{10... | collective-permute-start | bytes 626696 | tf_op jit(solution)/shard_map/ppermute | solution.py:23
  17.4 0.9 %copy-done = bf16[800,128]{1,0:T(8,128)(2,1)S(1)} copy-done((bf16[800,128]{1,0:T(8,128)(2,1)S(1)}, bf16[800,128]{1,0:T(8,128)(2,1)}, u32[]{:S(2)}) %copy-start) | copy-done | bytes 204824
  19.7 0.8 %collective-permute-done.5.m_ref = bf16[800,128]{1,0:T(8,128)(2,1)S(1)} collective-permute-done((bf16[800,128]{1,0:T(8,128)(2,1)}, bf16[800,128]{1,0:T(8,128)(2,1)S(1)}, u32[]{:S(2)}, u32[]{:S(2)}) %collective-permute-start.5) | collective-permute-done | bytes 204832 | tf_op jit(solution)/shard_map/ppermute | solution.py:23
  23.1 2.2 %shard_map.76 = (f32[512,1024]{1,0:T(8,128)S(1)}, f32[8,1536]{1,0:T(8,128)S(1)}, bf16[1024,768]{1,0:T(8,128)(2,1)S(1)}, bf16[512,768]{1,0:T(8,128)(2,1)S(1)}) custom-call(bf16[800,128]{1,0:T(8,128)(2,1)S(1)} %copy-done.1, bf16[800,128]{1,0:T(8,128)(2,1)S(1)} %collective-permute-done.m_ref.refs_1_, bf16[800,128]{1,0:T(8,128)(2,1)S(1)} %get-tuple-element.38.refs_2_, ...), custom_call_target="tpu_custom_call" | custom-call | flops 1 | bytes 7200000 | tf_op jit(solution)/shard_map/pallas_call | solution.py:32
  26.0 0.6 collective-permute-done.10.other_ref
  26.7 2.2 %collective-permute-start.13 = (f32[8,1024]{1,0:T(8,128)S(1)}, f32[8,1024]{1,0:T(8,128)S(1)}, u32[]{:S(2)}, u32[]{:S(2)}) collective-permute-start(f32[8,1024]{1,0:T(8,128)S(1)} %shard_map.78.own_ref), channel_id=1, source_target_pairs={{0,6},{1,25},{2,4},{3,27},{4,2},{5,29},{6,0},{7,31},{8,14},{9,17},... | collective-permute-start | bytes 98312 | tf_op jit(solution)/shard_map/ppermute | solution.py:547
  29.4 0.9 %collective-permute-start.11 = (f32[8,1024]{1,0:T(8,128)S(1)}, f32[8,1024]{1,0:T(8,128)S(1)}, u32[]{:S(2)}, u32[]{:S(2)}) collective-permute-start(f32[8,1024]{1,0:T(8,128)S(1)} %shard_map.78.own_ref), channel_id=1, source_target_pairs={{0,2},{1,9},{2,0},{3,11},{4,6},{5,13},{6,4},{7,15},{8,10},{9,1},{1... | collective-permute-start | bytes 98312 | tf_op jit(solution)/shard_map/ppermute | solution.py:547
  30.2 1.3 %collective-permute-done.13.refs_2_ = f32[8,1024]{1,0:T(8,128)S(1)} collective-permute-done((f32[8,1024]{1,0:T(8,128)S(1)}, f32[8,1024]{1,0:T(8,128)S(1)}, u32[]{:S(2)}, u32[]{:S(2)}) %collective-permute-start.13) | collective-permute-done | bytes 32800 | tf_op jit(solution)/shard_map/ppermute | solution.py:547
  31.6 1.2 %collective-permute-done.12.refs_1_ = f32[8,1024]{1,0:T(8,128)S(1)} collective-permute-done((f32[8,1024]{1,0:T(8,128)S(1)}, f32[8,1024]{1,0:T(8,128)S(1)}, u32[]{:S(2)}, u32[]{:S(2)}) %collective-permute-start.12) | collective-permute-done | bytes 32800 | tf_op jit(solution)/shard_map/ppermute | solution.py:547
  33.4 1.2 %collective-permute-start.14 = (f32[8,1024]{1,0:T(8,128)S(1)}, f32[8,1024]{1,0:T(8,128)S(1)}, u32[]{:S(2)}, u32[]{:S(2)}) collective-permute-start(f32[8,1024]{1,0:T(8,128)S(1)} %shard_map.79.own_ref), channel_id=1, source_target_pairs={{0,1},{1,0},{2,3},{3,2},{4,5},{5,4},{6,7},{7,6},{8,9},{9,8},{10,11... | collective-permute-start | bytes 98312 | tf_op jit(solution)/shard_map/ppermute | solution.py:23
  34.6 0.9 %collective-permute-done.14.other_ref = f32[8,1024]{1,0:T(8,128)S(1)} collective-permute-done((f32[8,1024]{1,0:T(8,128)S(1)}, f32[8,1024]{1,0:T(8,128)S(1)}, u32[]{:S(2)}, u32[]{:S(2)}) %collective-permute-start.14) | collective-permute-done | bytes 32800 | tf_op jit(solution)/shard_map/ppermute | solution.py:23
  36.0 0.7 %shard_map.87 = s16[784,128]{1,0:T(8,128)(2,1)S(1)} custom-call(bf16[1,128,1024]{2,1,0:T(8,128)(2,1)S(1)} %get-tuple-element.49.refs_0_.hi_ref, bf16[1,128,1024]{2,1,0:T(8,128)(2,1)S(1)} %get-tuple-element.50.refs_1_.lo_ref, bf16[1024,768]{1,0:T(8,128)(2,1)S(1)} %get-tuple-element.58.q_ref, f32[8,128]{1,0:T(8,128)S(1)} %get-tuple-element.53.refs_5_.info_ref), custom_call_target="tpu_custom_call" | custom-call | flops 1 | bytes 1440000 | tf_op jit(solution)/shard_map/pallas_call | solution.py:32
  36.7 1.0 %collective-permute-start.18 = (s16[784,128]{1,0:T(8,128)(2,1)S(1)}, s16[784,128]{1,0:T(8,128)(2,1)S(1)}, u32[]{:S(2)}, u32[]{:S(2)}) collective-permute-start(s16[784,128]{1,0:T(8,128)(2,1)S(1)} %shard_map.87), channel_id=1, source_target_pairs={{0,8},{8,0},{16,24},{24,16},{1,9},{9,1},{17,25},{25,17},{2,10},{10... | collective-permute-start | bytes 602120 | tf_op jit(solution)/shard_map/ppermute | solution.py:23
  37.7 1.0 %shard_map.82 = (bf16[3,128,1024]{2,1,0:T(8,128)(2,1)S(1)}, bf16[3,128,1024]{2,1,0:T(8,128)(2,1)S(1)}) custom-call(f32[512,1024]{1,0:T(8,128)S(1)} %get-tuple-element.44.s_ref, f32[8,1024]{1,0:T(8,128)S(1)} %get-tuple-element.47.row_ref, f32[512,128]{1,0:T(8,128)S(1)} %get-tuple-element.48.col_ref, s32[1,128,128]{2,1,0:T(8,128)S(1)} %shard_map.68.refs_2_.refs_12_.refs_0_, ...), custom_call_target="tpu_custom_call" | custom-call | flops 1 | bytes 4860000 | tf_op jit(solution)/shard_map/pallas_call | solution.py:32
  39.4 0.7 %shard_map.91 = s16[768,128]{1,0:T(8,128)(2,1)S(1)} custom-call(bf16[3,128,1024]{2,1,0:T(8,128)(2,1)S(1)} %get-tuple-element.51.refs_2_.hi_ref, bf16[3,128,1024]{2,1,0:T(8,128)(2,1)S(1)} %get-tuple-element.52.refs_3_.lo_ref, bf16[1024,768]{1,0:T(8,128)(2,1)S(1)} %get-tuple-element.58.q_ref, f32[8,128]{1,0:T(8,128)S(1)} %get-tuple-element.53.refs_5_.info_ref), custom_call_target="tpu_custom_call" | custom-call | flops 1 | bytes 1440000 | tf_op jit(solution)/shard_map/pallas_call | solution.py:32
  40.7 1.2 %collective-permute-start.22 = (s16[768,128]{1,0:T(8,128)(2,1)S(1)}, s16[768,128]{1,0:T(8,128)(2,1)S(1)}, u32[]{:S(2)}, u32[]{:S(2)}) collective-permute-start(s16[768,128]{1,0:T(8,128)(2,1)S(1)} %shard_map.91), channel_id=1, source_target_pairs={{0,8},{8,0},{16,24},{24,16},{1,9},{9,1},{17,25},{25,17},{2,10},{10... | collective-permute-start | bytes 589832 | tf_op jit(solution)/shard_map/ppermute | solution.py:23
  44.6 2.5 %collective-permute-start.24 = (s16[800,128]{1,0:T(8,128)(2,1)S(1)}, s16[800,128]{1,0:T(8,128)(2,1)S(1)}, u32[]{:S(2)}, u32[]{:S(2)}) collective-permute-start(s16[800,128]{1,0:T(8,128)(2,1)S(1)} %shard_map.94), channel_id=1, source_target_pairs={{0,16},{8,24},{16,0},{24,8},{1,17},{9,25},{17,1},{25,9},{2,18},{10... | collective-permute-start | bytes 614408 | tf_op jit(solution)/shard_map/ppermute | solution.py:23
  47.1 1.8 %collective-permute-start.17 = (s16[784,128]{1,0:T(8,128)(2,1)S(1)}, s16[784,128]{1,0:T(8,128)(2,1)S(1)}, u32[]{:S(2)}, u32[]{:S(2)}) collective-permute-start(s16[784,128]{1,0:T(8,128)(2,1)S(1)} %shard_map.85.refs_0_), channel_id=1, source_target_pairs={{0,6},{1,7},{2,4},{3,5},{4,2},{5,3},{6,0},{7,1},{8,14},{9,15},{10,... | collective-permute-start | bytes 602120 | tf_op jit(solution)/shard_map/ppermute | solution.py:23
  49.3 0.9 %collective-permute-start.23 = (s16[784,128]{1,0:T(8,128)(2,1)S(1)}, s16[784,128]{1,0:T(8,128)(2,1)S(1)}, u32[]{:S(2)}, u32[]{:S(2)}) collective-permute-start(s16[784,128]{1,0:T(8,128)(2,1)S(1)} %shard_map.92), channel_id=1, source_target_pairs={{0,4},{1,5},{2,6},{3,7},{4,0},{5,1},{6,2},{7,3},{8,12},{9,13},{10,... | collective-permute-start | bytes 602120 | tf_op jit(solution)/shard_map/ppermute | solution.py:23
  50.6 1.6 %collective-permute-start.20 = (s16[784,128]{1,0:T(8,128)(2,1)S(1)}, s16[784,128]{1,0:T(8,128)(2,1)S(1)}, u32[]{:S(2)}, u32[]{:S(2)}) collective-permute-start(s16[784,128]{1,0:T(8,128)(2,1)S(1)} %shard_map.89), channel_id=1, source_target_pairs={{0,2},{1,3},{2,0},{3,1},{4,6},{5,7},{6,4},{7,5},{8,10},{9,11},{10,... | collective-permute-start | bytes 602120 | tf_op jit(solution)/shard_map/ppermute | solution.py:23
  53.5 0.8 %collective-permute-done.15.refs_0_ = s16[768,128]{1,0:T(8,128)(2,1)S(1)} collective-permute-done((s16[768,128]{1,0:T(8,128)(2,1)S(1)}, s16[768,128]{1,0:T(8,128)(2,1)S(1)}, u32[]{:S(2)}, u32[]{:S(2)}) %collective-permute-start.15) | collective-permute-done | bytes 196640 | tf_op jit(solution)/shard_map/ppermute | solution.py:23
  54.3 1.7 %collective-permute-done.17.refs_1_.refs_2_ = s16[784,128]{1,0:T(8,128)(2,1)S(1)} collective-permute-done((s16[784,128]{1,0:T(8,128)(2,1)S(1)}, s16[784,128]{1,0:T(8,128)(2,1)S(1)}, u32[]{:S(2)}, u32[]{:S(2)}) %collective-permute-start.17) | collective-permute-done | bytes 200736 | tf_op jit(solution)/shard_map/ppermute | solution.py:23
  56.3 0.8 %collective-permute-done.24.refs_1_.refs_3_ = s16[800,128]{1,0:T(8,128)(2,1)S(1)} collective-permute-done((s16[800,128]{1,0:T(8,128)(2,1)S(1)}, s16[800,128]{1,0:T(8,128)(2,1)S(1)}, u32[]{:S(2)}, u32[]{:S(2)}) %collective-permute-start.24) | collective-permute-done | bytes 204832 | tf_op jit(solution)/shard_map/ppermute | solution.py:23
  57.1 1.2 %shard_map.96 = (f32[128,768]{1,0:T(8,128)}, f32[8,128]{1,0:T(8,128)S(1)}) custom-call(f32[768,128]{1,0:T(8,128)S(1)} %shard_map.95.own_ref, f32[8,128]{1,0:T(8,128)S(1)} %get-tuple-element.53.refs_5_.info_ref, s16[768,128]{1,0:T(8,128)(2,1)S(1)} %collective-permute-done.22.refs_0_, s16[800,128]{1,0:T(8,128)(2,1)S(1)} %collective-permute-done.24.refs_1_.refs_3_, ...), custom_call_target="tpu_custom_call" | custom-call | flops 1 | bytes 3600000 | tf_op jit(solution)/shard_map/pallas_call | solution.py:32
  58.3 0.9 %collective-permute-done.23.refs_1_ = s16[784,128]{1,0:T(8,128)(2,1)S(1)} collective-permute-done((s16[784,128]{1,0:T(8,128)(2,1)S(1)}, s16[784,128]{1,0:T(8,128)(2,1)S(1)}, u32[]{:S(2)}, u32[]{:S(2)}) %collective-permute-start.23) | collective-permute-done | bytes 200736 | tf_op jit(solution)/shard_map/ppermute | solution.py:23
  59.3 1.1 %shard_map.97 = (f32[1,1]{1,0:T(1,128)}, f32[128,768]{1,0:T(8,128)}) custom-call(f32[768,128]{1,0:T(8,128)S(1)} %shard_map.86.refs_2_.own_ref, f32[8,128]{1,0:T(8,128)S(1)} %get-tuple-element.53.refs_5_.info_ref, s16[784,128]{1,0:T(8,128)(2,1)S(1)} %collective-permute-done.18.arrived_ref.term_ref, s16[784,128]{1,0:T(8,128)(2,1)S(1)} %collective-permute-done.20.refs_0_, ...), custom_call_target="tpu_custom_call" | custom-call | flops 1 | bytes 3600000 | tf_op jit(solution)/shard_map/pallas_call | solution.py:32
  (55 shorter events, 13.3 us)
Async XLA Ops:
  2.7 14.1 %collective-permute-start.3 = (bf16[816,128]{1,0:T(8,128)(2,1)}, bf16[816,128]{1,0:T(8,128)(2,1)S(1)}, u32[]{:S(2)}, u32[]{:S(2)}) collective-permute-start(bf16[816,128]{1,0:T(8,128)(2,1)} %get-tuple-element.37), channel_id=1, source_target_pairs={{0,16},{8,24},{16,0},{24,8},{1,17},{9,25},{17,1},{25,9},{2,18},{10... | collective-permute-start | bytes 626696 | tf_op jit(solution)/shard_map/ppermute | solution.py:23
  6.8 11.9 %collective-permute-start.2 = (bf16[800,128]{1,0:T(8,128)(2,1)}, bf16[800,128]{1,0:T(8,128)(2,1)S(1)}, u32[]{:S(2)}, u32[]{:S(2)}) collective-permute-start(bf16[800,128]{1,0:T(8,128)(2,1)} %get-tuple-element.36.refs_8_), channel_id=1, source_target_pairs={{0,8},{8,0},{16,24},{24,16},{1,9},{9,1},{17,25},{25,17},{2,10},{10... | collective-permute-start | bytes 614408 | tf_op jit(solution)/shard_map/ppermute | solution.py:23
  8.3 10.4 %collective-permute-start.1 = (bf16[800,128]{1,0:T(8,128)(2,1)}, bf16[800,128]{1,0:T(8,128)(2,1)S(1)}, u32[]{:S(2)}, u32[]{:S(2)}) collective-permute-start(bf16[800,128]{1,0:T(8,128)(2,1)} %get-tuple-element.35.m_ref.refs_0_), channel_id=1, source_target_pairs={{0,2},{1,3},{2,0},{3,1},{4,6},{5,7},{6,4},{7,5},{8,10},{9,11},{10,... | collective-permute-start | bytes 614408 | tf_op jit(solution)/shard_map/ppermute | solution.py:23
  9.8 10.6 %collective-permute-start.5 = (bf16[800,128]{1,0:T(8,128)(2,1)}, bf16[800,128]{1,0:T(8,128)(2,1)S(1)}, u32[]{:S(2)}, u32[]{:S(2)}) collective-permute-start(bf16[800,128]{1,0:T(8,128)(2,1)} %get-tuple-element.35.m_ref.refs_0_), channel_id=1, source_target_pairs={{0,4},{1,5},{2,6},{3,7},{4,0},{5,1},{6,2},{7,3},{8,12},{9,13},{10,... | collective-permute-start | bytes 614408 | tf_op jit(solution)/shard_map/ppermute | solution.py:23
  11.4 9.5 %collective-permute-start.7 = (bf16[800,128]{1,0:T(8,128)(2,1)}, bf16[800,128]{1,0:T(8,128)(2,1)S(1)}, u32[]{:S(2)}, u32[]{:S(2)}) collective-permute-start(bf16[800,128]{1,0:T(8,128)(2,1)} %get-tuple-element.35.m_ref.refs_0_), channel_id=1, source_target_pairs={{0,6},{1,7},{2,4},{3,5},{4,2},{5,3},{6,0},{7,1},{8,14},{9,15},{10,... | collective-permute-start | bytes 614408 | tf_op jit(solution)/shard_map/ppermute | solution.py:23
  16.7 6.3 %collective-permute-start.9 = (bf16[816,128]{1,0:T(8,128)(2,1)S(1)}, bf16[816,128]{1,0:T(8,128)(2,1)S(1)}, u32[]{:S(2)}, u32[]{:S(2)}) collective-permute-start(bf16[816,128]{1,0:T(8,128)(2,1)S(1)} %collective-permute-done.3.refs_1_.refs_10_), channel_id=1, source_target_pairs={{0,8},{8,0},{16,24},{24,16},{1,9},{9,1},{17,25},{25,17},{2,10},{10... | collective-permute-start | bytes 626696 | tf_op jit(solution)/shard_map/ppermute | solution.py:23
  17.4 0.9 %copy-start = (bf16[800,128]{1,0:T(8,128)(2,1)S(1)}, bf16[800,128]{1,0:T(8,128)(2,1)}, u32[]{:S(2)}) copy-start(bf16[800,128]{1,0:T(8,128)(2,1)} %get-tuple-element.35.m_ref.refs_0_) | copy-start | bytes 614404
  18.4 4.7 %copy-start.1 = (bf16[800,128]{1,0:T(8,128)(2,1)S(1)}, bf16[800,128]{1,0:T(8,128)(2,1)}, u32[]{:S(2)}) copy-start(bf16[800,128]{1,0:T(8,128)(2,1)} %get-tuple-element.35.m_ref.refs_0_) | copy-start | bytes 614404
  18.4 4.7 %copy-start.2 = (bf16[800,128]{1,0:T(8,128)(2,1)S(1)}, bf16[800,128]{1,0:T(8,128)(2,1)}, u32[]{:S(2)}) copy-start(bf16[800,128]{1,0:T(8,128)(2,1)} %get-tuple-element.36.refs_8_) | copy-start | bytes 614404
  18.7 3.0 %collective-permute-start = (bf16[800,128]{1,0:T(8,128)(2,1)S(1)}, bf16[800,128]{1,0:T(8,128)(2,1)S(1)}, u32[]{:S(2)}, u32[]{:S(2)}) collective-permute-start(bf16[800,128]{1,0:T(8,128)(2,1)S(1)} %copy-done), channel_id=1, source_target_pairs={{0,1},{1,0},{2,3},{3,2},{4,5},{5,4},{6,7},{7,6},{8,9},{9,8},{10,11... | collective-permute-start | bytes 614408 | tf_op jit(solution)/shard_map/ppermute | solution.py:23
  19.1 2.9 %collective-permute-start.4 = (bf16[800,128]{1,0:T(8,128)(2,1)S(1)}, bf16[800,128]{1,0:T(8,128)(2,1)S(1)}, u32[]{:S(2)}, u32[]{:S(2)}) collective-permute-start(bf16[800,128]{1,0:T(8,128)(2,1)S(1)} %get-tuple-element.38.refs_2_), channel_id=1, source_target_pairs={{0,1},{1,0},{2,3},{3,2},{4,5},{5,4},{6,7},{7,6},{8,9},{9,8},{10,11... | collective-permute-start | bytes 614408 | tf_op jit(solution)/shard_map/ppermute | solution.py:23
  20.7 1.6 %collective-permute-start.6 = (bf16[800,128]{1,0:T(8,128)(2,1)S(1)}, bf16[800,128]{1,0:T(8,128)(2,1)S(1)}, u32[]{:S(2)}, u32[]{:S(2)}) collective-permute-start(bf16[800,128]{1,0:T(8,128)(2,1)S(1)} %get-tuple-element.39.refs_4_), channel_id=1, source_target_pairs={{0,1},{1,0},{2,3},{3,2},{4,5},{5,4},{6,7},{7,6},{8,9},{9,8},{10,11... | collective-permute-start | bytes 614408 | tf_op jit(solution)/shard_map/ppermute | solution.py:23
  21.1 1.6 %collective-permute-start.8 = (bf16[800,128]{1,0:T(8,128)(2,1)S(1)}, bf16[800,128]{1,0:T(8,128)(2,1)S(1)}, u32[]{:S(2)}, u32[]{:S(2)}) collective-permute-start(bf16[800,128]{1,0:T(8,128)(2,1)S(1)} %get-tuple-element.40.refs_6_), channel_id=1, source_target_pairs={{0,1},{1,0},{2,3},{3,2},{4,5},{5,4},{6,7},{7,6},{8,9},{9,8},{10,11... | collective-permute-start | bytes 614408 | tf_op jit(solution)/shard_map/ppermute | solution.py:23
  25.3 1.3 %collective-permute-start.10 = (f32[8,1536]{1,0:T(8,128)S(1)}, f32[8,1536]{1,0:T(8,128)S(1)}, u32[]{:S(2)}, u32[]{:S(2)}) collective-permute-start(f32[8,1536]{1,0:T(8,128)S(1)} %get-tuple-element.45.own_ref), channel_id=1, source_target_pairs={{0,1},{1,0},{2,3},{3,2},{4,5},{5,4},{6,7},{7,6},{8,9},{9,8},{10,11... | collective-permute-start | bytes 147464 | tf_op jit(solution)/shard_map/ppermute | solution.py:23
  26.7 4.9 %collective-permute-start.13 = (f32[8,1024]{1,0:T(8,128)S(1)}, f32[8,1024]{1,0:T(8,128)S(1)}, u32[]{:S(2)}, u32[]{:S(2)}) collective-permute-start(f32[8,1024]{1,0:T(8,128)S(1)} %shard_map.78.own_ref), channel_id=1, source_target_pairs={{0,6},{1,25},{2,4},{3,27},{4,2},{5,29},{6,0},{7,31},{8,14},{9,17},... | collective-permute-start | bytes 98312 | tf_op jit(solution)/shard_map/ppermute | solution.py:547
  28.9 3.9 %collective-permute-start.12 = (f32[8,1024]{1,0:T(8,128)S(1)}, f32[8,1024]{1,0:T(8,128)S(1)}, u32[]{:S(2)}, u32[]{:S(2)}) collective-permute-start(f32[8,1024]{1,0:T(8,128)S(1)} %shard_map.78.own_ref), channel_id=1, source_target_pairs={{0,4},{1,17},{2,6},{3,19},{4,0},{5,21},{6,2},{7,23},{8,12},{9,25},... | collective-permute-start | bytes 98312 | tf_op jit(solution)/shard_map/ppermute | solution.py:547
  29.4 3.9 %collective-permute-start.11 = (f32[8,1024]{1,0:T(8,128)S(1)}, f32[8,1024]{1,0:T(8,128)S(1)}, u32[]{:S(2)}, u32[]{:S(2)}) collective-permute-start(f32[8,1024]{1,0:T(8,128)S(1)} %shard_map.78.own_ref), channel_id=1, source_target_pairs={{0,2},{1,9},{2,0},{3,11},{4,6},{5,13},{6,4},{7,15},{8,10},{9,1},{1... | collective-permute-start | bytes 98312 | tf_op jit(solution)/shard_map/ppermute | solution.py:547
  33.4 2.1 %collective-permute-start.14 = (f32[8,1024]{1,0:T(8,128)S(1)}, f32[8,1024]{1,0:T(8,128)S(1)}, u32[]{:S(2)}, u32[]{:S(2)}) collective-permute-start(f32[8,1024]{1,0:T(8,128)S(1)} %shard_map.79.own_ref), channel_id=1, source_target_pairs={{0,1},{1,0},{2,3},{3,2},{4,5},{5,4},{6,7},{7,6},{8,9},{9,8},{10,11... | collective-permute-start | bytes 98312 | tf_op jit(solution)/shard_map/ppermute | solution.py:23
  36.7 7.5 %collective-permute-start.18 = (s16[784,128]{1,0:T(8,128)(2,1)S(1)}, s16[784,128]{1,0:T(8,128)(2,1)S(1)}, u32[]{:S(2)}, u32[]{:S(2)}) collective-permute-start(s16[784,128]{1,0:T(8,128)(2,1)S(1)} %shard_map.87), channel_id=1, source_target_pairs={{0,8},{8,0},{16,24},{24,16},{1,9},{9,1},{17,25},{25,17},{2,10},{10... | collective-permute-start | bytes 602120 | tf_op jit(solution)/shard_map/ppermute | solution.py:23
  39.4 4.4 %collective-permute-start.16 = (s16[768,128]{1,0:T(8,128)(2,1)S(1)}, s16[768,128]{1,0:T(8,128)(2,1)S(1)}, u32[]{:S(2)}, u32[]{:S(2)}) collective-permute-start(s16[768,128]{1,0:T(8,128)(2,1)S(1)} %get-tuple-element.57), channel_id=1, source_target_pairs={{0,1},{1,0},{2,3},{3,2},{4,5},{5,4},{6,7},{7,6},{8,9},{9,8},{10,11... | collective-permute-start | bytes 589832 | tf_op jit(solution)/shard_map/ppermute | solution.py:23
  40.7 8.1 %collective-permute-start.22 = (s16[768,128]{1,0:T(8,128)(2,1)S(1)}, s16[768,128]{1,0:T(8,128)(2,1)S(1)}, u32[]{:S(2)}, u32[]{:S(2)}) collective-permute-start(s16[768,128]{1,0:T(8,128)(2,1)S(1)} %shard_map.91), channel_id=1, source_target_pairs={{0,8},{8,0},{16,24},{24,16},{1,9},{9,1},{17,25},{25,17},{2,10},{10... | collective-permute-start | bytes 589832 | tf_op jit(solution)/shard_map/ppermute | solution.py:23
  41.9 7.0 %collective-permute-start.21 = (s16[768,128]{1,0:T(8,128)(2,1)S(1)}, s16[768,128]{1,0:T(8,128)(2,1)S(1)}, u32[]{:S(2)}, u32[]{:S(2)}) collective-permute-start(s16[768,128]{1,0:T(8,128)(2,1)S(1)} %get-tuple-element.62), channel_id=1, source_target_pairs={{0,1},{1,0},{2,3},{3,2},{4,5},{5,4},{6,7},{7,6},{8,9},{9,8},{10,11... | collective-permute-start | bytes 589832 | tf_op jit(solution)/shard_map/ppermute | solution.py:23
  42.7 7.5 %collective-permute-start.19 = (s16[768,128]{1,0:T(8,128)(2,1)S(1)}, s16[768,128]{1,0:T(8,128)(2,1)S(1)}, u32[]{:S(2)}, u32[]{:S(2)}) collective-permute-start(s16[768,128]{1,0:T(8,128)(2,1)S(1)} %get-tuple-element.60), channel_id=1, source_target_pairs={{0,1},{1,0},{2,3},{3,2},{4,5},{5,4},{6,7},{7,6},{8,9},{9,8},{10,11... | collective-permute-start | bytes 589832 | tf_op jit(solution)/shard_map/ppermute | solution.py:23
  44.6 12.5 %collective-permute-start.24 = (s16[800,128]{1,0:T(8,128)(2,1)S(1)}, s16[800,128]{1,0:T(8,128)(2,1)S(1)}, u32[]{:S(2)}, u32[]{:S(2)}) collective-permute-start(s16[800,128]{1,0:T(8,128)(2,1)S(1)} %shard_map.94), channel_id=1, source_target_pairs={{0,16},{8,24},{16,0},{24,8},{1,17},{9,25},{17,1},{25,9},{2,18},{10... | collective-permute-start | bytes 614408 | tf_op jit(solution)/shard_map/ppermute | solution.py:23
  47.1 8.8 %collective-permute-start.17 = (s16[784,128]{1,0:T(8,128)(2,1)S(1)}, s16[784,128]{1,0:T(8,128)(2,1)S(1)}, u32[]{:S(2)}, u32[]{:S(2)}) collective-permute-start(s16[784,128]{1,0:T(8,128)(2,1)S(1)} %shard_map.85.refs_0_), channel_id=1, source_target_pairs={{0,6},{1,7},{2,4},{3,5},{4,2},{5,3},{6,0},{7,1},{8,14},{9,15},{10,... | collective-permute-start | bytes 602120 | tf_op jit(solution)/shard_map/ppermute | solution.py:23
  49.3 9.9 %collective-permute-start.23 = (s16[784,128]{1,0:T(8,128)(2,1)S(1)}, s16[784,128]{1,0:T(8,128)(2,1)S(1)}, u32[]{:S(2)}, u32[]{:S(2)}) collective-permute-start(s16[784,128]{1,0:T(8,128)(2,1)S(1)} %shard_map.92), channel_id=1, source_target_pairs={{0,4},{1,5},{2,6},{3,7},{4,0},{5,1},{6,2},{7,3},{8,12},{9,13},{10,... | collective-permute-start | bytes 602120 | tf_op jit(solution)/shard_map/ppermute | solution.py:23
  50.6 8.7 %collective-permute-start.20 = (s16[784,128]{1,0:T(8,128)(2,1)S(1)}, s16[784,128]{1,0:T(8,128)(2,1)S(1)}, u32[]{:S(2)}, u32[]{:S(2)}) collective-permute-start(s16[784,128]{1,0:T(8,128)(2,1)S(1)} %shard_map.89), channel_id=1, source_target_pairs={{0,2},{1,3},{2,0},{3,1},{4,6},{5,7},{6,4},{7,5},{8,10},{9,11},{10,... | collective-permute-start | bytes 602120 | tf_op jit(solution)/shard_map/ppermute | solution.py:23
  52.8 1.5 %collective-permute-start.15 = (s16[768,128]{1,0:T(8,128)(2,1)S(1)}, s16[768,128]{1,0:T(8,128)(2,1)S(1)}, u32[]{:S(2)}, u32[]{:S(2)}) collective-permute-start(s16[768,128]{1,0:T(8,128)(2,1)S(1)} %get-tuple-element.55), channel_id=1, source_target_pairs={{0,1},{1,0},{2,3},{3,2},{4,5},{5,4},{6,7},{7,6},{8,9},{9,8},{10,11... | collective-permute-start | bytes 589832 | tf_op jit(solution)/shard_map/ppermute | solution.py:23

commit v6 on v5

--- a/solution.py
+++ b/solution.py
@@ -74,7 +74,8 @@
         part = p_ref[...].astype(BF16)
         for out in (near_out, far_out):
             put(out, part)
-            out[body:, :] = jnp.zeros((out.shape[0] - body, 128), BF16)
+            if out.shape[0] > body:
+                out[body:, :] = jnp.zeros((out.shape[0] - body, 128), BF16)
         put(q_out, q_ref[...].astype(BF16))
         ids = ids_ref[...].astype(F32)
         live = lax.broadcasted_iota(jnp.int32, (listed, rows), 0) < len_ref[...]
@@ -84,7 +85,7 @@
 
     return call(
         kernel,
-        [jax.ShapeDtypeStruct((body + listed + more, 128), BF16) for more in (0, 0, 16)],
+        [jax.ShapeDtypeStruct((body + listed + more, 128), BF16) for more in (0, -listed, 16)],
         [pltpu.VMEM(x.shape, x.dtype) for x in operands] + [pltpu.SemaphoreType.DMA((4,))],
         spare=operands,
         room=VMEM_MOST,
@@ -530,7 +531,7 @@
     messages, counts = [], []
     for k in row_turns:
         part = exchange(message, "pa", k) if k else message
-        part, count = count_listed(part, listed, down, [near, *far, counts[0]] if k else [])
+        part, count = count_listed(part, listed, down, [*far, counts[0], *([near] if k == across - 2 else [])] if k else [])
         other, other_count = count_listed(exchange(part, "pa", 1), listed, down)
         messages += [part, other]
         counts += [count, other_count]

time: 60.6 us -> 60.7 us (level)
  waiting for transfers between devices: 14.6 us -> 16.2 us
  starting transfers between devices: 25.9 us -> 24.5 us
    ppermute x22, starting transfers between devices: 22.4 us -> 20.9 us  [exchange(): return lax.ppermute(value, axis, [(i, i ^ turn) for i in range(size)])]
    ppermute x22, waiting for transfers between devices: 11.6 us -> 12.8 us  [exchange(): return lax.ppermute(value, axis, [(i, i ^ turn) for i in range(size)])]
where the time goes in v6:
time: 60.7 us; the launch traced here: 60.5 us
  starting transfers between devices  24.5 us (40%)
  Pallas kernels  18 us (30%)
  waiting for transfers between devices  16.2 us (27%)
  local copies, waits for them, and re-layouts  0.94 us (2%)
  between operations  0.88 us (1%)
    ppermute x22, starting transfers between devices, exchange(): return lax.ppermute(value, axis, [(i, i ^ turn) for i in range(size)])  20.9 us
    pallas_call x31, Pallas kernels, call(): pl.pallas_call(kernel, out_shape=out_shape, in_specs=spaces, out_specs=ja...  18 us
    ppermute x22, waiting for transfers between devices, exchange(): return lax.ppermute(value, axis, [(i, i ^ turn) for i in range(size)])  12.8 us
    ppermute x3, starting transfers between devices, per_device(): others.append(lax.ppermute(stats, ('pb', 'pa'), pairs))  3.55 us
    ppermute x3, waiting for transfers between devices, per_device(): others.append(lax.ppermute(stats, ('pb', 'pa'), pairs))  3.43 us
  transfers between devices with their start and end apart: 25, of which 13 were waited for; matrix products, arithmetic and copies ran while one was open for 0% of the time, Pallas kernels for 19%

profile of v6, /device:TPU:0, one launch (start us, length us, event | category | flops | bytes accessed | tf_op | source)
XLA Modules:
  0.0 60.5 jit_solution(17219817281990967649)
XLA Ops:
  0.6 2.0 %shard_map.67 = (bf16[800,128]{1,0:T(8,128)(2,1)}, bf16[768,128]{1,0:T(8,128)(2,1)}, bf16[816,128]{1,0:T(8,128)(2,1)}) custom-call(f32[128,768]{1,0:T(8,128)} %refs_0_.1, s32[32,128]{1,0:T(8,128)} %bitcast.3, s32[1,128]{1,0:T(1,128)} %bitcast.4, f32[128,768]{1,0:T(8,128)} %refs_3_.1), custom_call_target="tpu_custom_call" | custom-call | flops 1 | bytes 7200000 | tf_op jit(solution)/shard_map/pallas_call | solution.py:32
  2.7 4.1 %collective-permute-start.2 = (bf16[816,128]{1,0:T(8,128)(2,1)}, bf16[816,128]{1,0:T(8,128)(2,1)S(1)}, u32[]{:S(2)}, u32[]{:S(2)}) collective-permute-start(bf16[816,128]{1,0:T(8,128)(2,1)} %get-tuple-element.36), channel_id=1, source_target_pairs={{0,16},{8,24},{16,0},{24,8},{1,17},{9,25},{17,1},{25,9},{2,18},{10... | collective-permute-start | bytes 626696 | tf_op jit(solution)/shard_map/ppermute | solution.py:23
  6.8 1.5 %collective-permute-start.1 = (bf16[800,128]{1,0:T(8,128)(2,1)}, bf16[800,128]{1,0:T(8,128)(2,1)S(1)}, u32[]{:S(2)}, u32[]{:S(2)}) collective-permute-start(bf16[800,128]{1,0:T(8,128)(2,1)} %get-tuple-element.35.m_ref.refs_0_), channel_id=1, source_target_pairs={{0,2},{1,3},{2,0},{3,1},{4,6},{5,7},{6,4},{7,5},{8,10},{9,11},{10,... | collective-permute-start | bytes 614408 | tf_op jit(solution)/shard_map/ppermute | solution.py:23
  8.3 1.5 %collective-permute-start.4 = (bf16[800,128]{1,0:T(8,128)(2,1)}, bf16[800,128]{1,0:T(8,128)(2,1)S(1)}, u32[]{:S(2)}, u32[]{:S(2)}) collective-permute-start(bf16[800,128]{1,0:T(8,128)(2,1)} %get-tuple-element.35.m_ref.refs_0_), channel_id=1, source_target_pairs={{0,4},{1,5},{2,6},{3,7},{4,0},{5,1},{6,2},{7,3},{8,12},{9,13},{10,... | collective-permute-start | bytes 614408 | tf_op jit(solution)/shard_map/ppermute | solution.py:23
  10.3 1.6 %collective-permute-start.7 = (bf16[768,128]{1,0:T(8,128)(2,1)}, bf16[768,128]{1,0:T(8,128)(2,1)S(1)}, u32[]{:S(2)}, u32[]{:S(2)}) collective-permute-start(bf16[768,128]{1,0:T(8,128)(2,1)} %get-tuple-element.39.refs_8_), channel_id=1, source_target_pairs={{0,8},{8,0},{16,24},{24,16},{1,9},{9,1},{17,25},{25,17},{2,10},{10... | collective-permute-start | bytes 589832 | tf_op jit(solution)/shard_map/ppermute | solution.py:23
  11.8 4.9 %collective-permute-done.2.refs_0_.refs_10_ = bf16[816,128]{1,0:T(8,128)(2,1)S(1)} collective-permute-done((bf16[816,128]{1,0:T(8,128)(2,1)}, bf16[816,128]{1,0:T(8,128)(2,1)S(1)}, u32[]{:S(2)}, u32[]{:S(2)}) %collective-permute-start.2) | collective-permute-done | bytes 208928 | tf_op jit(solution)/shard_map/ppermute | solution.py:23
  16.7 0.8 %collective-permute-start.9 = (bf16[816,128]{1,0:T(8,128)(2,1)S(1)}, bf16[816,128]{1,0:T(8,128)(2,1)S(1)}, u32[]{:S(2)}, u32[]{:S(2)}) collective-permute-start(bf16[816,128]{1,0:T(8,128)(2,1)S(1)} %collective-permute-done.2.refs_0_.refs_10_), channel_id=1, source_target_pairs={{0,8},{8,0},{16,24},{24,16},{1,9},{9,1},{17,25},{25,17},{2,10},{10... | collective-permute-start | bytes 626696 | tf_op jit(solution)/shard_map/ppermute | solution.py:23
  17.5 0.9 %copy-done = bf16[800,128]{1,0:T(8,128)(2,1)S(1)} copy-done((bf16[800,128]{1,0:T(8,128)(2,1)S(1)}, bf16[800,128]{1,0:T(8,128)(2,1)}, u32[]{:S(2)}) %copy-start) | copy-done | bytes 204824
  22.4 1.4 %collective-permute-done.9.refs_11_ = bf16[816,128]{1,0:T(8,128)(2,1)S(1)} collective-permute-done((bf16[816,128]{1,0:T(8,128)(2,1)S(1)}, bf16[816,128]{1,0:T(8,128)(2,1)S(1)}, u32[]{:S(2)}, u32[]{:S(2)}) %collective-permute-start.9) | collective-permute-done | bytes 208928 | tf_op jit(solution)/shard_map/ppermute | solution.py:23
  23.8 2.2 %shard_map.76 = (f32[512,1024]{1,0:T(8,128)S(1)}, f32[8,1536]{1,0:T(8,128)S(1)}, bf16[1024,768]{1,0:T(8,128)(2,1)S(1)}, bf16[512,768]{1,0:T(8,128)(2,1)S(1)}) custom-call(bf16[800,128]{1,0:T(8,128)(2,1)S(1)} %copy-done.1, bf16[800,128]{1,0:T(8,128)(2,1)S(1)} %collective-permute-done.m_ref.refs_1_, bf16[800,128]{1,0:T(8,128)(2,1)S(1)} %get-tuple-element.37.refs_2_, ...), custom_call_target="tpu_custom_call" | custom-call | flops 1 | bytes 7200000 | tf_op jit(solution)/shard_map/pallas_call | solution.py:32
  26.4 0.9 %collective-permute-done.10.other_ref = f32[8,1536]{1,0:T(8,128)S(1)} collective-permute-done((f32[8,1536]{1,0:T(8,128)S(1)}, f32[8,1536]{1,0:T(8,128)S(1)}, u32[]{:S(2)}, u32[]{:S(2)}) %collective-permute-start.10) | collective-permute-done | bytes 49184 | tf_op jit(solution)/shard_map/ppermute | solution.py:23
  27.3 2.6 %collective-permute-start.13 = (f32[8,1024]{1,0:T(8,128)S(1)}, f32[8,1024]{1,0:T(8,128)S(1)}, u32[]{:S(2)}, u32[]{:S(2)}) collective-permute-start(f32[8,1024]{1,0:T(8,128)S(1)} %shard_map.78.own_ref), channel_id=1, source_target_pairs={{0,6},{1,25},{2,4},{3,27},{4,2},{5,29},{6,0},{7,31},{8,14},{9,17},... | collective-permute-start | bytes 98312 | tf_op jit(solution)/shard_map/ppermute | solution.py:548
  30.9 1.3 %collective-permute-done.13.refs_2_ = f32[8,1024]{1,0:T(8,128)S(1)} collective-permute-done((f32[8,1024]{1,0:T(8,128)S(1)}, f32[8,1024]{1,0:T(8,128)S(1)}, u32[]{:S(2)}, u32[]{:S(2)}) %collective-permute-start.13) | collective-permute-done | bytes 32800 | tf_op jit(solution)/shard_map/ppermute | solution.py:548
  32.2 1.6 %collective-permute-done.12.refs_1_ = f32[8,1024]{1,0:T(8,128)S(1)} collective-permute-done((f32[8,1024]{1,0:T(8,128)S(1)}, f32[8,1024]{1,0:T(8,128)S(1)}, u32[]{:S(2)}, u32[]{:S(2)}) %collective-permute-start.12) | collective-permute-done | bytes 32800 | tf_op jit(solution)/shard_map/ppermute | solution.py:548
  34.6 1.1 %collective-permute-done.14.other_ref = f32[8,1024]{1,0:T(8,128)S(1)} collective-permute-done((f32[8,1024]{1,0:T(8,128)S(1)}, f32[8,1024]{1,0:T(8,128)S(1)}, u32[]{:S(2)}, u32[]{:S(2)}) %collective-permute-start.14) | collective-permute-done | bytes 32800 | tf_op jit(solution)/shard_map/ppermute | solution.py:23
  36.2 0.7 %shard_map.87 = s16[784,128]{1,0:T(8,128)(2,1)S(1)} custom-call(bf16[1,128,1024]{2,1,0:T(8,128)(2,1)S(1)} %get-tuple-element.49.refs_0_.hi_ref, bf16[1,128,1024]{2,1,0:T(8,128)(2,1)S(1)} %get-tuple-element.50.refs_1_.lo_ref, bf16[1024,768]{1,0:T(8,128)(2,1)S(1)} %get-tuple-element.58.q_ref, f32[8,128]{1,0:T(8,128)S(1)} %get-tuple-element.53.refs_5_.info_ref), custom_call_target="tpu_custom_call" | custom-call | flops 1 | bytes 1440000 | tf_op jit(solution)/shard_map/pallas_call | solution.py:32
  36.9 0.8 %collective-permute-start.18 = (s16[784,128]{1,0:T(8,128)(2,1)S(1)}, s16[784,128]{1,0:T(8,128)(2,1)S(1)}, u32[]{:S(2)}, u32[]{:S(2)}) collective-permute-start(s16[784,128]{1,0:T(8,128)(2,1)S(1)} %shard_map.87), channel_id=1, source_target_pairs={{0,8},{8,0},{16,24},{24,16},{1,9},{9,1},{17,25},{25,17},{2,10},{10... | collective-permute-start | bytes 602120 | tf_op jit(solution)/shard_map/ppermute | solution.py:23
  37.7 1.0 %shard_map.82 = (bf16[3,128,1024]{2,1,0:T(8,128)(2,1)S(1)}, bf16[3,128,1024]{2,1,0:T(8,128)(2,1)S(1)}) custom-call(f32[512,1024]{1,0:T(8,128)S(1)} %get-tuple-element.44.s_ref, f32[8,1024]{1,0:T(8,128)S(1)} %get-tuple-element.47.row_ref, f32[512,128]{1,0:T(8,128)S(1)} %get-tuple-element.48.col_ref, s32[1,128,128]{2,1,0:T(8,128)S(1)} %shard_map.68.refs_1_.refs_12_.refs_0_, ...), custom_call_target="tpu_custom_call" | custom-call | flops 1 | bytes 4860000 | tf_op jit(solution)/shard_map/pallas_call | solution.py:32
  39.5 0.7 %shard_map.91 = s16[768,128]{1,0:T(8,128)(2,1)S(1)} custom-call(bf16[3,128,1024]{2,1,0:T(8,128)(2,1)S(1)} %get-tuple-element.51.refs_2_.hi_ref, bf16[3,128,1024]{2,1,0:T(8,128)(2,1)S(1)} %get-tuple-element.52.refs_3_.lo_ref, bf16[1024,768]{1,0:T(8,128)(2,1)S(1)} %get-tuple-element.58.q_ref, f32[8,128]{1,0:T(8,128)S(1)} %get-tuple-element.53.refs_5_.info_ref), custom_call_target="tpu_custom_call" | custom-call | flops 1 | bytes 1440000 | tf_op jit(solution)/shard_map/pallas_call | solution.py:32
  40.2 0.6 shard_map.90
  40.8 1.3 %collective-permute-start.22 = (s16[768,128]{1,0:T(8,128)(2,1)S(1)}, s16[768,128]{1,0:T(8,128)(2,1)S(1)}, u32[]{:S(2)}, u32[]{:S(2)}) collective-permute-start(s16[768,128]{1,0:T(8,128)(2,1)S(1)} %shard_map.91), channel_id=1, source_target_pairs={{0,8},{8,0},{16,24},{24,16},{1,9},{9,1},{17,25},{25,17},{2,10},{10... | collective-permute-start | bytes 589832 | tf_op jit(solution)/shard_map/ppermute | solution.py:23
  44.8 2.4 %collective-permute-start.24 = (s16[800,128]{1,0:T(8,128)(2,1)S(1)}, s16[800,128]{1,0:T(8,128)(2,1)S(1)}, u32[]{:S(2)}, u32[]{:S(2)}) collective-permute-start(s16[800,128]{1,0:T(8,128)(2,1)S(1)} %shard_map.94), channel_id=1, source_target_pairs={{0,16},{8,24},{16,0},{24,8},{1,17},{9,25},{17,1},{25,9},{2,18},{10... | collective-permute-start | bytes 614408 | tf_op jit(solution)/shard_map/ppermute | solution.py:23
  47.2 1.8 %collective-permute-start.17 = (s16[784,128]{1,0:T(8,128)(2,1)S(1)}, s16[784,128]{1,0:T(8,128)(2,1)S(1)}, u32[]{:S(2)}, u32[]{:S(2)}) collective-permute-start(s16[784,128]{1,0:T(8,128)(2,1)S(1)} %shard_map.85.refs_0_), channel_id=1, source_target_pairs={{0,6},{1,7},{2,4},{3,5},{4,2},{5,3},{6,0},{7,1},{8,14},{9,15},{10,... | collective-permute-start | bytes 602120 | tf_op jit(solution)/shard_map/ppermute | solution.py:23
  49.3 0.9 %collective-permute-start.23 = (s16[784,128]{1,0:T(8,128)(2,1)S(1)}, s16[784,128]{1,0:T(8,128)(2,1)S(1)}, u32[]{:S(2)}, u32[]{:S(2)}) collective-permute-start(s16[784,128]{1,0:T(8,128)(2,1)S(1)} %shard_map.92), channel_id=1, source_target_pairs={{0,4},{1,5},{2,6},{3,7},{4,0},{5,1},{6,2},{7,3},{8,12},{9,13},{10,... | collective-permute-start | bytes 602120 | tf_op jit(solution)/shard_map/ppermute | solution.py:23
  50.7 1.5 %collective-permute-start.20 = (s16[784,128]{1,0:T(8,128)(2,1)S(1)}, s16[784,128]{1,0:T(8,128)(2,1)S(1)}, u32[]{:S(2)}, u32[]{:S(2)}) collective-permute-start(s16[784,128]{1,0:T(8,128)(2,1)S(1)} %shard_map.89), channel_id=1, source_target_pairs={{0,2},{1,3},{2,0},{3,1},{4,6},{5,7},{6,4},{7,5},{8,10},{9,11},{10,... | collective-permute-start | bytes 602120 | tf_op jit(solution)/shard_map/ppermute | solution.py:23
  52.2 0.6 shard_map.83
  53.5 0.8 %collective-permute-done.15.refs_0_ = s16[768,128]{1,0:T(8,128)(2,1)S(1)} collective-permute-done((s16[768,128]{1,0:T(8,128)(2,1)S(1)}, s16[768,128]{1,0:T(8,128)(2,1)S(1)}, u32[]{:S(2)}, u32[]{:S(2)}) %collective-permute-start.15) | collective-permute-done | bytes 196640 | tf_op jit(solution)/shard_map/ppermute | solution.py:23
  54.3 1.6 %collective-permute-done.17.refs_1_.refs_2_ = s16[784,128]{1,0:T(8,128)(2,1)S(1)} collective-permute-done((s16[784,128]{1,0:T(8,128)(2,1)S(1)}, s16[784,128]{1,0:T(8,128)(2,1)S(1)}, u32[]{:S(2)}, u32[]{:S(2)}) %collective-permute-start.17) | collective-permute-done | bytes 200736 | tf_op jit(solution)/shard_map/ppermute | solution.py:23
  56.4 1.0 %collective-permute-done.24.refs_1_.refs_3_ = s16[800,128]{1,0:T(8,128)(2,1)S(1)} collective-permute-done((s16[800,128]{1,0:T(8,128)(2,1)S(1)}, s16[800,128]{1,0:T(8,128)(2,1)S(1)}, u32[]{:S(2)}, u32[]{:S(2)}) %collective-permute-start.24) | collective-permute-done | bytes 204832 | tf_op jit(solution)/shard_map/ppermute | solution.py:23
  57.4 1.2 %shard_map.96 = (f32[128,768]{1,0:T(8,128)}, f32[8,128]{1,0:T(8,128)S(1)}) custom-call(f32[768,128]{1,0:T(8,128)S(1)} %shard_map.95.own_ref, f32[8,128]{1,0:T(8,128)S(1)} %get-tuple-element.53.refs_5_.info_ref, s16[768,128]{1,0:T(8,128)(2,1)S(1)} %collective-permute-done.22.refs_0_, s16[800,128]{1,0:T(8,128)(2,1)S(1)} %collective-permute-done.24.refs_1_.refs_3_, ...), custom_call_target="tpu_custom_call" | custom-call | flops 1 | bytes 3600000 | tf_op jit(solution)/shard_map/pallas_call | solution.py:32
  58.5 0.7 %collective-permute-done.23.refs_1_ = s16[784,128]{1,0:T(8,128)(2,1)S(1)} collective-permute-done((s16[784,128]{1,0:T(8,128)(2,1)S(1)}, s16[784,128]{1,0:T(8,128)(2,1)S(1)}, u32[]{:S(2)}, u32[]{:S(2)}) %collective-permute-start.23) | collective-permute-done | bytes 200736 | tf_op jit(solution)/shard_map/ppermute | solution.py:23
  59.4 1.1 %shard_map.97 = (f32[1,1]{1,0:T(1,128)}, f32[128,768]{1,0:T(8,128)}) custom-call(f32[768,128]{1,0:T(8,128)S(1)} %shard_map.86.refs_2_.own_ref, f32[8,128]{1,0:T(8,128)S(1)} %get-tuple-element.53.refs_5_.info_ref, s16[784,128]{1,0:T(8,128)(2,1)S(1)} %collective-permute-done.18.arrived_ref.term_ref, s16[784,128]{1,0:T(8,128)(2,1)S(1)} %collective-permute-done.20.refs_0_, ...), custom_call_target="tpu_custom_call" | custom-call | flops 1 | bytes 3600000 | tf_op jit(solution)/shard_map/pallas_call | solution.py:32
  (55 shorter events, 12.4 us)
Async XLA Ops:
  2.7 14.1 %collective-permute-start.2 = (bf16[816,128]{1,0:T(8,128)(2,1)}, bf16[816,128]{1,0:T(8,128)(2,1)S(1)}, u32[]{:S(2)}, u32[]{:S(2)}) collective-permute-start(bf16[816,128]{1,0:T(8,128)(2,1)} %get-tuple-element.36), channel_id=1, source_target_pairs={{0,16},{8,24},{16,0},{24,8},{1,17},{9,25},{17,1},{25,9},{2,18},{10... | collective-permute-start | bytes 626696 | tf_op jit(solution)/shard_map/ppermute | solution.py:23
  6.8 12.0 %collective-permute-start.1 = (bf16[800,128]{1,0:T(8,128)(2,1)}, bf16[800,128]{1,0:T(8,128)(2,1)S(1)}, u32[]{:S(2)}, u32[]{:S(2)}) collective-permute-start(bf16[800,128]{1,0:T(8,128)(2,1)} %get-tuple-element.35.m_ref.refs_0_), channel_id=1, source_target_pairs={{0,2},{1,3},{2,0},{3,1},{4,6},{5,7},{6,4},{7,5},{8,10},{9,11},{10,... | collective-permute-start | bytes 614408 | tf_op jit(solution)/shard_map/ppermute | solution.py:23
  8.3 10.9 %collective-permute-start.4 = (bf16[800,128]{1,0:T(8,128)(2,1)}, bf16[800,128]{1,0:T(8,128)(2,1)S(1)}, u32[]{:S(2)}, u32[]{:S(2)}) collective-permute-start(bf16[800,128]{1,0:T(8,128)(2,1)} %get-tuple-element.35.m_ref.refs_0_), channel_id=1, source_target_pairs={{0,4},{1,5},{2,6},{3,7},{4,0},{5,1},{6,2},{7,3},{8,12},{9,13},{10,... | collective-permute-start | bytes 614408 | tf_op jit(solution)/shard_map/ppermute | solution.py:23
  9.8 10.3 %collective-permute-start.6 = (bf16[800,128]{1,0:T(8,128)(2,1)}, bf16[800,128]{1,0:T(8,128)(2,1)S(1)}, u32[]{:S(2)}, u32[]{:S(2)}) collective-permute-start(bf16[800,128]{1,0:T(8,128)(2,1)} %get-tuple-element.35.m_ref.refs_0_), channel_id=1, source_target_pairs={{0,6},{1,7},{2,4},{3,5},{4,2},{5,3},{6,0},{7,1},{8,14},{9,15},{10,... | collective-permute-start | bytes 614408 | tf_op jit(solution)/shard_map/ppermute | solution.py:23
  10.3 9.8 %collective-permute-start.7 = (bf16[768,128]{1,0:T(8,128)(2,1)}, bf16[768,128]{1,0:T(8,128)(2,1)S(1)}, u32[]{:S(2)}, u32[]{:S(2)}) collective-permute-start(bf16[768,128]{1,0:T(8,128)(2,1)} %get-tuple-element.39.refs_8_), channel_id=1, source_target_pairs={{0,8},{8,0},{16,24},{24,16},{1,9},{9,1},{17,25},{25,17},{2,10},{10... | collective-permute-start | bytes 589832 | tf_op jit(solution)/shard_map/ppermute | solution.py:23
  16.7 7.1 %collective-permute-start.9 = (bf16[816,128]{1,0:T(8,128)(2,1)S(1)}, bf16[816,128]{1,0:T(8,128)(2,1)S(1)}, u32[]{:S(2)}, u32[]{:S(2)}) collective-permute-start(bf16[816,128]{1,0:T(8,128)(2,1)S(1)} %collective-permute-done.2.refs_0_.refs_10_), channel_id=1, source_target_pairs={{0,8},{8,0},{16,24},{24,16},{1,9},{9,1},{17,25},{25,17},{2,10},{10... | collective-permute-start | bytes 626696 | tf_op jit(solution)/shard_map/ppermute | solution.py:23
  17.5 0.9 %copy-start = (bf16[800,128]{1,0:T(8,128)(2,1)S(1)}, bf16[800,128]{1,0:T(8,128)(2,1)}, u32[]{:S(2)}) copy-start(bf16[800,128]{1,0:T(8,128)(2,1)} %get-tuple-element.35.m_ref.refs_0_) | copy-start | bytes 614404
  18.4 5.4 %copy-start.1 = (bf16[800,128]{1,0:T(8,128)(2,1)S(1)}, bf16[800,128]{1,0:T(8,128)(2,1)}, u32[]{:S(2)}) copy-start(bf16[800,128]{1,0:T(8,128)(2,1)} %get-tuple-element.35.m_ref.refs_0_) | copy-start | bytes 614404
  18.4 5.4 %copy-start.2 = (bf16[768,128]{1,0:T(8,128)(2,1)S(1)}, bf16[768,128]{1,0:T(8,128)(2,1)}, u32[]{:S(2)}) copy-start(bf16[768,128]{1,0:T(8,128)(2,1)} %get-tuple-element.39.refs_8_) | copy-start | bytes 589828
  18.7 2.3 %collective-permute-start = (bf16[800,128]{1,0:T(8,128)(2,1)S(1)}, bf16[800,128]{1,0:T(8,128)(2,1)S(1)}, u32[]{:S(2)}, u32[]{:S(2)}) collective-permute-start(bf16[800,128]{1,0:T(8,128)(2,1)S(1)} %copy-done), channel_id=1, source_target_pairs={{0,1},{1,0},{2,3},{3,2},{4,5},{5,4},{6,7},{7,6},{8,9},{9,8},{10,11... | collective-permute-start | bytes 614408 | tf_op jit(solution)/shard_map/ppermute | solution.py:23
  19.1 2.2 %collective-permute-start.3 = (bf16[800,128]{1,0:T(8,128)(2,1)S(1)}, bf16[800,128]{1,0:T(8,128)(2,1)S(1)}, u32[]{:S(2)}, u32[]{:S(2)}) collective-permute-start(bf16[800,128]{1,0:T(8,128)(2,1)S(1)} %get-tuple-element.37.refs_2_), channel_id=1, source_target_pairs={{0,1},{1,0},{2,3},{3,2},{4,5},{5,4},{6,7},{7,6},{8,9},{9,8},{10,11... | collective-permute-start | bytes 614408 | tf_op jit(solution)/shard_map/ppermute | solution.py:23
  20.0 1.6 %collective-permute-start.5 = (bf16[800,128]{1,0:T(8,128)(2,1)S(1)}, bf16[800,128]{1,0:T(8,128)(2,1)S(1)}, u32[]{:S(2)}, u32[]{:S(2)}) collective-permute-start(bf16[800,128]{1,0:T(8,128)(2,1)S(1)} %get-tuple-element.38.refs_4_), channel_id=1, source_target_pairs={{0,1},{1,0},{2,3},{3,2},{4,5},{5,4},{6,7},{7,6},{8,9},{9,8},{10,11... | collective-permute-start | bytes 614408 | tf_op jit(solution)/shard_map/ppermute | solution.py:23
  20.4 1.6 %collective-permute-start.8 = (bf16[800,128]{1,0:T(8,128)(2,1)S(1)}, bf16[800,128]{1,0:T(8,128)(2,1)S(1)}, u32[]{:S(2)}, u32[]{:S(2)}) collective-permute-start(bf16[800,128]{1,0:T(8,128)(2,1)S(1)} %get-tuple-element.40.refs_6_), channel_id=1, source_target_pairs={{0,1},{1,0},{2,3},{3,2},{4,5},{5,4},{6,7},{7,6},{8,9},{9,8},{10,11... | collective-permute-start | bytes 614408 | tf_op jit(solution)/shard_map/ppermute | solution.py:23
  26.0 1.3 %collective-permute-start.10 = (f32[8,1536]{1,0:T(8,128)S(1)}, f32[8,1536]{1,0:T(8,128)S(1)}, u32[]{:S(2)}, u32[]{:S(2)}) collective-permute-start(f32[8,1536]{1,0:T(8,128)S(1)} %get-tuple-element.45.own_ref), channel_id=1, source_target_pairs={{0,1},{1,0},{2,3},{3,2},{4,5},{5,4},{6,7},{7,6},{8,9},{9,8},{10,11... | collective-permute-start | bytes 147464 | tf_op jit(solution)/shard_map/ppermute | solution.py:23
  27.3 4.9 %collective-permute-start.13 = (f32[8,1024]{1,0:T(8,128)S(1)}, f32[8,1024]{1,0:T(8,128)S(1)}, u32[]{:S(2)}, u32[]{:S(2)}) collective-permute-start(f32[8,1024]{1,0:T(8,128)S(1)} %shard_map.78.own_ref), channel_id=1, source_target_pairs={{0,6},{1,25},{2,4},{3,27},{4,2},{5,29},{6,0},{7,31},{8,14},{9,17},... | collective-permute-start | bytes 98312 | tf_op jit(solution)/shard_map/ppermute | solution.py:548
  29.9 3.9 %collective-permute-start.12 = (f32[8,1024]{1,0:T(8,128)S(1)}, f32[8,1024]{1,0:T(8,128)S(1)}, u32[]{:S(2)}, u32[]{:S(2)}) collective-permute-start(f32[8,1024]{1,0:T(8,128)S(1)} %shard_map.78.own_ref), channel_id=1, source_target_pairs={{0,4},{1,17},{2,6},{3,19},{4,0},{5,21},{6,2},{7,23},{8,12},{9,25},... | collective-permute-start | bytes 98312 | tf_op jit(solution)/shard_map/ppermute | solution.py:548
  30.4 3.9 %collective-permute-start.11 = (f32[8,1024]{1,0:T(8,128)S(1)}, f32[8,1024]{1,0:T(8,128)S(1)}, u32[]{:S(2)}, u32[]{:S(2)}) collective-permute-start(f32[8,1024]{1,0:T(8,128)S(1)} %shard_map.78.own_ref), channel_id=1, source_target_pairs={{0,2},{1,9},{2,0},{3,11},{4,6},{5,13},{6,4},{7,15},{8,10},{9,1},{1... | collective-permute-start | bytes 98312 | tf_op jit(solution)/shard_map/ppermute | solution.py:548
  34.4 1.3 %collective-permute-start.14 = (f32[8,1024]{1,0:T(8,128)S(1)}, f32[8,1024]{1,0:T(8,128)S(1)}, u32[]{:S(2)}, u32[]{:S(2)}) collective-permute-start(f32[8,1024]{1,0:T(8,128)S(1)} %shard_map.79.own_ref), channel_id=1, source_target_pairs={{0,1},{1,0},{2,3},{3,2},{4,5},{5,4},{6,7},{7,6},{8,9},{9,8},{10,11... | collective-permute-start | bytes 98312 | tf_op jit(solution)/shard_map/ppermute | solution.py:23
  36.9 7.4 %collective-permute-start.18 = (s16[784,128]{1,0:T(8,128)(2,1)S(1)}, s16[784,128]{1,0:T(8,128)(2,1)S(1)}, u32[]{:S(2)}, u32[]{:S(2)}) collective-permute-start(s16[784,128]{1,0:T(8,128)(2,1)S(1)} %shard_map.87), channel_id=1, source_target_pairs={{0,8},{8,0},{16,24},{24,16},{1,9},{9,1},{17,25},{25,17},{2,10},{10... | collective-permute-start | bytes 602120 | tf_op jit(solution)/shard_map/ppermute | solution.py:23
  39.4 4.5 %collective-permute-start.16 = (s16[768,128]{1,0:T(8,128)(2,1)S(1)}, s16[768,128]{1,0:T(8,128)(2,1)S(1)}, u32[]{:S(2)}, u32[]{:S(2)}) collective-permute-start(s16[768,128]{1,0:T(8,128)(2,1)S(1)} %get-tuple-element.57), channel_id=1, source_target_pairs={{0,1},{1,0},{2,3},{3,2},{4,5},{5,4},{6,7},{7,6},{8,9},{9,8},{10,11... | collective-permute-start | bytes 589832 | tf_op jit(solution)/shard_map/ppermute | solution.py:23
  40.8 8.1 %collective-permute-start.22 = (s16[768,128]{1,0:T(8,128)(2,1)S(1)}, s16[768,128]{1,0:T(8,128)(2,1)S(1)}, u32[]{:S(2)}, u32[]{:S(2)}) collective-permute-start(s16[768,128]{1,0:T(8,128)(2,1)S(1)} %shard_map.91), channel_id=1, source_target_pairs={{0,8},{8,0},{16,24},{24,16},{1,9},{9,1},{17,25},{25,17},{2,10},{10... | collective-permute-start | bytes 589832 | tf_op jit(solution)/shard_map/ppermute | solution.py:23
  42.1 6.8 %collective-permute-start.21 = (s16[768,128]{1,0:T(8,128)(2,1)S(1)}, s16[768,128]{1,0:T(8,128)(2,1)S(1)}, u32[]{:S(2)}, u32[]{:S(2)}) collective-permute-start(s16[768,128]{1,0:T(8,128)(2,1)S(1)} %get-tuple-element.62), channel_id=1, source_target_pairs={{0,1},{1,0},{2,3},{3,2},{4,5},{5,4},{6,7},{7,6},{8,9},{9,8},{10,11... | collective-permute-start | bytes 589832 | tf_op jit(solution)/shard_map/ppermute | solution.py:23
  42.9 7.3 %collective-permute-start.19 = (s16[768,128]{1,0:T(8,128)(2,1)S(1)}, s16[768,128]{1,0:T(8,128)(2,1)S(1)}, u32[]{:S(2)}, u32[]{:S(2)}) collective-permute-start(s16[768,128]{1,0:T(8,128)(2,1)S(1)} %get-tuple-element.60), channel_id=1, source_target_pairs={{0,1},{1,0},{2,3},{3,2},{4,5},{5,4},{6,7},{7,6},{8,9},{9,8},{10,11... | collective-permute-start | bytes 589832 | tf_op jit(solution)/shard_map/ppermute | solution.py:23
  44.8 12.5 %collective-permute-start.24 = (s16[800,128]{1,0:T(8,128)(2,1)S(1)}, s16[800,128]{1,0:T(8,128)(2,1)S(1)}, u32[]{:S(2)}, u32[]{:S(2)}) collective-permute-start(s16[800,128]{1,0:T(8,128)(2,1)S(1)} %shard_map.94), channel_id=1, source_target_pairs={{0,16},{8,24},{16,0},{24,8},{1,17},{9,25},{17,1},{25,9},{2,18},{10... | collective-permute-start | bytes 614408 | tf_op jit(solution)/shard_map/ppermute | solution.py:23
  47.2 8.8 %collective-permute-start.17 = (s16[784,128]{1,0:T(8,128)(2,1)S(1)}, s16[784,128]{1,0:T(8,128)(2,1)S(1)}, u32[]{:S(2)}, u32[]{:S(2)}) collective-permute-start(s16[784,128]{1,0:T(8,128)(2,1)S(1)} %shard_map.85.refs_0_), channel_id=1, source_target_pairs={{0,6},{1,7},{2,4},{3,5},{4,2},{5,3},{6,0},{7,1},{8,14},{9,15},{10,... | collective-permute-start | bytes 602120 | tf_op jit(solution)/shard_map/ppermute | solution.py:23
  49.3 9.9 %collective-permute-start.23 = (s16[784,128]{1,0:T(8,128)(2,1)S(1)}, s16[784,128]{1,0:T(8,128)(2,1)S(1)}, u32[]{:S(2)}, u32[]{:S(2)}) collective-permute-start(s16[784,128]{1,0:T(8,128)(2,1)S(1)} %shard_map.92), channel_id=1, source_target_pairs={{0,4},{1,5},{2,6},{3,7},{4,0},{5,1},{6,2},{7,3},{8,12},{9,13},{10,... | collective-permute-start | bytes 602120 | tf_op jit(solution)/shard_map/ppermute | solution.py:23
  50.7 8.7 %collective-permute-start.20 = (s16[784,128]{1,0:T(8,128)(2,1)S(1)}, s16[784,128]{1,0:T(8,128)(2,1)S(1)}, u32[]{:S(2)}, u32[]{:S(2)}) collective-permute-start(s16[784,128]{1,0:T(8,128)(2,1)S(1)} %shard_map.89), channel_id=1, source_target_pairs={{0,2},{1,3},{2,0},{3,1},{4,6},{5,7},{6,4},{7,5},{8,10},{9,11},{10,... | collective-permute-start | bytes 602120 | tf_op jit(solution)/shard_map/ppermute | solution.py:23
  52.8 1.5 %collective-permute-start.15 = (s16[768,128]{1,0:T(8,128)(2,1)S(1)}, s16[768,128]{1,0:T(8,128)(2,1)S(1)}, u32[]{:S(2)}, u32[]{:S(2)}) collective-permute-start(s16[768,128]{1,0:T(8,128)(2,1)S(1)} %get-tuple-element.55), channel_id=1, source_target_pairs={{0,1},{1,0},{2,3},{3,2},{4,5},{5,4},{6,7},{7,6},{8,9},{9,8},{10,11... | collective-permute-start | bytes 589832 | tf_op jit(solution)/shard_map/ppermute | solution.py:23
